TPU v7x, 768 devices: a whole 4x8x12 slice. The times are simulated.
768 devices in a mesh: blk: 48 (over y, z_hi, core), grp: 16 (over x, z_lo).
Axes of the slice: x: 4, y: 8, z: 12 (z_hi: 3, z_lo: 4; z = z_hi * 4 + z_lo), core: 2. Of those that a mesh axis runs over, the one named last changes fastest.
Arguments:
- images: bfloat16 [110592, 1152], P(('blk', 'grp')), may hold values from -0.17675781 to 0.17675781
- texts: bfloat16 [110592, 1152], P(('blk', 'grp')), may hold values from -0.17675781 to 0.17675781
Outputs:
- row_loss: float32 [110592], P(('blk', 'grp'))
- image_grad: float32 [110592, 1152], P(('blk', 'grp'))
- text_grad: float32 [110592, 1152], P(('blk', 'grp'))
All inputs are finite; a program needn't handle non-finite values.
Results may differ from a plain program's by a relative error of at most 0.022.
Values may be sent and summed in bfloat16 or wider, within the bound.
No kernel may reach another device: no remote copies, remote signals or barrier semaphores. Data moves between devices by JAX's collectives and lax.ppermute only.
A program may use at most 64 MiB of HBM per device.

v0:
```python
import jax
import jax.numpy as jnp
from jax import lax
from jax.sharding import PartitionSpec as P

STEPS = 2


multiplicative_scaling_factor = 10.0
additive_shift_term = -2.0
epsilon = 1e-06


def shifted(value, axis, steps):
    count = lax.axis_size(axis)
    pairs = [(source, (source + steps) % count) for source in range(count)]
    return lax.ppermute(value, axis, pairs)


def normalize(values_in):
    widened = values_in.astype(jnp.float32)
    length = jnp.sqrt(jnp.sum(widened * widened, axis=-1, keepdims=True) + epsilon)
    return (widened / length, length)


def project(unit_rows, length, grads):
    radial = jnp.sum(unit_rows * grads, axis=-1, keepdims=True)
    return (grads - unit_rows * radial) / length


def on_device(images, texts):
    img_unit, img_len = normalize(images)
    txt_unit, txt_len = normalize(texts)
    image_lower_bound = img_unit.astype(jnp.bfloat16)
    txt_low = txt_unit.astype(jnp.bfloat16)
    own_rows = images.shape[0]
    features = images.shape[1]
    anchor = lax.all_gather(txt_low, "grp", axis=0, tiled=True)
    block_rows = anchor.shape[0]
    member = lax.axis_index("grp")
    row_ids = lax.broadcasted_iota(jnp.int32, (own_rows, block_rows), 0)
    column_ids = lax.broadcasted_iota(jnp.int32, (own_rows, block_rows), 1)
    matches = column_ids == member * own_rows + row_ids
    img_grad = jnp.zeros((own_rows, features), jnp.float32)
    row_loss = jnp.zeros((own_rows,), jnp.float32)
    home_grads = jnp.zeros((own_rows, features), jnp.float32)
    present_block = anchor
    for offset in range(STEPS):
        if offset > 0:
            moved_rows = shifted(txt_low, "blk", offset)
            present_block = lax.all_gather(moved_rows, "grp", axis=0, tiled=True)
        similarity_matrix = (
            jnp.dot(image_lower_bound, present_block.T, preferred_element_type=jnp.float32)
            * multiplicative_scaling_factor
            + additive_shift_term
        )
        if offset == 0:
            match_target_signs = jnp.where(matches, 1.0, -1.0).astype(jnp.float32)
        else:
            match_target_signs = -jnp.ones_like(similarity_matrix)
        row_loss = row_loss + jnp.sum(
            jax.nn.softplus(-match_target_signs * similarity_matrix), axis=1
        )
        logistic_derivatives = (
            -match_target_signs
            * jax.nn.sigmoid(-match_target_signs * similarity_matrix)
            * multiplicative_scaling_factor
        ).astype(jnp.bfloat16)
        img_grad = img_grad + jnp.dot(
            logistic_derivatives, present_block, preferred_element_type=jnp.float32
        )
        partial_grad = jnp.dot(
            logistic_derivatives.T, image_lower_bound, preferred_element_type=jnp.float32
        )
        rounded = lax.optimization_barrier(partial_grad.astype(jnp.bfloat16))
        summed = lax.psum_scatter(
            rounded.astype(jnp.float32).astype(jnp.bfloat16), "grp", scatter_dimension=0, tiled=True
        ).astype(jnp.float32)
        if offset > 0:
            summed = shifted(summed.astype(jnp.bfloat16), "blk", -offset).astype(summed.dtype)
        home_grads = home_grads + summed
    image_grad = project(img_unit, img_len, img_grad)
    text_grad = project(txt_unit, txt_len, home_grads)
    return (row_loss, image_grad, text_grad)


def solution(mesh):
    in_specs = (P(("blk", "grp"), None), P(("blk", "grp"), None))
    out_specs = (P(("blk", "grp")), P(("blk", "grp"), None), P(("blk", "grp"), None))
    return jax.shard_map(
        on_device, mesh=mesh, in_specs=in_specs, out_specs=out_specs, check_vma=False
    )
```

profile of v0, /device:TPU:1, one launch (start us, length us, event | category | flops | bytes accessed | tf_op | source)
XLA Modules:
  0.0 575.7 jit_solution(4525930521688266136)
XLA Ops:
  7.2 0.0 copy-start.1
  7.2 0.0 all-gather.5.cloned.1.call-start
  7.2 1.2 fusion.6
  8.4 1.1 fusion.8
  9.5 0.0 copy-start.2
  9.5 12.0 %collective-permute-start = (bf16[144,1152]{1,0:T(8,128)(2,1)S(1)}, bf16[144,1152]{1,0:T(8,128)(2,1)S(1)}, u32[]{:S(2)}, u32[]{:S(2)}) collective-permute-start(bf16[144,1152]{1,0:T(8,128)(2,1)S(1)} %fusion.8), channel_id=1, source_target_pairs={{0,16},{16,32},{32,48},{48,64},{64,80},{80,96},{96,112},{112,128},... | collective-permute-start | bytes 995336 | tf_op jit(solution)/shard_map/ppermute | solution.py:17
  21.6 4.3 collective-permute-done
  25.8 0.0 copy-start.3
  25.8 0.7 copy-done.3
  26.6 0.0 all-gather.5.cloned.1.call-update
  26.6 0.0 all-gather.3.cloned.1.call-start
  26.6 0.0 copy-done.2
  26.6 0.7 all-gather.3.cloned.1.call-update
  27.3 0.0 reduce-scatter.5.cloned.1.call-start
  27.4 0.0 copy-done.1
  27.4 0.1 fusion.5
  27.6 142.0 %all-gather.5.cloned.1.call-done = bf16[2304,1152]{1,0:T(8,128)(2,1)} async-done(((bf16[144,1152]{1,0:T(8,128)(2,1)}), bf16[2304,1152]{1,0:T(8,128)(2,1)}) %all-gather.5.cloned.1.call-update) | async-done | bytes 5308432 | tf_op jit(solution)/shard_map/all_gather | solution.py:51
  169.5 4.4 fusion.4
  174.0 4.2 convolution_convert_fusion
  178.2 0.0 reduce-scatter.5.cloned.1.call-update
  178.2 0.0 reduce-scatter.3.cloned.1.call-start
  178.3 121.6 %all-gather.3.cloned.1.call-done = bf16[2304,1152]{1,0:T(8,128)(2,1)} async-done(((bf16[144,1152]{1,0:T(8,128)(2,1)}), bf16[2304,1152]{1,0:T(8,128)(2,1)}) %all-gather.3.cloned.1.call-update) | async-done | bytes 5308432 | tf_op jit(solution)/shard_map/all_gather | solution.py:38
  299.9 4.5 fusion.3
  304.4 4.3 convolution_convert_fusion.1
  308.7 0.0 reduce-scatter.3.cloned.1.call-update
  308.7 3.7 fusion.13
  312.5 0.6 add.63
  313.1 3.8 multiply_reduce_fusion.1
  316.9 0.0 copy-start
  316.9 114.8 %reduce-scatter.5.cloned.1.call-done = bf16[144,1152]{1,0:T(8,128)(2,1)} async-done(((bf16[2304,1152]{1,0:T(8,128)(2,1)}), bf16[144,1152]{1,0:T(8,128)(2,1)}) %reduce-scatter.5.cloned.1.call-update) | async-done | bytes 331792 | tf_op jit(solution)/shard_map/reduce_scatter | solution.py:76
  431.7 2.7 collective-permute-start.1
  434.4 1.0 subtract_divide_fusion.1
  435.5 130.3 %reduce-scatter.3.cloned.1.call-done = bf16[144,1152]{1,0:T(8,128)(2,1)} async-done(((bf16[2304,1152]{1,0:T(8,128)(2,1)}), bf16[144,1152]{1,0:T(8,128)(2,1)}) %reduce-scatter.3.cloned.1.call-update) | async-done | bytes 331792 | tf_op jit(solution)/shard_map/reduce_scatter | solution.py:76
  565.8 0.0 collective-permute-done.1
  565.8 0.0 copy-done
  565.8 1.3 multiply_reduce_fusion
  567.1 2.1 subtract_divide_fusion
  (3 shorter events, 0.0 us)
Async XLA Ops:
  7.2 20.2 %copy-start.1 = (bf16[144,1152]{1,0:T(8,128)(2,1)S(1)}, bf16[144,1152]{1,0:T(8,128)(2,1)}, u32[]{:S(2)}) copy-start(bf16[144,1152]{1,0:T(8,128)(2,1)} %param.2) | copy-start | bytes 995332
  7.2 162.4 %all-gather.5.cloned.1.call-start = ((), (), s32[]{:S(2)}) async-start(), calls=%async_computation.3 | async-start | bytes 5640192 | tf_op jit(solution)/shard_map/all_gather | solution.py:51
  9.5 17.1 %copy-start.2 = (bf16[144,1152]{1,0:T(8,128)(2,1)}, bf16[144,1152]{1,0:T(8,128)(2,1)S(1)}, u32[]{:S(2)}) copy-start(bf16[144,1152]{1,0:T(8,128)(2,1)S(1)} %fusion.8) | copy-start | bytes 995332
  9.5 16.3 %collective-permute-start = (bf16[144,1152]{1,0:T(8,128)(2,1)S(1)}, bf16[144,1152]{1,0:T(8,128)(2,1)S(1)}, u32[]{:S(2)}, u32[]{:S(2)}) collective-permute-start(bf16[144,1152]{1,0:T(8,128)(2,1)S(1)} %fusion.8), channel_id=1, source_target_pairs={{0,16},{16,32},{32,48},{48,64},{64,80},{80,96},{96,112},{112,128},... | collective-permute-start | bytes 995336 | tf_op jit(solution)/shard_map/ppermute | solution.py:17
  25.8 0.7 copy-start.3
  26.6 273.3 %all-gather.3.cloned.1.call-start = ((), (), s32[]{:S(2)}) async-start(), calls=%async_computation.2 | async-start | bytes 5640192 | tf_op jit(solution)/shard_map/all_gather | solution.py:38
  27.3 404.4 %reduce-scatter.5.cloned.1.call-start = ((), (), s32[]{:S(2)}) async-start(), calls=%async_computation.5 | async-start | bytes 5640192 | tf_op jit(solution)/shard_map/reduce_scatter | solution.py:76
  178.2 387.6 %reduce-scatter.3.cloned.1.call-start = ((), (), s32[]{:S(2)}) async-start(), calls=%async_computation.4 | async-start | bytes 5640192 | tf_op jit(solution)/shard_map/reduce_scatter | solution.py:76
  316.9 248.9 %copy-start = (bf16[144,1152]{1,0:T(8,128)(2,1)S(1)}, bf16[144,1152]{1,0:T(8,128)(2,1)}, u32[]{:S(2)}) copy-start(bf16[144,1152]{1,0:T(8,128)(2,1)} %param.3) | copy-start | bytes 995332
  431.7 134.1 %collective-permute-start.1 = (bf16[144,1152]{1,0:T(8,128)(2,1)}, bf16[144,1152]{1,0:T(8,128)(2,1)S(1)}, u32[]{:S(2)}, u32[]{:S(2)}) collective-permute-start(bf16[144,1152]{1,0:T(8,128)(2,1)} %reduce-scatter.5.cloned.1.call-done), channel_id=1, source_target_pairs={{0,752},{16,0},{32,16},{48,32},{64,48},{80,64},{96,80},{112,96},{1... | collective-permute-start | bytes 995336 | tf_op jit(solution)/shard_map/ppermute | solution.py:17
Sparse Core Ops, SparseCore 0:
  26.7 142.7 all-gather.4
  172.5 127.3 all-gather.2
  303.0 128.6 reduce-scatter.4
  434.7 131.0 reduce-scatter.2
where the time goes:
time: 576 us
  waiting for transfers between devices  514 us (89%)
  matrix products  25.1 us (4%)
  starting transfers between devices  14.9 us (3%)
  between operations  13.8 us (2%)
  other arithmetic  7.38 us (1%)
    reduce_scatter x2, waiting for transfers between devices, on_device(): lax.psum_scatter(rounded.astype(jnp.float32).astype(jnp.bfloat16), 'grp',...  245 us
    all_gather x1, waiting for transfers between devices, on_device(): present_block = lax.all_gather(moved_rows, 'grp', axis=0, tiled=True)  142 us
    all_gather x1, waiting for transfers between devices, on_device(): anchor = lax.all_gather(txt_low, 'grp', axis=0, tiled=True)  122 us
    ppermute x2, starting transfers between devices, shifted(): return lax.ppermute(value, axis, pairs)  14.8 us
  transfers between devices with their start and end apart: 6, of which 5 were waited for; matrix products, arithmetic and copies ran while one was open for 5% of the time, Pallas kernels for 0%

commit v1 on v0

v1 whole, which is shorter than its diff:
```python
import functools

import jax
import jax.numpy as jnp
from jax import lax
from jax.experimental import pallas as pl
from jax.experimental.pallas import tpu as pltpu
from jax.sharding import Mesh
from jax.sharding import PartitionSpec as P

SCALE = 10.0
SHIFT = -2.0
EPS = 1e-06
CORES, NX, NZ = 2, 4, 4
BLK, GRP = ("g", "core"), ("x", "z")
F32, BF16 = jnp.float32, jnp.bfloat16
VMEM_LIMIT = 48 * 1024 * 1024


def normalize(values_in):
    widened = values_in.astype(F32)
    length = jnp.sqrt(jnp.sum(widened * widened, axis=-1, keepdims=True) + EPS)
    return (widened / length, length)


def project(unit_rows, length, grads):
    radial = jnp.sum(unit_rows * grads, axis=-1, keepdims=True)
    return (grads - unit_rows * radial) / length


def shifted(value, axis, steps):
    count = lax.axis_size(axis)
    return lax.ppermute(value, axis, [(i, (i + steps) % count) for i in range(count)])


def gathered(value, axis):
    return [value] + [shifted(value, axis, s) for s in (1, 2, 3)]


def returned(parts, axis):
    total = parts[0].astype(F32)
    for s in (1, 2, 3):
        total = total + shifted(parts[s], axis, -s).astype(F32)
    return total


def slopes_kernel(paired, *refs):
    images, texts = refs[0:4], refs[4:8]
    slopes_ref, parts, loss_ref = refs[8], refs[9:13], refs[13]
    img_all, txt_all = refs[14:16]
    own = images[0].shape[0]
    for s in range(4):
        img_all[pl.ds(s * own, own), :] = images[s][...]
        txt_all[pl.ds(s * own, own), :] = texts[s][...]
    logits = lax.dot_general(
        img_all[...], txt_all[...], (((1,), (1,)), ((), ())), preferred_element_type=F32
    )
    logits = logits * SCALE + SHIFT
    if paired:
        rows = lax.broadcasted_iota(jnp.int32, logits.shape, 0)
        cols = lax.broadcasted_iota(jnp.int32, logits.shape, 1)
        match = (rows == cols) & (rows < own)
        signed = jnp.where(match, -logits, logits)
    else:
        signed = logits
    small = jnp.exp(-jnp.abs(signed))
    losses = jnp.maximum(signed, 0.0) + jnp.log1p(small)
    sig = jnp.where(signed >= 0.0, 1.0, small) / (1.0 + small)
    slopes = sig * SCALE
    if paired:
        slopes = jnp.where(match, -slopes, slopes)
    low = slopes.astype(BF16)
    slopes_ref[...] = low
    width = losses.shape[1]
    lanes = losses[:, 0:128]
    for c in range(128, width - 127, 128):
        lanes = lanes + losses[:, c : c + 128]
    rest = width % 128
    loss_row = jnp.sum(lanes.T, axis=0, keepdims=True)
    if rest:
        loss_row = loss_row + jnp.sum(losses[:, width - rest :].T, axis=0, keepdims=True)
    loss_ref[...] = loss_row
    grads = lax.dot_general(
        low, img_all[...], (((0,), (0,)), ((), ())), preferred_element_type=F32
    ).astype(BF16)
    for s in range(4):
        parts[s][...] = grads[s * own : (s + 1) * own, :]


def slopes_call(paired, images, texts):
    own, features = images[0].shape
    rows = 4 * own
    unit = jax.ShapeDtypeStruct((own, features), BF16)
    out = pl.pallas_call(
        functools.partial(slopes_kernel, paired),
        out_shape=[jax.ShapeDtypeStruct((rows, rows), BF16)]
        + [unit] * 4
        + [jax.ShapeDtypeStruct((1, rows), F32)],
        in_specs=[pl.BlockSpec(memory_space=pltpu.VMEM)] * 8,
        out_specs=[pl.BlockSpec(memory_space=pltpu.VMEM)] * 6,
        scratch_shapes=[pltpu.VMEM((rows, features), BF16)] * 2,
        compiler_params=pltpu.CompilerParams(vmem_limit_bytes=VMEM_LIMIT),
        cost_estimate=pl.CostEstimate(
            flops=4 * rows * rows * features,
            bytes_accessed=12 * 2 * own * features + 2 * rows * rows,
            transcendentals=3 * rows * rows,
        ),
    )(*images, *texts)
    return out[0], out[1:5], out[5]


def image_kernel(*refs):
    first, second = refs[0:2]
    texts, later = refs[2:6], refs[6:10]
    parts = refs[10:14]
    txt_all = refs[14]
    own = texts[0].shape[0]
    for s in range(4):
        txt_all[pl.ds(s * own, own), :] = texts[s][...]
        txt_all[pl.ds((4 + s) * own, own), :] = later[s][...]
    half = 4 * own
    grads = jnp.dot(first[...], txt_all[0:half, :], preferred_element_type=F32)
    grads = grads + jnp.dot(second[...], txt_all[half:, :], preferred_element_type=F32)
    grads = grads.astype(BF16)
    for s in range(4):
        parts[s][...] = grads[s * own : (s + 1) * own, :]


def image_call(first, second, texts, later):
    own, features = texts[0].shape
    rows = 4 * own
    unit = jax.ShapeDtypeStruct((own, features), BF16)
    return pl.pallas_call(
        image_kernel,
        out_shape=[unit] * 4,
        in_specs=[pl.BlockSpec(memory_space=pltpu.VMEM)] * 10,
        out_specs=[pl.BlockSpec(memory_space=pltpu.VMEM)] * 4,
        scratch_shapes=[pltpu.VMEM((2 * rows, features), BF16)],
        compiler_params=pltpu.CompilerParams(vmem_limit_bytes=VMEM_LIMIT),
        cost_estimate=pl.CostEstimate(
            flops=4 * rows * rows * features,
            bytes_accessed=12 * 2 * own * features + 4 * rows * rows,
            transcendentals=0,
        ),
    )(first, second, *texts, *later)


def on_device(images, texts):
    img_unit, img_len = normalize(images)
    txt_unit, txt_len = normalize(texts)
    img_low, txt_low = img_unit.astype(BF16), txt_unit.astype(BF16)
    own = images.shape[0]
    moved = shifted(txt_low, BLK, 1)
    img_slots = gathered(img_low, "z")
    txt_slots = gathered(txt_low, "x")
    moved_slots = gathered(moved, "x")

    slopes0, parts0, loss0 = slopes_call(True, img_slots, txt_slots)
    slopes1, parts1, loss1 = slopes_call(False, img_slots, moved_slots)
    img_parts = image_call(slopes0, slopes1, txt_slots, moved_slots)

    home1 = shifted(returned(parts1, "x").astype(BF16), BLK, -1).astype(F32)
    img_grad = returned(img_parts, "z")
    txt_grad = returned(parts0, "x") + home1

    loss_slots = (loss0 + loss1).reshape(4, own)
    place = lax.axis_index("z")
    owner = lax.broadcasted_iota(jnp.int32, (NZ, own), 0)
    slot = lax.rem(place - owner + NZ, NZ)
    loss_at = jnp.zeros((NZ, own), F32)
    for s in range(4):
        loss_at = loss_at + jnp.where(slot == s, loss_slots[s][None, :], 0.0)
    row_loss = lax.psum_scatter(loss_at.reshape(-1), "z", scatter_dimension=0, tiled=True)

    image_grad = project(img_unit, img_len, img_grad)
    text_grad = project(txt_unit, txt_len, txt_grad)
    return (row_loss, image_grad, text_grad)


def solution(mesh):
    groups = mesh.devices.shape[0] // CORES
    fine = Mesh(mesh.devices.reshape(groups, CORES, NX, NZ), BLK + GRP)
    rows = P(BLK + GRP, None)
    return jax.shard_map(
        on_device,
        mesh=fine,
        in_specs=(rows, rows),
        out_specs=(P(BLK + GRP), rows, rows),
        check_vma=False,
    )
```

time: 576 us -> 173 us (0.30)
  waiting for transfers between devices: 514 us -> 45.9 us
  starting transfers between devices: 14.9 us -> 71.6 us
  matrix products: 25.1 us -> 0 us
  blocking collectives: 0 us -> 19.4 us
  between operations: 13.8 us -> 1.7 us
  Pallas kernels: 0 us -> 12.1 us
  local copies, waits for them, and re-layouts: 0.74 us -> 12.6 us
    all_gather x2 -> x0, waiting for transfers between devices: 264 us -> none  [the longest x1 142 us: on_device(): present_block = lax.all_gather(moved_rows, 'grp', axis=0, tiled=True)]
    reduce_scatter x2 -> x0, waiting for transfers between devices: 245 us -> none  [on_device(): lax.psum_scatter(rounded.astype(jnp.float32).astype(jnp.bfloat16), 'grp',...]
    ppermute x2 -> x20, starting transfers between devices: 14.8 us -> 71.6 us  [shifted(): lax.ppermute(value, axis, [(i, (i + steps) % count) for i in range(count)])]
    ppermute x2 -> x20, waiting for transfers between devices: 4.28 us -> 45.9 us  [shifted(): lax.ppermute(value, axis, [(i, (i + steps) % count) for i in range(count)])]
    dot_general x6 -> x0, matrix products: 25.1 us -> none  [the longest x2 8.97 us: on_device(): jnp.dot(image_lower_bound, present_block.T, preferred_element_type=jnp.fl...]
    unnamed x0 -> x1, blocking collectives: none -> 19.4 us
    pallas_call x0 -> x3, Pallas kernels: none -> 12.1 us  [the longest x2 8.51 us: slopes_call(): pl.pallas_call(functools.partial(slopes_kernel, paired), out_shape=[jax.S...]
    unnamed x8 -> x36, local copies, waits for them, and re-layouts: 0.74 us -> 12 us
  transfers between devices with their start and end apart: 6 -> 20, of which waited for: 5 -> 6; matrix products, arithmetic and copies ran while one was open for 5% -> 3% of each run, Pallas kernels for 0% -> 7%
where the time goes in v1:
time: 173 us; the launch traced here: 172 us
  starting transfers between devices  71.6 us (41%)
  waiting for transfers between devices  45.9 us (27%)
  blocking collectives  19.4 us (11%)
  local copies, waits for them, and re-layouts  12.6 us (7%)
  Pallas kernels  12.1 us (7%)
  other arithmetic  8.26 us (5%)
    ppermute x20, starting transfers between devices, shifted(): lax.ppermute(value, axis, [(i, (i + steps) % count) for i in range(count)])  71.6 us
    ppermute x20, waiting for transfers between devices, shifted(): lax.ppermute(value, axis, [(i, (i + steps) % count) for i in range(count)])  45.9 us
    unnamed x1, blocking collectives  19.4 us
    unnamed x36, local copies, waits for them, and re-layouts  12 us
    pallas_call x2, Pallas kernels, slopes_call(): pl.pallas_call(functools.partial(slopes_kernel, paired), out_shape=[jax.S...  8.51 us
    pallas_call x1, Pallas kernels, image_call(): pl.pallas_call(image_kernel, out_shape=[unit] * 4, in_specs=[pl.BlockSpec...  3.61 us
  transfers between devices with their start and end apart: 20, of which 6 were waited for; matrix products, arithmetic and copies ran while one was open for 3% of the time, Pallas kernels for 7%

profile of v1, /device:TPU:1, one launch (start us, length us, event | category | flops | bytes accessed | tf_op | source)
XLA Modules:
  0.0 171.6 jit_solution(480796772684858196)
XLA Ops:
  0.6 0.0 copy-start.13
  0.6 1.2 fusion.1
  1.8 0.0 copy-start.15
  1.9 0.1 fusion.4.refs_4_.refs_2_
  2.0 12.0 %collective-permute-start.6 = (bf16[144,1152]{1,0:T(8,128)(2,1)S(1)}, bf16[144,1152]{1,0:T(8,128)(2,1)S(1)}, u32[]{:S(2)}, u32[]{:S(2)}) collective-permute-start(bf16[144,1152]{1,0:T(8,128)(2,1)S(1)} %fusion.4.refs_4_.refs_2_), channel_id=1, source_target_pairs={{0,16},{16,32},{32,48},{48,64},{64,80},{80,96},{96,112},{112,128},... | collective-permute-start | bytes 995336 | tf_op jit(solution)/shard_map/ppermute | solution.py:33
  14.0 0.1 fusion
  14.2 0.1 fusion.3.refs_0_
  14.3 4.0 %collective-permute-start = (bf16[144,1152]{1,0:T(8,128)(2,1)S(1)}, bf16[144,1152]{1,0:T(8,128)(2,1)S(1)}, u32[]{:S(2)}, u32[]{:S(2)}) collective-permute-start(bf16[144,1152]{1,0:T(8,128)(2,1)S(1)} %fusion.3.refs_0_), channel_id=1, source_target_pairs={{0,1},{1,2},{2,3},{3,0},{4,5},{5,6},{6,7},{7,4},{8,9},{9,10},{10,1... | collective-permute-start | bytes 995336 | tf_op jit(solution)/shard_map/ppermute | solution.py:33
  18.4 5.5 %collective-permute-start.1 = (bf16[144,1152]{1,0:T(8,128)(2,1)S(1)}, bf16[144,1152]{1,0:T(8,128)(2,1)S(1)}, u32[]{:S(2)}, u32[]{:S(2)}) collective-permute-start(bf16[144,1152]{1,0:T(8,128)(2,1)S(1)} %fusion.3.refs_0_), channel_id=1, source_target_pairs={{0,2},{1,3},{2,0},{3,1},{4,6},{5,7},{6,4},{7,5},{8,10},{9,11},{10,... | collective-permute-start | bytes 995336 | tf_op jit(solution)/shard_map/ppermute | solution.py:33
  23.9 2.5 %collective-permute-start.2 = (bf16[144,1152]{1,0:T(8,128)(2,1)S(1)}, bf16[144,1152]{1,0:T(8,128)(2,1)S(1)}, u32[]{:S(2)}, u32[]{:S(2)}) collective-permute-start(bf16[144,1152]{1,0:T(8,128)(2,1)S(1)} %fusion.3.refs_0_), channel_id=1, source_target_pairs={{0,3},{1,0},{2,1},{3,2},{4,7},{5,4},{6,5},{7,6},{8,11},{9,8},{10,9... | collective-permute-start | bytes 995336 | tf_op jit(solution)/shard_map/ppermute | solution.py:33
  26.4 3.1 %collective-permute-start.3 = (bf16[144,1152]{1,0:T(8,128)(2,1)S(1)}, bf16[144,1152]{1,0:T(8,128)(2,1)S(1)}, u32[]{:S(2)}, u32[]{:S(2)}) collective-permute-start(bf16[144,1152]{1,0:T(8,128)(2,1)S(1)} %fusion.4.refs_4_.refs_2_), channel_id=1, source_target_pairs={{0,4},{4,8},{8,12},{12,0},{1,5},{5,9},{9,13},{13,1},{2,6},{6,10},{... | collective-permute-start | bytes 995336 | tf_op jit(solution)/shard_map/ppermute | solution.py:33
  29.5 0.0 collective-permute-done.6.refs_4_.refs_6_
  29.5 4.4 %collective-permute-start.4 = (bf16[144,1152]{1,0:T(8,128)(2,1)S(1)}, bf16[144,1152]{1,0:T(8,128)(2,1)S(1)}, u32[]{:S(2)}, u32[]{:S(2)}) collective-permute-start(bf16[144,1152]{1,0:T(8,128)(2,1)S(1)} %fusion.4.refs_4_.refs_2_), channel_id=1, source_target_pairs={{0,8},{4,12},{8,0},{12,4},{1,9},{5,13},{9,1},{13,5},{2,10},{6,14},... | collective-permute-start | bytes 995336 | tf_op jit(solution)/shard_map/ppermute | solution.py:33
  33.9 2.7 %collective-permute-done.refs_1_ = bf16[144,1152]{1,0:T(8,128)(2,1)S(1)} collective-permute-done((bf16[144,1152]{1,0:T(8,128)(2,1)S(1)}, bf16[144,1152]{1,0:T(8,128)(2,1)S(1)}, u32[]{:S(2)}, u32[]{:S(2)}) %collective-permute-start) | collective-permute-done | bytes 331808 | tf_op jit(solution)/shard_map/ppermute | solution.py:33
  36.6 0.7 copy-done.2
  37.3 4.9 %collective-permute-start.5 = (bf16[144,1152]{1,0:T(8,128)(2,1)S(1)}, bf16[144,1152]{1,0:T(8,128)(2,1)S(1)}, u32[]{:S(2)}, u32[]{:S(2)}) collective-permute-start(bf16[144,1152]{1,0:T(8,128)(2,1)S(1)} %fusion.4.refs_4_.refs_2_), channel_id=1, source_target_pairs={{0,12},{4,0},{8,4},{12,8},{1,13},{5,1},{9,5},{13,9},{2,14},{6,2},{... | collective-permute-start | bytes 995336 | tf_op jit(solution)/shard_map/ppermute | solution.py:33
  42.3 1.4 collective-permute-done.1.refs_2_
  43.7 0.7 copy-done.5
  44.4 2.4 %collective-permute-start.7 = (bf16[144,1152]{1,0:T(8,128)(2,1)S(1)}, bf16[144,1152]{1,0:T(8,128)(2,1)}, u32[]{:S(2)}, u32[]{:S(2)}) collective-permute-start(bf16[144,1152]{1,0:T(8,128)(2,1)S(1)} %collective-permute-done.6.refs_4_.refs_6_), channel_id=1, source_target_pairs={{0,4},{4,8},{8,12},{12,0},{1,5},{5,9},{9,13},{13,1},{2,6},{6,10},{... | collective-permute-start | bytes 995336 | tf_op jit(solution)/shard_map/ppermute | solution.py:33
  46.8 3.3 %collective-permute-done.2.refs_3_ = bf16[144,1152]{1,0:T(8,128)(2,1)S(1)} collective-permute-done((bf16[144,1152]{1,0:T(8,128)(2,1)S(1)}, bf16[144,1152]{1,0:T(8,128)(2,1)S(1)}, u32[]{:S(2)}, u32[]{:S(2)}) %collective-permute-start.2) | collective-permute-done | bytes 331808 | tf_op jit(solution)/shard_map/ppermute | solution.py:33
  50.1 0.7 copy-done.7
  50.8 1.9 %collective-permute-start.8 = (bf16[144,1152]{1,0:T(8,128)(2,1)S(1)}, bf16[144,1152]{1,0:T(8,128)(2,1)}, u32[]{:S(2)}, u32[]{:S(2)}) collective-permute-start(bf16[144,1152]{1,0:T(8,128)(2,1)S(1)} %collective-permute-done.6.refs_4_.refs_6_), channel_id=1, source_target_pairs={{0,8},{4,12},{8,0},{12,4},{1,9},{5,13},{9,1},{13,5},{2,10},{6,14},... | collective-permute-start | bytes 995336 | tf_op jit(solution)/shard_map/ppermute | solution.py:33
  52.8 2.2 %collective-permute-start.9 = (bf16[144,1152]{1,0:T(8,128)(2,1)S(1)}, bf16[144,1152]{1,0:T(8,128)(2,1)}, u32[]{:S(2)}, u32[]{:S(2)}) collective-permute-start(bf16[144,1152]{1,0:T(8,128)(2,1)S(1)} %collective-permute-done.6.refs_4_.refs_6_), channel_id=1, source_target_pairs={{0,12},{4,0},{8,4},{12,8},{1,13},{5,1},{9,5},{13,9},{2,14},{6,2},{... | collective-permute-start | bytes 995336 | tf_op jit(solution)/shard_map/ppermute | solution.py:33
  55.0 0.1 iota.7
  55.1 0.1 add.72
  55.2 1.3 dynamic-slice
  57.1 0.0 copy-start.3
  57.1 1.0 copy-done.3
  58.1 1.0 copy-done.6
  59.1 1.0 copy-done.8
  60.1 3.2 %shard_map.49 = (bf16[576,576]{1,0:T(8,128)(2,1)S(1)}, bf16[144,1152]{1,0:T(8,128)(2,1)S(1)}, bf16[144,1152]{1,0:T(8,128)(2,1)S(1)}, bf16[144,1152]{1,0:T(8,128)...) custom-call(bf16[144,1152]{1,0:T(8,128)(2,1)S(1)} %fusion.3.refs_0_, bf16[144,1152]{1,0:T(8,128)(2,1)S(1)} %copy-done.3, ...), custom_call_target="tpu_custom_call" | custom-call | flops 1528823808 | bytes 4644864 | tf_op jit(solution)/shard_map/pallas_call | solution.py:94
  63.3 0.9 copy-done.9
  64.2 4.8 %collective-permute-start.13 = (bf16[144,1152]{1,0:T(8,128)(2,1)S(1)}, bf16[144,1152]{1,0:T(8,128)(2,1)}, u32[]{:S(2)}, u32[]{:S(2)}) collective-permute-start(bf16[144,1152]{1,0:T(8,128)(2,1)S(1)} %get-tuple-element.28), channel_id=1, source_target_pairs={{0,12},{4,0},{8,4},{12,8},{1,13},{5,1},{9,5},{13,9},{2,14},{6,2},{... | collective-permute-start | bytes 995336 | tf_op jit(solution)/shard_map/ppermute | solution.py:33
  69.0 1.9 %collective-permute-start.14 = (bf16[144,1152]{1,0:T(8,128)(2,1)S(1)}, bf16[144,1152]{1,0:T(8,128)(2,1)}, u32[]{:S(2)}, u32[]{:S(2)}) collective-permute-start(bf16[144,1152]{1,0:T(8,128)(2,1)S(1)} %get-tuple-element.29), channel_id=1, source_target_pairs={{0,8},{4,12},{8,0},{12,4},{1,9},{5,13},{9,1},{13,5},{2,10},{6,14},... | collective-permute-start | bytes 995336 | tf_op jit(solution)/shard_map/ppermute | solution.py:33
  71.0 5.3 %shard_map.50 = (bf16[576,576]{1,0:T(8,128)(2,1)S(1)}, bf16[144,1152]{1,0:T(8,128)(2,1)S(1)}, bf16[144,1152]{1,0:T(8,128)(2,1)}, bf16[144,1152]{1,0:T(8,128)(2,1...) custom-call(bf16[144,1152]{1,0:T(8,128)(2,1)S(1)} %fusion.3.refs_0_, bf16[144,1152]{1,0:T(8,128)(2,1)S(1)} %copy-done.4, ...), custom_call_target="tpu_custom_call" | custom-call | flops 1528823808 | bytes 4644864 | tf_op jit(solution)/shard_map/pallas_call | solution.py:94
  76.2 0.9 copy-done.11
  77.1 2.8 %collective-permute-start.16 = (bf16[144,1152]{1,0:T(8,128)(2,1)}, bf16[144,1152]{1,0:T(8,128)(2,1)}, u32[]{:S(2)}, u32[]{:S(2)}) collective-permute-start(bf16[144,1152]{1,0:T(8,128)(2,1)} %get-tuple-element.32), channel_id=1, source_target_pairs={{0,12},{4,0},{8,4},{12,8},{1,13},{5,1},{9,5},{13,9},{2,14},{6,2},{... | collective-permute-start | bytes 995336 | tf_op jit(solution)/shard_map/ppermute | solution.py:33
  80.0 3.9 %collective-permute-start.17 = (bf16[144,1152]{1,0:T(8,128)(2,1)}, bf16[144,1152]{1,0:T(8,128)(2,1)}, u32[]{:S(2)}, u32[]{:S(2)}) collective-permute-start(bf16[144,1152]{1,0:T(8,128)(2,1)} %get-tuple-element.33), channel_id=1, source_target_pairs={{0,8},{4,12},{8,0},{12,4},{1,9},{5,13},{9,1},{13,5},{2,10},{6,14},... | collective-permute-start | bytes 995336 | tf_op jit(solution)/shard_map/ppermute | solution.py:33
  83.9 2.8 %collective-permute-start.18 = (bf16[144,1152]{1,0:T(8,128)(2,1)}, bf16[144,1152]{1,0:T(8,128)(2,1)}, u32[]{:S(2)}, u32[]{:S(2)}) collective-permute-start(bf16[144,1152]{1,0:T(8,128)(2,1)} %get-tuple-element.34), channel_id=1, source_target_pairs={{0,4},{4,8},{8,12},{12,0},{1,5},{5,9},{9,13},{13,1},{2,6},{6,10},{... | collective-permute-start | bytes 995336 | tf_op jit(solution)/shard_map/ppermute | solution.py:33
  86.7 0.1 fusion.5
  86.8 0.1 broadcast_in_dim.52
  86.9 0.1 broadcast_in_dim.56
  87.0 0.1 broadcast_in_dim.59
  87.0 0.1 broadcast_in_dim.62
  87.2 19.4 %all-reduce = f32[576]{0:T(1024)S(1)} all-reduce(f32[576]{0:T(1024)S(1)} %select_add_fusion), channel_id=2, replica_groups=mesh['g'=24,'core'=2,'x'=4,'z'=4] {'z'}, use_global_device_ids=true, to_apply=%region_2.3.clone | all-reduce | flops 576 | bytes 4608
  106.6 0.6 dynamic-slice.1
  107.2 1.0 copy-done.1
  108.2 1.1 copy-done.10
  109.3 1.1 copy-done.12
  110.4 3.6 %shard_map.51 = (bf16[144,1152]{1,0:T(8,128)(2,1)S(1)}, bf16[144,1152]{1,0:T(8,128)(2,1)S(1)}, bf16[144,1152]{1,0:T(8,128)(2,1)S(1)}, bf16[144,1152]{1,0:T(8,128)(2,1)S(1)}) custom-call(bf16[576,576]{1,0:T(8,128)(2,1)S(1)} %copy-done.10, bf16[576,576]{1,0:T(8,128)(2,1)S(1)} %copy-done.12, bf16[144,1152]{1,0:T(8,128)(2,1)S(1)} %fusion.4.refs_4_.refs_2_, ...), custom_call_target="tpu_custom_call" | custom-call | flops 1528823808 | bytes 5308416 | tf_op jit(solution)/shard_map/pallas_call | solution.py:133
  114.0 1.9 %collective-permute-start.10 = (bf16[144,1152]{1,0:T(8,128)(2,1)S(1)}, bf16[144,1152]{1,0:T(8,128)(2,1)S(1)}, u32[]{:S(2)}, u32[]{:S(2)}) collective-permute-start(bf16[144,1152]{1,0:T(8,128)(2,1)S(1)} %get-tuple-element.24), channel_id=1, source_target_pairs={{0,3},{1,0},{2,1},{3,2},{4,7},{5,4},{6,5},{7,6},{8,11},{9,8},{10,9... | collective-permute-start | bytes 995336 | tf_op jit(solution)/shard_map/ppermute | solution.py:33
  116.0 2.9 %collective-permute-start.11 = (bf16[144,1152]{1,0:T(8,128)(2,1)S(1)}, bf16[144,1152]{1,0:T(8,128)(2,1)S(1)}, u32[]{:S(2)}, u32[]{:S(2)}) collective-permute-start(bf16[144,1152]{1,0:T(8,128)(2,1)S(1)} %get-tuple-element.25), channel_id=1, source_target_pairs={{0,2},{1,3},{2,0},{3,1},{4,6},{5,7},{6,4},{7,5},{8,10},{9,11},{10,... | collective-permute-start | bytes 995336 | tf_op jit(solution)/shard_map/ppermute | solution.py:33
  118.9 2.4 %collective-permute-start.12 = (bf16[144,1152]{1,0:T(8,128)(2,1)S(1)}, bf16[144,1152]{1,0:T(8,128)(2,1)S(1)}, u32[]{:S(2)}, u32[]{:S(2)}) collective-permute-start(bf16[144,1152]{1,0:T(8,128)(2,1)S(1)} %get-tuple-element.26), channel_id=1, source_target_pairs={{0,1},{1,2},{2,3},{3,0},{4,5},{5,6},{6,7},{7,4},{8,9},{9,10},{10,1... | collective-permute-start | bytes 995336 | tf_op jit(solution)/shard_map/ppermute | solution.py:33
  121.3 0.0 copy-start.16
  121.3 1.4 add_convert_fusion
  122.7 4.4 %collective-permute-done.10 = bf16[144,1152]{1,0:T(8,128)(2,1)S(1)} collective-permute-done((bf16[144,1152]{1,0:T(8,128)(2,1)S(1)}, bf16[144,1152]{1,0:T(8,128)(2,1)S(1)}, u32[]{:S(2)}, u32[]{:S(2)}) %collective-permute-start.10) | collective-permute-done | bytes 331808 | tf_op jit(solution)/shard_map/ppermute | solution.py:33
  127.1 3.3 %collective-permute-start.15 = (bf16[144,1152]{1,0:T(8,128)(2,1)S(1)}, bf16[144,1152]{1,0:T(8,128)(2,1)S(1)}, u32[]{:S(2)}, u32[]{:S(2)}) collective-permute-start(bf16[144,1152]{1,0:T(8,128)(2,1)S(1)} %get-tuple-element.30), channel_id=1, source_target_pairs={{0,4},{4,8},{8,12},{12,0},{1,5},{5,9},{9,13},{13,1},{2,6},{6,10},{... | collective-permute-start | bytes 995336 | tf_op jit(solution)/shard_map/ppermute | solution.py:33
  130.4 13.7 %collective-permute-done.11 = bf16[144,1152]{1,0:T(8,128)(2,1)S(1)} collective-permute-done((bf16[144,1152]{1,0:T(8,128)(2,1)S(1)}, bf16[144,1152]{1,0:T(8,128)(2,1)S(1)}, u32[]{:S(2)}, u32[]{:S(2)}) %collective-permute-start.11) | collective-permute-done | bytes 331808 | tf_op jit(solution)/shard_map/ppermute | solution.py:33
  144.1 1.9 %collective-permute-start.19 = (bf16[144,1152]{1,0:T(8,128)(2,1)S(1)}, bf16[144,1152]{1,0:T(8,128)(2,1)S(1)}, u32[]{:S(2)}, u32[]{:S(2)}) collective-permute-start(bf16[144,1152]{1,0:T(8,128)(2,1)S(1)} %add_convert_fusion), channel_id=1, source_target_pairs={{0,752},{16,0},{32,16},{48,32},{64,48},{80,64},{96,80},{112,96},{1... | collective-permute-start | bytes 995336 | tf_op jit(solution)/shard_map/ppermute | solution.py:33
  146.0 0.3 multiply_reduce_fusion.1
  146.4 1.1 subtract_divide_fusion.1
  147.5 20.3 %collective-permute-done.19 = bf16[144,1152]{1,0:T(8,128)(2,1)S(1)} collective-permute-done((bf16[144,1152]{1,0:T(8,128)(2,1)S(1)}, bf16[144,1152]{1,0:T(8,128)(2,1)S(1)}, u32[]{:S(2)}, u32[]{:S(2)}) %collective-permute-start.19) | collective-permute-done | bytes 331808 | tf_op jit(solution)/shard_map/ppermute | solution.py:33
  167.9 1.5 multiply_reduce_fusion
  169.3 2.3 %subtract_divide_fusion = f32[144,1152]{1,0:T(8,128)} fusion(f32[144]{0:T(256)S(1)} %multiply_reduce_fusion, f32[144]{0:T(256)S(1)} %add_sqrt_fusion, bf16[144,1152]{1,0:T(8,128)(2,1)S(1)} %collective-permute-done.19, bf16[144,1152]{1,0:T(8,128)(2,1)S(1)} %collective-permute-done.15, bf16[144,1152]{1,0:T(8,128)(2,1)} %collective-permute-done.14, ...), kind=kLoop, calls=%fused_computation.6 | loop fusion | flops 2322432 | bytes 2655360 | tf_op jit(solution)/shard_map/div | solution.py:28
  (41 shorter events, 0.1 us)
Async XLA Ops:
  0.6 1.2 copy-start.13
  1.8 12.2 %copy-start.15 = (bf16[144,1152]{1,0:T(8,128)(2,1)S(1)}, bf16[144,1152]{1,0:T(8,128)(2,1)}, u32[]{:S(2)}) copy-start(bf16[144,1152]{1,0:T(8,128)(2,1)} %param.2) | copy-start | bytes 995332
  2.0 27.5 %collective-permute-start.6 = (bf16[144,1152]{1,0:T(8,128)(2,1)S(1)}, bf16[144,1152]{1,0:T(8,128)(2,1)S(1)}, u32[]{:S(2)}, u32[]{:S(2)}) collective-permute-start(bf16[144,1152]{1,0:T(8,128)(2,1)S(1)} %fusion.4.refs_4_.refs_2_), channel_id=1, source_target_pairs={{0,16},{16,32},{32,48},{48,64},{64,80},{80,96},{96,112},{112,128},... | collective-permute-start | bytes 995336 | tf_op jit(solution)/shard_map/ppermute | solution.py:33
  14.3 22.3 %collective-permute-start = (bf16[144,1152]{1,0:T(8,128)(2,1)S(1)}, bf16[144,1152]{1,0:T(8,128)(2,1)S(1)}, u32[]{:S(2)}, u32[]{:S(2)}) collective-permute-start(bf16[144,1152]{1,0:T(8,128)(2,1)S(1)} %fusion.3.refs_0_), channel_id=1, source_target_pairs={{0,1},{1,2},{2,3},{3,0},{4,5},{5,6},{6,7},{7,4},{8,9},{9,10},{10,1... | collective-permute-start | bytes 995336 | tf_op jit(solution)/shard_map/ppermute | solution.py:33
  18.4 25.4 %collective-permute-start.1 = (bf16[144,1152]{1,0:T(8,128)(2,1)S(1)}, bf16[144,1152]{1,0:T(8,128)(2,1)S(1)}, u32[]{:S(2)}, u32[]{:S(2)}) collective-permute-start(bf16[144,1152]{1,0:T(8,128)(2,1)S(1)} %fusion.3.refs_0_), channel_id=1, source_target_pairs={{0,2},{1,3},{2,0},{3,1},{4,6},{5,7},{6,4},{7,5},{8,10},{9,11},{10,... | collective-permute-start | bytes 995336 | tf_op jit(solution)/shard_map/ppermute | solution.py:33
  23.9 26.2 %collective-permute-start.2 = (bf16[144,1152]{1,0:T(8,128)(2,1)S(1)}, bf16[144,1152]{1,0:T(8,128)(2,1)S(1)}, u32[]{:S(2)}, u32[]{:S(2)}) collective-permute-start(bf16[144,1152]{1,0:T(8,128)(2,1)S(1)} %fusion.3.refs_0_), channel_id=1, source_target_pairs={{0,3},{1,0},{2,1},{3,2},{4,7},{5,4},{6,5},{7,6},{8,11},{9,8},{10,9... | collective-permute-start | bytes 995336 | tf_op jit(solution)/shard_map/ppermute | solution.py:33
  26.4 26.4 %collective-permute-start.3 = (bf16[144,1152]{1,0:T(8,128)(2,1)S(1)}, bf16[144,1152]{1,0:T(8,128)(2,1)S(1)}, u32[]{:S(2)}, u32[]{:S(2)}) collective-permute-start(bf16[144,1152]{1,0:T(8,128)(2,1)S(1)} %fusion.4.refs_4_.refs_2_), channel_id=1, source_target_pairs={{0,4},{4,8},{8,12},{12,0},{1,5},{5,9},{9,13},{13,1},{2,6},{6,10},{... | collective-permute-start | bytes 995336 | tf_op jit(solution)/shard_map/ppermute | solution.py:33
  29.5 27.6 %collective-permute-start.4 = (bf16[144,1152]{1,0:T(8,128)(2,1)S(1)}, bf16[144,1152]{1,0:T(8,128)(2,1)S(1)}, u32[]{:S(2)}, u32[]{:S(2)}) collective-permute-start(bf16[144,1152]{1,0:T(8,128)(2,1)S(1)} %fusion.4.refs_4_.refs_2_), channel_id=1, source_target_pairs={{0,8},{4,12},{8,0},{12,4},{1,9},{5,13},{9,1},{13,5},{2,10},{6,14},... | collective-permute-start | bytes 995336 | tf_op jit(solution)/shard_map/ppermute | solution.py:33
  36.6 0.7 copy-start.2
  37.3 19.8 %collective-permute-start.5 = (bf16[144,1152]{1,0:T(8,128)(2,1)S(1)}, bf16[144,1152]{1,0:T(8,128)(2,1)S(1)}, u32[]{:S(2)}, u32[]{:S(2)}) collective-permute-start(bf16[144,1152]{1,0:T(8,128)(2,1)S(1)} %fusion.4.refs_4_.refs_2_), channel_id=1, source_target_pairs={{0,12},{4,0},{8,4},{12,8},{1,13},{5,1},{9,5},{13,9},{2,14},{6,2},{... | collective-permute-start | bytes 995336 | tf_op jit(solution)/shard_map/ppermute | solution.py:33
  43.7 0.7 copy-start.5
  44.4 26.5 %collective-permute-start.7 = (bf16[144,1152]{1,0:T(8,128)(2,1)S(1)}, bf16[144,1152]{1,0:T(8,128)(2,1)}, u32[]{:S(2)}, u32[]{:S(2)}) collective-permute-start(bf16[144,1152]{1,0:T(8,128)(2,1)S(1)} %collective-permute-done.6.refs_4_.refs_6_), channel_id=1, source_target_pairs={{0,4},{4,8},{8,12},{12,0},{1,5},{5,9},{9,13},{13,1},{2,6},{6,10},{... | collective-permute-start | bytes 995336 | tf_op jit(solution)/shard_map/ppermute | solution.py:33
  50.1 0.7 copy-start.7
  50.8 20.1 %collective-permute-start.8 = (bf16[144,1152]{1,0:T(8,128)(2,1)S(1)}, bf16[144,1152]{1,0:T(8,128)(2,1)}, u32[]{:S(2)}, u32[]{:S(2)}) collective-permute-start(bf16[144,1152]{1,0:T(8,128)(2,1)S(1)} %collective-permute-done.6.refs_4_.refs_6_), channel_id=1, source_target_pairs={{0,8},{4,12},{8,0},{12,4},{1,9},{5,13},{9,1},{13,5},{2,10},{6,14},... | collective-permute-start | bytes 995336 | tf_op jit(solution)/shard_map/ppermute | solution.py:33
  52.8 18.2 %collective-permute-start.9 = (bf16[144,1152]{1,0:T(8,128)(2,1)S(1)}, bf16[144,1152]{1,0:T(8,128)(2,1)}, u32[]{:S(2)}, u32[]{:S(2)}) collective-permute-start(bf16[144,1152]{1,0:T(8,128)(2,1)S(1)} %collective-permute-done.6.refs_4_.refs_6_), channel_id=1, source_target_pairs={{0,12},{4,0},{8,4},{12,8},{1,13},{5,1},{9,5},{13,9},{2,14},{6,2},{... | collective-permute-start | bytes 995336 | tf_op jit(solution)/shard_map/ppermute | solution.py:33
  57.1 1.0 copy-start.3
  58.1 1.0 copy-start.6
  59.1 1.0 copy-start.8
  60.1 3.3 %copy-start = (bf16[144,1152]{1,0:T(8,128)(2,1)}, bf16[144,1152]{1,0:T(8,128)(2,1)S(1)}, u32[]{:S(2)}) copy-start(bf16[144,1152]{1,0:T(8,128)(2,1)S(1)} %collective-permute-done.5.refs_7_.refs_5_) | copy-start | bytes 995332
  60.1 10.9 %copy-start.4 = (bf16[144,1152]{1,0:T(8,128)(2,1)S(1)}, bf16[144,1152]{1,0:T(8,128)(2,1)}, u32[]{:S(2)}) copy-start(bf16[144,1152]{1,0:T(8,128)(2,1)} %copy-done.2) | copy-start | bytes 995332
  63.3 0.9 copy-start.9
  64.2 83.3 %collective-permute-start.13 = (bf16[144,1152]{1,0:T(8,128)(2,1)S(1)}, bf16[144,1152]{1,0:T(8,128)(2,1)}, u32[]{:S(2)}, u32[]{:S(2)}) collective-permute-start(bf16[144,1152]{1,0:T(8,128)(2,1)S(1)} %get-tuple-element.28), channel_id=1, source_target_pairs={{0,12},{4,0},{8,4},{12,8},{1,13},{5,1},{9,5},{13,9},{2,14},{6,2},{... | collective-permute-start | bytes 995336 | tf_op jit(solution)/shard_map/ppermute | solution.py:33
  69.0 78.5 %collective-permute-start.14 = (bf16[144,1152]{1,0:T(8,128)(2,1)S(1)}, bf16[144,1152]{1,0:T(8,128)(2,1)}, u32[]{:S(2)}, u32[]{:S(2)}) collective-permute-start(bf16[144,1152]{1,0:T(8,128)(2,1)S(1)} %get-tuple-element.29), channel_id=1, source_target_pairs={{0,8},{4,12},{8,0},{12,4},{1,9},{5,13},{9,1},{13,5},{2,10},{6,14},... | collective-permute-start | bytes 995336 | tf_op jit(solution)/shard_map/ppermute | solution.py:33
  76.2 0.9 copy-start.11
  77.1 36.9 %collective-permute-start.16 = (bf16[144,1152]{1,0:T(8,128)(2,1)}, bf16[144,1152]{1,0:T(8,128)(2,1)}, u32[]{:S(2)}, u32[]{:S(2)}) collective-permute-start(bf16[144,1152]{1,0:T(8,128)(2,1)} %get-tuple-element.32), channel_id=1, source_target_pairs={{0,12},{4,0},{8,4},{12,8},{1,13},{5,1},{9,5},{13,9},{2,14},{6,2},{... | collective-permute-start | bytes 995336 | tf_op jit(solution)/shard_map/ppermute | solution.py:33
  80.0 36.0 %collective-permute-start.17 = (bf16[144,1152]{1,0:T(8,128)(2,1)}, bf16[144,1152]{1,0:T(8,128)(2,1)}, u32[]{:S(2)}, u32[]{:S(2)}) collective-permute-start(bf16[144,1152]{1,0:T(8,128)(2,1)} %get-tuple-element.33), channel_id=1, source_target_pairs={{0,8},{4,12},{8,0},{12,4},{1,9},{5,13},{9,1},{13,5},{2,10},{6,14},... | collective-permute-start | bytes 995336 | tf_op jit(solution)/shard_map/ppermute | solution.py:33
  83.9 35.0 %collective-permute-start.18 = (bf16[144,1152]{1,0:T(8,128)(2,1)}, bf16[144,1152]{1,0:T(8,128)(2,1)}, u32[]{:S(2)}, u32[]{:S(2)}) collective-permute-start(bf16[144,1152]{1,0:T(8,128)(2,1)} %get-tuple-element.34), channel_id=1, source_target_pairs={{0,4},{4,8},{8,12},{12,0},{1,5},{5,9},{9,13},{13,1},{2,6},{6,10},{... | collective-permute-start | bytes 995336 | tf_op jit(solution)/shard_map/ppermute | solution.py:33
  107.2 1.0 copy-start.1
  108.2 1.1 copy-start.10
  109.3 1.1 copy-start.12
  114.0 13.1 %collective-permute-start.10 = (bf16[144,1152]{1,0:T(8,128)(2,1)S(1)}, bf16[144,1152]{1,0:T(8,128)(2,1)S(1)}, u32[]{:S(2)}, u32[]{:S(2)}) collective-permute-start(bf16[144,1152]{1,0:T(8,128)(2,1)S(1)} %get-tuple-element.24), channel_id=1, source_target_pairs={{0,3},{1,0},{2,1},{3,2},{4,7},{5,4},{6,5},{7,6},{8,11},{9,8},{10,9... | collective-permute-start | bytes 995336 | tf_op jit(solution)/shard_map/ppermute | solution.py:33
  116.0 28.1 %collective-permute-start.11 = (bf16[144,1152]{1,0:T(8,128)(2,1)S(1)}, bf16[144,1152]{1,0:T(8,128)(2,1)S(1)}, u32[]{:S(2)}, u32[]{:S(2)}) collective-permute-start(bf16[144,1152]{1,0:T(8,128)(2,1)S(1)} %get-tuple-element.25), channel_id=1, source_target_pairs={{0,2},{1,3},{2,0},{3,1},{4,6},{5,7},{6,4},{7,5},{8,10},{9,11},{10,... | collective-permute-start | bytes 995336 | tf_op jit(solution)/shard_map/ppermute | solution.py:33
  118.9 27.1 %collective-permute-start.12 = (bf16[144,1152]{1,0:T(8,128)(2,1)S(1)}, bf16[144,1152]{1,0:T(8,128)(2,1)S(1)}, u32[]{:S(2)}, u32[]{:S(2)}) collective-permute-start(bf16[144,1152]{1,0:T(8,128)(2,1)S(1)} %get-tuple-element.26), channel_id=1, source_target_pairs={{0,1},{1,2},{2,3},{3,0},{4,5},{5,6},{6,7},{7,4},{8,9},{9,10},{10,1... | collective-permute-start | bytes 995336 | tf_op jit(solution)/shard_map/ppermute | solution.py:33
  121.3 24.7 %copy-start.16 = (bf16[144,1152]{1,0:T(8,128)(2,1)S(1)}, bf16[144,1152]{1,0:T(8,128)(2,1)}, u32[]{:S(2)}) copy-start(bf16[144,1152]{1,0:T(8,128)(2,1)} %param.2) | copy-start | bytes 995332
  127.1 20.4 %collective-permute-start.15 = (bf16[144,1152]{1,0:T(8,128)(2,1)S(1)}, bf16[144,1152]{1,0:T(8,128)(2,1)S(1)}, u32[]{:S(2)}, u32[]{:S(2)}) collective-permute-start(bf16[144,1152]{1,0:T(8,128)(2,1)S(1)} %get-tuple-element.30), channel_id=1, source_target_pairs={{0,4},{4,8},{8,12},{12,0},{1,5},{5,9},{9,13},{13,1},{2,6},{6,10},{... | collective-permute-start | bytes 995336 | tf_op jit(solution)/shard_map/ppermute | solution.py:33
  144.1 23.8 %collective-permute-start.19 = (bf16[144,1152]{1,0:T(8,128)(2,1)S(1)}, bf16[144,1152]{1,0:T(8,128)(2,1)S(1)}, u32[]{:S(2)}, u32[]{:S(2)}) collective-permute-start(bf16[144,1152]{1,0:T(8,128)(2,1)S(1)} %add_convert_fusion), channel_id=1, source_target_pairs={{0,752},{16,0},{32,16},{48,32},{64,48},{80,64},{96,80},{112,96},{1... | collective-permute-start | bytes 995336 | tf_op jit(solution)/shard_map/ppermute | solution.py:33
  146.4 21.5 %copy-start.14 = (bf16[144,1152]{1,0:T(8,128)(2,1)S(1)}, bf16[144,1152]{1,0:T(8,128)(2,1)}, u32[]{:S(2)}) copy-start(bf16[144,1152]{1,0:T(8,128)(2,1)} %param.3) | copy-start | bytes 995332

commit v2 on v0

v2 whole, which is shorter than its diff:
```python
import jax
import jax.numpy as jnp
from jax import lax
from jax.experimental import pallas as pl
from jax.experimental.pallas import tpu as pltpu
from jax.sharding import Mesh
from jax.sharding import PartitionSpec as P

SCALE = 10.0
SHIFT = -2.0
EPS = 1e-06
CORES, NX, NZ = 2, 4, 4
BLK, GRP = ("g", "core"), ("x", "z")
F32, BF16 = jnp.float32, jnp.bfloat16
MIB = 1024 * 1024
LOSS_ROWS = 16
CHUNK = 16
LANES = 128
WEIGHT = 60_000_000_000


def shifted(value, axis, steps):
    count = lax.axis_size(axis)
    return lax.ppermute(value, axis, [(i, (i + steps) % count) for i in range(count)])


def ring(value, steps):
    pairs = []
    for core in range(CORES):
        for x in range(NX):
            to = (x + (steps if core == 0 else -steps)) % NX
            pairs.append((core * NX + x, core * NX + to))
    return lax.ppermute(value, ("core", "x"), pairs)


def vmem_call(body, ins, outs, limit, scratch=(), flops=0, transcendentals=0, smem=0):
    size = sum(a.size * a.dtype.itemsize for a in list(ins) + list(outs))
    return pl.pallas_call(
        body,
        out_shape=list(outs),
        in_specs=[pl.BlockSpec(memory_space=pltpu.SMEM)] * smem
        + [pl.BlockSpec(memory_space=pltpu.VMEM)] * (len(ins) - smem),
        out_specs=[pl.BlockSpec(memory_space=pltpu.VMEM)] * len(outs),
        scratch_shapes=list(scratch),
        compiler_params=pltpu.CompilerParams(vmem_limit_bytes=limit * MIB),
        cost_estimate=pl.CostEstimate(
            flops=flops, bytes_accessed=size, transcendentals=transcendentals
        ),
    )(*ins)


def shape(dims, dtype):
    return jax.ShapeDtypeStruct(dims, dtype)


def unit_rows(values):
    wide = values.astype(F32)
    length = jnp.sqrt(jnp.sum(wide * wide, axis=-1, keepdims=True) + EPS)
    return wide / length, length


def low_kernel(img_ref, txt_ref, spread_ref, low_ref):
    unit, _ = unit_rows(txt_ref[...])
    low_ref[...] = unit.astype(BF16)
    unit, _ = unit_rows(img_ref[...])
    for z in range(NZ):
        spread_ref[z] = unit.astype(BF16)


def slopes_kernel(*refs):
    place_ref, img_all, texts = refs[0], refs[1], refs[2:6]
    slopes_ref, loss_ref, parts = refs[6], refs[7], refs[8:12]
    txt_all, scores, lanes_ref = refs[12:15]
    own = img_all.shape[0] // NZ
    pair = texts[0].shape[0]
    first = place_ref[0] * (own // CHUNK)
    for s in range(4):
        txt_all[pl.ds(s * pair, pair), :] = texts[s][...]
    scores[...] = lax.dot_general(
        img_all[...], txt_all[...], (((1,), (1,)), ((), ())), preferred_element_type=F32
    )
    width = scores.shape[1]

    def chunk(i, paired):
        rows = pl.ds(pl.multiple_of(i * CHUNK, CHUNK), CHUNK)
        logits = scores[rows, :] * SCALE + SHIFT
        if paired:
            row = lax.broadcasted_iota(jnp.int32, logits.shape, 0) + (i - first) * CHUNK
            col = lax.broadcasted_iota(jnp.int32, logits.shape, 1)
            match = row == col
            logits = jnp.where(match, -logits, logits)
        grown = jnp.exp(logits)
        losses = jnp.log1p(grown)
        slopes = SCALE * grown / (1.0 + grown)
        if paired:
            slopes = jnp.where(match, -slopes, slopes)
        slopes_ref[rows, :] = slopes.astype(BF16)
        total = losses[:, 0:LANES]
        for c in range(LANES, width, LANES):
            total = total + losses[:, c : c + LANES]
        lanes_ref[rows, :] = total

    @pl.loop(0, first)
    def _(i):
        chunk(i, False)

    @pl.loop(first, first + own // CHUNK)
    def _(i):
        chunk(i, True)

    @pl.loop(first + own // CHUNK, NZ * own // CHUNK)
    def _(i):
        chunk(i, False)

    loss_ref[...] = jnp.sum(lanes_ref[...].T, axis=0, keepdims=True)
    grads = lax.dot_general(
        slopes_ref[...], img_all[...], (((0,), (0,)), ((), ())), preferred_element_type=F32
    ).astype(BF16)
    for s in range(4):
        parts[s][...] = grads[s * pair : (s + 1) * pair, :]


def slopes_call(place, images, texts):
    rows, features = images.shape
    pair = texts[0].shape[0]
    cols = 4 * pair
    out = vmem_call(
        slopes_kernel,
        [place, images] + list(texts),
        [shape((rows, cols), BF16), shape((1, rows), F32)] + [shape((pair, features), BF16)] * 4,
        18,
        [
            pltpu.VMEM((cols, features), BF16),
            pltpu.VMEM((rows, cols), F32),
            pltpu.VMEM((rows, LANES), F32),
        ],
        flops=4 * rows * cols * features,
        transcendentals=3 * rows * cols,
        smem=1,
    )
    return out[0], out[1], out[2:6]


def image_kernel(*refs):
    slopes_ref, loss_ref = refs[0:2]
    texts, out_ref, txt_all = refs[2:6], refs[6], refs[7]
    pair = texts[0].shape[0]
    own = slopes_ref.shape[0] // 4
    for s in range(4):
        txt_all[pl.ds(s * pair, pair), :] = texts[s][...]
    grads = jnp.dot(slopes_ref[...], txt_all[...], preferred_element_type=F32).astype(BF16)
    row = lax.broadcasted_iota(jnp.int32, (LOSS_ROWS, own), 0)
    for s in range(4):
        out_ref[s, 0:own, :] = grads[s * own : (s + 1) * own, :]
        loss = loss_ref[:, s * own : (s + 1) * own]
        main = loss.astype(BF16).astype(F32)
        both = jnp.where(row == 0, main, jnp.where(row == 1, loss - main, 0.0))
        out_ref[s, own : own + LOSS_ROWS, :] = jnp.zeros((LOSS_ROWS, out_ref.shape[2]), BF16)
        out_ref[s, own : own + LOSS_ROWS, 0:own] = both.astype(BF16)


def image_call(slopes, loss, texts):
    pair, features = texts[0].shape
    rows, cols = slopes.shape
    (out,) = vmem_call(
        image_kernel,
        [slopes, loss] + list(texts),
        [shape((NZ, rows // NZ + LOSS_ROWS, features), BF16)],
        12,
        [pltpu.VMEM((cols, features), BF16)],
        flops=2 * rows * cols * features,
    )
    return out


def project(values, grads):
    unit, length = unit_rows(values)
    radial = jnp.sum(unit * grads, axis=-1, keepdims=True)
    return (grads - unit * radial) / length


def image_end_kernel(raw_ref, parts_ref, grad_ref, loss_ref):
    own = raw_ref.shape[0]
    grads = parts_ref[0, 0:own, :].astype(F32)
    tail = parts_ref[0, own : own + LOSS_ROWS, 0:own].astype(F32)
    for z in range(1, NZ):
        grads = grads + parts_ref[z, 0:own, :].astype(F32)
        tail = tail + parts_ref[z, own : own + LOSS_ROWS, 0:own].astype(F32)
    grad_ref[...] = project(raw_ref[...], grads)
    loss_ref[...] = jnp.sum(tail, axis=0, keepdims=True)


def text_end_kernel(raw_ref, a, b, c, home, grad_ref):
    own = raw_ref.shape[0]
    grads = a[0:own, :].astype(F32) + b[0:own, :].astype(F32)
    grads = grads + c[0:own, :].astype(F32) + home[...].astype(F32)
    grad_ref[...] = project(raw_ref[...], grads)


def later_kernel(a, b, c, out_ref):
    own = out_ref.shape[0]
    total = a[own:, :].astype(F32) + b[own:, :].astype(F32) + c[own:, :].astype(F32)
    out_ref[...] = total.astype(BF16)


def stack_kernel(a, b, out_ref):
    own = a.shape[0]
    out_ref[0:own, :] = a[...]
    out_ref[own:, :] = b[...]


def add_kernel(a, b, out_ref):
    out_ref[...] = (a[...].astype(F32) + b[...].astype(F32)).astype(BF16)


def on_device(images, texts):
    own, features = images.shape
    unit = shape((own, features), BF16)
    spread, txt_low = vmem_call(
        low_kernel, [images, texts], [shape((NZ, own, features), BF16), unit], 8
    )
    moved = shifted(txt_low, BLK, 1)
    img_all = lax.all_to_all(spread, "z", 0, 0).reshape(NZ * own, features)
    (both,) = vmem_call(
        stack_kernel, [txt_low, moved], [shape((2 * own, features), BF16)], 8, flops=WEIGHT
    )
    after, before = ring(both, 1), ring(both, -1)
    txt_slots = [both, after, before, ring(after, 1)]

    place = lax.axis_index("z").reshape(1).astype(jnp.int32)
    slopes, loss, txt_parts = slopes_call(place, img_all, txt_slots)
    far = ring(txt_parts[3], -1)
    img_parts = image_call(slopes, loss, txt_slots)
    img_back = lax.all_to_all(img_parts, "z", 0, 0)
    (joined,) = vmem_call(add_kernel, [txt_parts[1], far], [shape(far.shape, BF16)], 8, flops=WEIGHT)
    back1, back2 = ring(joined, -1), ring(txt_parts[2], 1)
    (later,) = vmem_call(later_kernel, [txt_parts[0], back1, back2], [unit], 8)
    home = shifted(later, BLK, -1)

    wide = shape((own, features), F32)
    image_grad, row_loss = vmem_call(
        image_end_kernel, [images, img_back], [wide, shape((1, own), F32)], 12
    )
    (text_grad,) = vmem_call(
        text_end_kernel, [texts, txt_parts[0], back1, back2, home], [wide], 12
    )
    return (row_loss.reshape(own), image_grad, text_grad)


def solution(mesh):
    groups = mesh.devices.shape[0] // CORES
    fine = Mesh(mesh.devices.reshape(groups, CORES, NX, NZ), BLK + GRP)
    rows = P(BLK + GRP, None)
    return jax.shard_map(
        on_device,
        mesh=fine,
        in_specs=(rows, rows),
        out_specs=(P(BLK + GRP), rows, rows),
        check_vma=False,
    )
```

time: 576 us -> 141 us (0.24)
  the two profiles are of different devices: /device:TPU:1 before, /device:TPU:169 now
where the time goes in v2:
time: 141 us; the launch traced here: 140 us
  waiting for transfers between devices  66.8 us (47%)
  starting transfers between devices  49 us (35%)
  Pallas kernels  17.4 us (12%)
  local copies, waits for them, and re-layouts  5.85 us (4%)
    ppermute x2, waiting for transfers between devices, shifted(): lax.ppermute(value, axis, [(i, (i + steps) % count) for i in range(count)])  39.5 us
    ppermute x6, waiting for transfers between devices, ring(): return lax.ppermute(value, ('core', 'x'), pairs)  27.3 us
    ppermute x6, starting transfers between devices, ring(): return lax.ppermute(value, ('core', 'x'), pairs)  20.7 us
    ppermute x2, starting transfers between devices, shifted(): lax.ppermute(value, axis, [(i, (i + steps) % count) for i in range(count)])  18.2 us
    pallas_call x8, Pallas kernels, vmem_call(): pl.pallas_call(body, out_shape=list(outs), in_specs=[pl.BlockSpec(memory_...  17.4 us
    unnamed x18, local copies, waits for them, and re-layouts  5.85 us
    all_to_all x1, starting transfers between devices, on_device(): img_all = lax.all_to_all(spread, 'z', 0, 0).reshape(NZ * own, features)  5.16 us
    all_to_all x1, starting transfers between devices, on_device(): img_back = lax.all_to_all(img_parts, 'z', 0, 0)  4.91 us
  transfers between devices with their start and end apart: 10, of which 6 were waited for; matrix products, arithmetic and copies ran while one was open for 0% of the time, Pallas kernels for 4%

profile of v2, /device:TPU:169, one launch (start us, length us, event | category | flops | bytes accessed | tf_op | source)
XLA Modules:
  0.0 139.8 jit_solution(93237251875907765)
XLA Ops:
  0.6 0.0 copy-start.1
  0.6 1.0 copy-done.1
  1.6 0.0 copy-start.3
  1.6 1.0 copy-done.3
  2.6 1.3 shard_map.49
  3.9 11.2 %collective-permute-start = (bf16[144,1152]{1,0:T(8,128)(2,1)S(1)}, bf16[144,1152]{1,0:T(8,128)(2,1)S(1)}, u32[]{:S(2)}, u32[]{:S(2)}) collective-permute-start(bf16[144,1152]{1,0:T(8,128)(2,1)S(1)} %get-tuple-element.14.a), channel_id=1, source_target_pairs={{0,16},{16,32},{32,48},{48,64},{64,80},{80,96},{96,112},{112,128},... | collective-permute-start | bytes 995336 | tf_op jit(solution)/shard_map/ppermute | solution.py:24
  15.1 5.2 %all-to-all-start = ((bf16[4,144,1152]{2,1,0:T(8,128)(2,1)}), bf16[4,144,1152]{2,1,0:T(8,128)(2,1)S(1)}, u32[]{:S(2)}, u32[]{:S(2)}) async-start(bf16[4,144,1152]{2,1,0:T(8,128)(2,1)} %get-tuple-element.13), calls=%async_computation | async-start | bytes 2654208 | tf_op jit(solution)/shard_map/all_to_all | solution.py:223
  20.2 13.9 %collective-permute-done.b = bf16[144,1152]{1,0:T(8,128)(2,1)S(1)} collective-permute-done((bf16[144,1152]{1,0:T(8,128)(2,1)S(1)}, bf16[144,1152]{1,0:T(8,128)(2,1)S(1)}, u32[]{:S(2)}, u32[]{:S(2)}) %collective-permute-start) | collective-permute-done | bytes 331808 | tf_op jit(solution)/shard_map/ppermute | solution.py:24
  34.2 4.4 %collective-permute-start.1 = (bf16[288,1152]{1,0:T(8,128)(2,1)S(1)}, bf16[288,1152]{1,0:T(8,128)(2,1)S(1)}, u32[]{:S(2)}, u32[]{:S(2)}) collective-permute-start(bf16[288,1152]{1,0:T(8,128)(2,1)S(1)} %shard_map.50.refs_2_), channel_id=1, source_target_pairs={{0,4},{4,8},{8,12},{12,0},{16,28},{20,16},{24,20},{28,24},{1,5},{5... | collective-permute-start | bytes 1990664 | tf_op jit(solution)/shard_map/ppermute | solution.py:33
  38.6 1.9 %collective-permute-start.2 = (bf16[288,1152]{1,0:T(8,128)(2,1)S(1)}, bf16[288,1152]{1,0:T(8,128)(2,1)S(1)}, u32[]{:S(2)}, u32[]{:S(2)}) collective-permute-start(bf16[288,1152]{1,0:T(8,128)(2,1)S(1)} %shard_map.50.refs_2_), channel_id=1, source_target_pairs={{0,12},{4,0},{8,4},{12,8},{16,20},{20,24},{24,28},{28,16},{1,13},{... | collective-permute-start | bytes 1990664 | tf_op jit(solution)/shard_map/ppermute | solution.py:33
  40.5 7.5 %collective-permute-done.1.refs_3_ = bf16[288,1152]{1,0:T(8,128)(2,1)S(1)} collective-permute-done((bf16[288,1152]{1,0:T(8,128)(2,1)S(1)}, bf16[288,1152]{1,0:T(8,128)(2,1)S(1)}, u32[]{:S(2)}, u32[]{:S(2)}) %collective-permute-start.1) | collective-permute-done | bytes 663584 | tf_op jit(solution)/shard_map/ppermute | solution.py:33
  48.0 5.3 %collective-permute-start.3 = (bf16[288,1152]{1,0:T(8,128)(2,1)S(1)}, bf16[288,1152]{1,0:T(8,128)(2,1)}, u32[]{:S(2)}, u32[]{:S(2)}) collective-permute-start(bf16[288,1152]{1,0:T(8,128)(2,1)S(1)} %collective-permute-done.1.refs_3_), channel_id=1, source_target_pairs={{0,4},{4,8},{8,12},{12,0},{16,28},{20,16},{24,20},{28,24},{1,5},{5... | collective-permute-start | bytes 1990664 | tf_op jit(solution)/shard_map/ppermute | solution.py:33
  53.3 3.4 %collective-permute-done.2.refs_4_ = bf16[288,1152]{1,0:T(8,128)(2,1)S(1)} collective-permute-done((bf16[288,1152]{1,0:T(8,128)(2,1)S(1)}, bf16[288,1152]{1,0:T(8,128)(2,1)S(1)}, u32[]{:S(2)}, u32[]{:S(2)}) %collective-permute-start.2) | collective-permute-done | bytes 663584 | tf_op jit(solution)/shard_map/ppermute | solution.py:33
  56.7 0.0 copy-start.5
  56.7 0.8 copy-done.5
  57.6 3.4 %collective-permute-done.3.refs_5_ = bf16[288,1152]{1,0:T(8,128)(2,1)} collective-permute-done((bf16[288,1152]{1,0:T(8,128)(2,1)S(1)}, bf16[288,1152]{1,0:T(8,128)(2,1)}, u32[]{:S(2)}, u32[]{:S(2)}) %collective-permute-start.3) | collective-permute-done | bytes 663584 | tf_op jit(solution)/shard_map/ppermute | solution.py:33
  60.9 0.0 all-to-all-done
  60.9 0.0 copy-start.6
  60.9 1.1 copy-done.6
  62.0 9.0 %shard_map.51 = (bf16[576,1152]{1,0:T(8,128)(2,1)S(1)}, f32[1,576]{1,0:T(1,128)S(1)}, bf16[288,1152]{1,0:T(8,128)(2,1)S(1)}, bf16[288,1152]{1,0:T(8,128)(2,1)S(1...) custom-call(s32[1]{0:T(128)} %bitcast.refs_0_, bf16[576,1152]{1,0:T(8,128)(2,1)S(1)} %bitcast.3, ...), custom_call_target="tpu_custom_call" | custom-call | flops 3057647616 | bytes 7964932 | tf_op jit(solution)/shard_map/pallas_call | solution.py:38
  71.0 0.0 copy-start.7
  71.0 0.8 copy-done.7
  71.9 2.1 %collective-permute-start.4 = (bf16[288,1152]{1,0:T(8,128)(2,1)}, bf16[288,1152]{1,0:T(8,128)(2,1)}, u32[]{:S(2)}, u32[]{:S(2)}) collective-permute-start(bf16[288,1152]{1,0:T(8,128)(2,1)} %get-tuple-element.21), channel_id=1, source_target_pairs={{0,12},{4,0},{8,4},{12,8},{16,20},{20,24},{24,28},{28,16},{1,13},{... | collective-permute-start | bytes 1990664 | tf_op jit(solution)/shard_map/ppermute | solution.py:33
  74.0 4.9 %collective-permute-start.6 = (bf16[288,1152]{1,0:T(8,128)(2,1)}, bf16[288,1152]{1,0:T(8,128)(2,1)S(1)}, u32[]{:S(2)}, u32[]{:S(2)}) collective-permute-start(bf16[288,1152]{1,0:T(8,128)(2,1)} %get-tuple-element.22), channel_id=1, source_target_pairs={{0,4},{4,8},{8,12},{12,0},{16,28},{20,16},{24,20},{28,24},{1,5},{5... | collective-permute-start | bytes 1990664 | tf_op jit(solution)/shard_map/ppermute | solution.py:33
  78.9 3.2 %shard_map.52 = bf16[4,160,1152]{2,1,0:T(8,128)(2,1)S(1)} custom-call(bf16[576,1152]{1,0:T(8,128)(2,1)S(1)} %get-tuple-element.15.refs_0_, f32[1,576]{1,0:T(1,128)S(1)} %get-tuple-element.16.refs_1_, bf16[288,1152]{1,0:T(8,128)(2,1)S(1)} %shard_map.50.refs_2_, bf16[288,1152]{1,0:T(8,128)(2,1)S(1)} %collective-permute-done.1.refs_3_, ...), custom_call_target="tpu_custom_call" | custom-call | flops 1528823808 | bytes 5458176 | tf_op jit(solution)/shard_map/pallas_call | solution.py:38
  82.2 0.0 copy-start
  82.2 1.1 copy-done
  83.3 0.0 copy-start.8
  83.3 4.9 %all-to-all-start.1 = ((bf16[4,160,1152]{2,1,0:T(8,128)(2,1)}), bf16[4,160,1152]{2,1,0:T(8,128)(2,1)S(1)}, u32[]{:S(2)}, u32[]{:S(2)}) async-start(bf16[4,160,1152]{2,1,0:T(8,128)(2,1)} %copy-done), calls=%async_computation.1 | async-start | bytes 2949120 | tf_op jit(solution)/shard_map/all_to_all | solution.py:234
  88.2 0.0 collective-permute-done.4.b
  88.2 0.0 copy-done.8
  88.2 1.2 shard_map.54
  89.5 0.0 copy-start.2
  89.5 2.1 %collective-permute-start.5 = (bf16[288,1152]{1,0:T(8,128)(2,1)S(1)}, bf16[288,1152]{1,0:T(8,128)(2,1)S(1)}, u32[]{:S(2)}, u32[]{:S(2)}) collective-permute-start(bf16[288,1152]{1,0:T(8,128)(2,1)S(1)} %shard_map.54), channel_id=1, source_target_pairs={{0,12},{4,0},{8,4},{12,8},{16,20},{20,24},{24,28},{28,16},{1,13},{... | collective-permute-start | bytes 1990664 | tf_op jit(solution)/shard_map/ppermute | solution.py:33
  91.5 0.0 collective-permute-done.6.c
  91.5 13.0 %collective-permute-done.5.b = bf16[288,1152]{1,0:T(8,128)(2,1)S(1)} collective-permute-done((bf16[288,1152]{1,0:T(8,128)(2,1)S(1)}, bf16[288,1152]{1,0:T(8,128)(2,1)S(1)}, u32[]{:S(2)}, u32[]{:S(2)}) %collective-permute-start.5) | collective-permute-done | bytes 663584 | tf_op jit(solution)/shard_map/ppermute | solution.py:33
  104.5 0.1 shard_map.55
  104.7 0.0 copy-start.4
  104.7 7.0 %collective-permute-start.7 = (bf16[144,1152]{1,0:T(8,128)(2,1)S(1)}, bf16[144,1152]{1,0:T(8,128)(2,1)S(1)}, u32[]{:S(2)}, u32[]{:S(2)}) collective-permute-start(bf16[144,1152]{1,0:T(8,128)(2,1)S(1)} %shard_map.55), channel_id=1, source_target_pairs={{0,752},{16,0},{32,16},{48,32},{64,48},{80,64},{96,80},{112,96},{1... | collective-permute-start | bytes 995336 | tf_op jit(solution)/shard_map/ppermute | solution.py:24
  111.7 25.6 %collective-permute-done.7.home = bf16[144,1152]{1,0:T(8,128)(2,1)S(1)} collective-permute-done((bf16[144,1152]{1,0:T(8,128)(2,1)S(1)}, bf16[144,1152]{1,0:T(8,128)(2,1)S(1)}, u32[]{:S(2)}, u32[]{:S(2)}) %collective-permute-start.7) | collective-permute-done | bytes 331808 | tf_op jit(solution)/shard_map/ppermute | solution.py:24
  137.3 0.0 copy-done.2
  137.3 1.2 shard_map.56
  138.5 0.0 all-to-all-done.1.parts_ref
  138.5 0.0 copy-done.4
  138.6 1.2 shard_map.53
  (1 shorter events, 0.0 us)
Async XLA Ops:
  0.6 1.0 copy-start.1
  1.6 1.0 copy-start.3
  3.9 30.2 %collective-permute-start = (bf16[144,1152]{1,0:T(8,128)(2,1)S(1)}, bf16[144,1152]{1,0:T(8,128)(2,1)S(1)}, u32[]{:S(2)}, u32[]{:S(2)}) collective-permute-start(bf16[144,1152]{1,0:T(8,128)(2,1)S(1)} %get-tuple-element.14.a), channel_id=1, source_target_pairs={{0,16},{16,32},{32,48},{48,64},{64,80},{80,96},{96,112},{112,128},... | collective-permute-start | bytes 995336 | tf_op jit(solution)/shard_map/ppermute | solution.py:24
  15.1 45.9 %all-to-all-start = ((bf16[4,144,1152]{2,1,0:T(8,128)(2,1)}), bf16[4,144,1152]{2,1,0:T(8,128)(2,1)S(1)}, u32[]{:S(2)}, u32[]{:S(2)}) async-start(bf16[4,144,1152]{2,1,0:T(8,128)(2,1)} %get-tuple-element.13), calls=%async_computation | async-start | bytes 2654208 | tf_op jit(solution)/shard_map/all_to_all | solution.py:223
  34.2 13.8 %collective-permute-start.1 = (bf16[288,1152]{1,0:T(8,128)(2,1)S(1)}, bf16[288,1152]{1,0:T(8,128)(2,1)S(1)}, u32[]{:S(2)}, u32[]{:S(2)}) collective-permute-start(bf16[288,1152]{1,0:T(8,128)(2,1)S(1)} %shard_map.50.refs_2_), channel_id=1, source_target_pairs={{0,4},{4,8},{8,12},{12,0},{16,28},{20,16},{24,20},{28,24},{1,5},{5... | collective-permute-start | bytes 1990664 | tf_op jit(solution)/shard_map/ppermute | solution.py:33
  38.6 18.1 %collective-permute-start.2 = (bf16[288,1152]{1,0:T(8,128)(2,1)S(1)}, bf16[288,1152]{1,0:T(8,128)(2,1)S(1)}, u32[]{:S(2)}, u32[]{:S(2)}) collective-permute-start(bf16[288,1152]{1,0:T(8,128)(2,1)S(1)} %shard_map.50.refs_2_), channel_id=1, source_target_pairs={{0,12},{4,0},{8,4},{12,8},{16,20},{20,24},{24,28},{28,16},{1,13},{... | collective-permute-start | bytes 1990664 | tf_op jit(solution)/shard_map/ppermute | solution.py:33
  48.0 12.9 %collective-permute-start.3 = (bf16[288,1152]{1,0:T(8,128)(2,1)S(1)}, bf16[288,1152]{1,0:T(8,128)(2,1)}, u32[]{:S(2)}, u32[]{:S(2)}) collective-permute-start(bf16[288,1152]{1,0:T(8,128)(2,1)S(1)} %collective-permute-done.1.refs_3_), channel_id=1, source_target_pairs={{0,4},{4,8},{8,12},{12,0},{16,28},{20,16},{24,20},{28,24},{1,5},{5... | collective-permute-start | bytes 1990664 | tf_op jit(solution)/shard_map/ppermute | solution.py:33
  56.7 0.8 copy-start.5
  60.9 1.1 copy-start.6
  71.0 0.8 copy-start.7
  71.9 16.4 %collective-permute-start.4 = (bf16[288,1152]{1,0:T(8,128)(2,1)}, bf16[288,1152]{1,0:T(8,128)(2,1)}, u32[]{:S(2)}, u32[]{:S(2)}) collective-permute-start(bf16[288,1152]{1,0:T(8,128)(2,1)} %get-tuple-element.21), channel_id=1, source_target_pairs={{0,12},{4,0},{8,4},{12,8},{16,20},{20,24},{24,28},{28,16},{1,13},{... | collective-permute-start | bytes 1990664 | tf_op jit(solution)/shard_map/ppermute | solution.py:33
  74.0 17.6 %collective-permute-start.6 = (bf16[288,1152]{1,0:T(8,128)(2,1)}, bf16[288,1152]{1,0:T(8,128)(2,1)S(1)}, u32[]{:S(2)}, u32[]{:S(2)}) collective-permute-start(bf16[288,1152]{1,0:T(8,128)(2,1)} %get-tuple-element.22), channel_id=1, source_target_pairs={{0,4},{4,8},{8,12},{12,0},{16,28},{20,16},{24,20},{28,24},{1,5},{5... | collective-permute-start | bytes 1990664 | tf_op jit(solution)/shard_map/ppermute | solution.py:33
  82.2 1.1 copy-start
  83.3 4.9 %copy-start.8 = (bf16[288,1152]{1,0:T(8,128)(2,1)S(1)}, bf16[288,1152]{1,0:T(8,128)(2,1)}, u32[]{:S(2)}) copy-start(bf16[288,1152]{1,0:T(8,128)(2,1)} %copy-done.7) | copy-start | bytes 1990660
  83.3 55.3 %all-to-all-start.1 = ((bf16[4,160,1152]{2,1,0:T(8,128)(2,1)}), bf16[4,160,1152]{2,1,0:T(8,128)(2,1)S(1)}, u32[]{:S(2)}, u32[]{:S(2)}) async-start(bf16[4,160,1152]{2,1,0:T(8,128)(2,1)} %copy-done), calls=%async_computation.1 | async-start | bytes 2949120 | tf_op jit(solution)/shard_map/all_to_all | solution.py:234
  89.5 47.8 %copy-start.2 = (bf16[144,1152]{1,0:T(8,128)(2,1)S(1)}, bf16[144,1152]{1,0:T(8,128)(2,1)}, u32[]{:S(2)}) copy-start(bf16[144,1152]{1,0:T(8,128)(2,1)} %raw_ref.3) | copy-start | bytes 995332
  89.5 15.1 %collective-permute-start.5 = (bf16[288,1152]{1,0:T(8,128)(2,1)S(1)}, bf16[288,1152]{1,0:T(8,128)(2,1)S(1)}, u32[]{:S(2)}, u32[]{:S(2)}) collective-permute-start(bf16[288,1152]{1,0:T(8,128)(2,1)S(1)} %shard_map.54), channel_id=1, source_target_pairs={{0,12},{4,0},{8,4},{12,8},{16,20},{20,24},{24,28},{28,16},{1,13},{... | collective-permute-start | bytes 1990664 | tf_op jit(solution)/shard_map/ppermute | solution.py:33
  104.7 33.9 %copy-start.4 = (bf16[144,1152]{1,0:T(8,128)(2,1)S(1)}, bf16[144,1152]{1,0:T(8,128)(2,1)}, u32[]{:S(2)}) copy-start(bf16[144,1152]{1,0:T(8,128)(2,1)} %raw_ref.2) | copy-start | bytes 995332
  104.7 32.6 %collective-permute-start.7 = (bf16[144,1152]{1,0:T(8,128)(2,1)S(1)}, bf16[144,1152]{1,0:T(8,128)(2,1)S(1)}, u32[]{:S(2)}, u32[]{:S(2)}) collective-permute-start(bf16[144,1152]{1,0:T(8,128)(2,1)S(1)} %shard_map.55), channel_id=1, source_target_pairs={{0,752},{16,0},{32,16},{48,32},{64,48},{80,64},{96,80},{112,96},{1... | collective-permute-start | bytes 995336 | tf_op jit(solution)/shard_map/ppermute | solution.py:24

commit v3 on v2

v3 whole, which is shorter than its diff:
```python
import functools

import jax
import jax.numpy as jnp
from jax import lax
from jax.experimental import pallas as pl
from jax.experimental.pallas import tpu as pltpu
from jax.sharding import Mesh
from jax.sharding import PartitionSpec as P

SCALE = 10.0
SHIFT = -2.0
EPS = 1e-06
CORES, NX, NZ = 2, 4, 4
BLK, GRP = ("g", "core"), ("x", "z")
F32, BF16 = jnp.float32, jnp.bfloat16
MIB = 1024 * 1024
LOSS_ROWS = 16
CHUNK = 16
LANES = 128
WEIGHT = 60_000_000_000


def shifted(value, axis, steps):
    count = lax.axis_size(axis)
    return lax.ppermute(value, axis, [(i, (i + steps) % count) for i in range(count)])


def vmem_call(body, ins, outs, limit, scratch=(), flops=0, transcendentals=0, smem=0):
    size = sum(a.size * a.dtype.itemsize for a in list(ins) + list(outs))
    return pl.pallas_call(
        body,
        out_shape=list(outs),
        in_specs=[pl.BlockSpec(memory_space=pltpu.SMEM)] * smem
        + [pl.BlockSpec(memory_space=pltpu.VMEM)] * (len(ins) - smem),
        out_specs=[pl.BlockSpec(memory_space=pltpu.VMEM)] * len(outs),
        scratch_shapes=list(scratch),
        compiler_params=pltpu.CompilerParams(vmem_limit_bytes=limit * MIB),
        cost_estimate=pl.CostEstimate(
            flops=flops, bytes_accessed=size, transcendentals=transcendentals
        ),
    )(*ins)


def shape(dims, dtype):
    return jax.ShapeDtypeStruct(dims, dtype)


def unit_rows(values):
    wide = values.astype(F32)
    length = jnp.sqrt(jnp.sum(wide * wide, axis=-1, keepdims=True) + EPS)
    return wide / length, length


def low_kernel(img_ref, txt_ref, spread_ref, low_ref):
    unit, _ = unit_rows(img_ref[...])
    for z in range(NZ):
        spread_ref[z] = unit.astype(BF16)
    unit, _ = unit_rows(txt_ref[...])
    low_ref[...] = unit.astype(BF16)


def moved_kernel(txt_ref, low_ref):
    unit, _ = unit_rows(txt_ref[...])
    low_ref[...] = unit.astype(BF16)


def slopes_kernel(*refs):
    place_ref, img_all, texts = refs[0], refs[1], refs[2:10]
    slopes_ref, out_ref = refs[10:12]
    txt_all, scores, lanes_ref = refs[12:15]
    own = img_all.shape[0] // NZ
    first = place_ref[0] * (own // CHUNK)
    for s in range(8):
        txt_all[pl.ds(s * own, own), :] = texts[s][...]
    scores[...] = lax.dot_general(
        img_all[...], txt_all[...], (((1,), (1,)), ((), ())), preferred_element_type=F32
    )
    width = scores.shape[1]

    def chunk(i, paired):
        rows = pl.ds(pl.multiple_of(i * CHUNK, CHUNK), CHUNK)
        logits = scores[rows, :] * SCALE + SHIFT
        if paired:
            row = lax.broadcasted_iota(jnp.int32, logits.shape, 0) + (i - first) * CHUNK
            col = lax.broadcasted_iota(jnp.int32, logits.shape, 1)
            match = row == col
            logits = jnp.where(match, -logits, logits)
        grown = jnp.exp(logits)
        losses = jnp.log1p(grown)
        slopes = SCALE * grown / (1.0 + grown)
        if paired:
            slopes = jnp.where(match, -slopes, slopes)
        slopes_ref[rows, :] = slopes.astype(BF16)
        total = losses[:, 0:LANES]
        for c in range(LANES, width, LANES):
            total = total + losses[:, c : c + LANES]
        lanes_ref[rows, :] = total

    @pl.loop(0, first)
    def _(i):
        chunk(i, False)

    @pl.loop(first, first + own // CHUNK)
    def _(i):
        chunk(i, True)

    @pl.loop(first + own // CHUNK, NZ * own // CHUNK)
    def _(i):
        chunk(i, False)

    loss_row = jnp.sum(lanes_ref[...].T, axis=0, keepdims=True)
    grads = jnp.dot(slopes_ref[...], txt_all[...], preferred_element_type=F32).astype(BF16)
    row = lax.broadcasted_iota(jnp.int32, (LOSS_ROWS, own), 0)
    for s in range(NZ):
        out_ref[s, 0:own, :] = grads[s * own : (s + 1) * own, :]
        loss = loss_row[:, s * own : (s + 1) * own]
        main = loss.astype(BF16).astype(F32)
        both = jnp.where(row == 0, main, jnp.where(row == 1, loss - main, 0.0))
        out_ref[s, own : own + LOSS_ROWS, :] = jnp.zeros((LOSS_ROWS, out_ref.shape[2]), BF16)
        out_ref[s, own : own + LOSS_ROWS, 0:own] = both.astype(BF16)


def slopes_call(place, images, texts):
    rows, features = images.shape
    own = rows // NZ
    cols = len(texts) * own
    return vmem_call(
        slopes_kernel,
        [place, images] + list(texts),
        [shape((rows, cols), BF16), shape((NZ, own + LOSS_ROWS, features), BF16)],
        18,
        [
            pltpu.VMEM((cols, features), BF16),
            pltpu.VMEM((rows, cols), F32),
            pltpu.VMEM((rows, LANES), F32),
        ],
        flops=4 * rows * cols * features,
        transcendentals=3 * rows * cols,
        smem=1,
    )


def text_kernel(base, slopes_ref, img_all, *parts):
    own = parts[0].shape[0]
    cols = len(parts) * own
    wide = slopes_ref.shape[1]
    start = base * cols // LANES * LANES
    grads = lax.dot_general(
        slopes_ref[:, start : wide if base else -(-cols // LANES) * LANES],
        img_all[...],
        (((0,), (0,)), ((), ())),
        preferred_element_type=F32,
    ).astype(BF16)
    skip = base * cols - start
    for s, part in enumerate(parts):
        part[...] = grads[skip + s * own : skip + (s + 1) * own, :]


def text_call(base, slopes, images):
    rows, features = images.shape
    own = rows // NZ
    return vmem_call(
        functools.partial(text_kernel, base),
        [slopes, images],
        [shape((own, features), BF16)] * NX,
        12,
        flops=2 * rows * NX * own * features,
    )


def project(values, grads):
    unit, length = unit_rows(values)
    radial = jnp.sum(unit * grads, axis=-1, keepdims=True)
    return (grads - unit * radial) / length


def image_end_kernel(raw_ref, parts_ref, grad_ref, loss_ref):
    own = raw_ref.shape[0]
    grads = parts_ref[0, 0:own, :].astype(F32)
    tail = parts_ref[0, own : own + LOSS_ROWS, 0:own].astype(F32)
    for z in range(1, NZ):
        grads = grads + parts_ref[z, 0:own, :].astype(F32)
        tail = tail + parts_ref[z, own : own + LOSS_ROWS, 0:own].astype(F32)
    grad_ref[...] = project(raw_ref[...], grads)
    loss_ref[...] = jnp.sum(tail, axis=0, keepdims=True)


def text_end_kernel(raw_ref, a, b, c, d, home, grad_ref):
    grads = a[...].astype(F32) + b[...].astype(F32)
    grads = grads + c[...].astype(F32) + d[...].astype(F32)
    grads = grads + home[...].astype(F32)
    grad_ref[...] = project(raw_ref[...], grads)


def later_kernel(a, b, c, d, out_ref):
    total = a[...].astype(F32) + b[...].astype(F32)
    total = total + c[...].astype(F32) + d[...].astype(F32)
    out_ref[...] = total.astype(BF16)


def spread_x(value):
    return [value] + [shifted(value, "x", s) for s in (2, 1, 3)]


def return_x(parts):
    return [parts[0]] + [shifted(p, "x", -s) for p, s in zip(parts[1:], (2, 1, 3))]


def on_device(images, texts):
    own, features = images.shape
    unit = shape((own, features), BF16)
    moved = shifted(texts, BLK, 1)
    spread, txt_low = vmem_call(
        low_kernel, [images, texts], [shape((NZ, own, features), BF16), unit], 8
    )
    img_all = lax.all_to_all(spread, "z", 0, 0).reshape(NZ * own, features)
    now_slots = spread_x(txt_low)
    (moved_low,) = vmem_call(moved_kernel, [moved], [unit], 8, flops=WEIGHT)
    later_slots = spread_x(moved_low)

    place = lax.axis_index("z").reshape(1).astype(jnp.int32)
    slopes, img_parts = slopes_call(place, img_all, now_slots + later_slots)
    img_back = lax.all_to_all(img_parts, "z", 0, 0)
    later_back = return_x(text_call(1, slopes, img_all))
    (later,) = vmem_call(later_kernel, later_back, [unit], 8)
    home = shifted(later, BLK, -1)
    now_back = return_x(text_call(0, slopes, img_all))

    wide = shape((own, features), F32)
    image_grad, row_loss = vmem_call(
        image_end_kernel, [images, img_back], [wide, shape((1, own), F32)], 12
    )
    (text_grad,) = vmem_call(text_end_kernel, [texts] + now_back + [home], [wide], 12)
    return (row_loss.reshape(own), image_grad, text_grad)


def solution(mesh):
    groups = mesh.devices.shape[0] // CORES
    fine = Mesh(mesh.devices.reshape(groups, CORES, NX, NZ), BLK + GRP)
    rows = P(BLK + GRP, None)
    return jax.shard_map(
        on_device,
        mesh=fine,
        in_specs=(rows, rows),
        out_specs=(P(BLK + GRP), rows, rows),
        check_vma=False,
    )
```

time: 141 us -> 130 us (0.922)
  the two profiles are of different devices: /device:TPU:169 before, /device:TPU:113 now
where the time goes in v3:
time: 130 us; the launch traced here: 129 us
  starting transfers between devices  61.8 us (48%)
  waiting for transfers between devices  46.3 us (36%)
  Pallas kernels  15.9 us (12%)
  local copies, waits for them, and re-layouts  4.36 us (3%)
    ppermute x14, starting transfers between devices, shifted(): lax.ppermute(value, axis, [(i, (i + steps) % count) for i in range(count)])  50.6 us
    ppermute x14, waiting for transfers between devices, shifted(): lax.ppermute(value, axis, [(i, (i + steps) % count) for i in range(count)])  38.2 us
    pallas_call x8, Pallas kernels, vmem_call(): pl.pallas_call(body, out_shape=list(outs), in_specs=[pl.BlockSpec(memory_...  15.9 us
    all_to_all x1, waiting for transfers between devices, on_device(): img_all = lax.all_to_all(spread, 'z', 0, 0).reshape(NZ * own, features)  8.07 us
    all_to_all x1, starting transfers between devices, on_device(): img_all = lax.all_to_all(spread, 'z', 0, 0).reshape(NZ * own, features)  6.07 us
    all_to_all x1, starting transfers between devices, on_device(): img_back = lax.all_to_all(img_parts, 'z', 0, 0)  5.15 us
    unnamed x14, local copies, waits for them, and re-layouts  4.36 us
  transfers between devices with their start and end apart: 16, of which 7 were waited for; matrix products, arithmetic and copies ran while one was open for 0% of the time, Pallas kernels for 4%

profile of v3, /device:TPU:113, one launch (start us, length us, event | category | flops | bytes accessed | tf_op | source)
XLA Modules:
  0.0 129.3 jit_solution(1568445387728990237)
XLA Ops:
  0.6 11.2 %collective-permute-start.3 = (bf16[144,1152]{1,0:T(8,128)(2,1)}, bf16[144,1152]{1,0:T(8,128)(2,1)S(1)}, u32[]{:S(2)}, u32[]{:S(2)}) collective-permute-start(bf16[144,1152]{1,0:T(8,128)(2,1)} %raw_ref.3), channel_id=1, source_target_pairs={{0,16},{16,32},{32,48},{48,64},{64,80},{80,96},{96,112},{112,128},... | collective-permute-start | bytes 995336 | tf_op jit(solution)/shard_map/ppermute | solution.py:26
  11.8 0.0 copy-start
  11.8 1.0 copy-done
  12.8 0.0 copy-start.2
  12.8 1.0 copy-done.2
  13.8 1.3 %shard_map.49 = (bf16[4,144,1152]{2,1,0:T(8,128)(2,1)}, bf16[144,1152]{1,0:T(8,128)(2,1)S(1)}) custom-call(bf16[144,1152]{1,0:T(8,128)(2,1)S(1)} %copy-done, bf16[144,1152]{1,0:T(8,128)(2,1)S(1)} %copy-done.2), custom_call_target="tpu_custom_call" | custom-call | bytes 2322432 | tf_op jit(solution)/shard_map/pallas_call | solution.py:31
  15.1 4.4 %collective-permute-start.2 = (bf16[144,1152]{1,0:T(8,128)(2,1)S(1)}, bf16[144,1152]{1,0:T(8,128)(2,1)S(1)}, u32[]{:S(2)}, u32[]{:S(2)}) collective-permute-start(bf16[144,1152]{1,0:T(8,128)(2,1)S(1)} %get-tuple-element.18.refs_2_), channel_id=1, source_target_pairs={{0,12},{4,0},{8,4},{12,8},{1,13},{5,1},{9,5},{13,9},{2,14},{6,2},{... | collective-permute-start | bytes 995336 | tf_op jit(solution)/shard_map/ppermute | solution.py:26
  19.5 1.9 %collective-permute-start.1 = (bf16[144,1152]{1,0:T(8,128)(2,1)S(1)}, bf16[144,1152]{1,0:T(8,128)(2,1)S(1)}, u32[]{:S(2)}, u32[]{:S(2)}) collective-permute-start(bf16[144,1152]{1,0:T(8,128)(2,1)S(1)} %get-tuple-element.18.refs_2_), channel_id=1, source_target_pairs={{0,4},{4,8},{8,12},{12,0},{1,5},{5,9},{9,13},{13,1},{2,6},{6,10},{... | collective-permute-start | bytes 995336 | tf_op jit(solution)/shard_map/ppermute | solution.py:26
  21.4 3.6 %collective-permute-start = (bf16[144,1152]{1,0:T(8,128)(2,1)S(1)}, bf16[144,1152]{1,0:T(8,128)(2,1)S(1)}, u32[]{:S(2)}, u32[]{:S(2)}) collective-permute-start(bf16[144,1152]{1,0:T(8,128)(2,1)S(1)} %get-tuple-element.18.refs_2_), channel_id=1, source_target_pairs={{0,8},{4,12},{8,0},{12,4},{1,9},{5,13},{9,1},{13,5},{2,10},{6,14},... | collective-permute-start | bytes 995336 | tf_op jit(solution)/shard_map/ppermute | solution.py:26
  25.1 6.1 %all-to-all-start = ((bf16[4,144,1152]{2,1,0:T(8,128)(2,1)}), bf16[4,144,1152]{2,1,0:T(8,128)(2,1)S(1)}, u32[]{:S(2)}, u32[]{:S(2)}) async-start(bf16[4,144,1152]{2,1,0:T(8,128)(2,1)} %get-tuple-element.17), calls=%async_computation | async-start | bytes 2654208 | tf_op jit(solution)/shard_map/all_to_all | solution.py:217
  31.1 0.0 collective-permute-done.3.txt_ref
  31.1 0.2 shard_map.50.refs_6_
  31.3 2.9 %collective-permute-start.6 = (bf16[144,1152]{1,0:T(8,128)(2,1)S(1)}, bf16[144,1152]{1,0:T(8,128)(2,1)S(1)}, u32[]{:S(2)}, u32[]{:S(2)}) collective-permute-start(bf16[144,1152]{1,0:T(8,128)(2,1)S(1)} %shard_map.50.refs_6_), channel_id=1, source_target_pairs={{0,12},{4,0},{8,4},{12,8},{1,13},{5,1},{9,5},{13,9},{2,14},{6,2},{... | collective-permute-start | bytes 995336 | tf_op jit(solution)/shard_map/ppermute | solution.py:26
  34.2 2.5 %collective-permute-start.5 = (bf16[144,1152]{1,0:T(8,128)(2,1)S(1)}, bf16[144,1152]{1,0:T(8,128)(2,1)}, u32[]{:S(2)}, u32[]{:S(2)}) collective-permute-start(bf16[144,1152]{1,0:T(8,128)(2,1)S(1)} %shard_map.50.refs_6_), channel_id=1, source_target_pairs={{0,4},{4,8},{8,12},{12,0},{1,5},{5,9},{9,13},{13,1},{2,6},{6,10},{... | collective-permute-start | bytes 995336 | tf_op jit(solution)/shard_map/ppermute | solution.py:26
  36.7 0.0 collective-permute-done.2.refs_5_
  36.7 3.7 %collective-permute-start.4 = (bf16[144,1152]{1,0:T(8,128)(2,1)S(1)}, bf16[144,1152]{1,0:T(8,128)(2,1)}, u32[]{:S(2)}, u32[]{:S(2)}) collective-permute-start(bf16[144,1152]{1,0:T(8,128)(2,1)S(1)} %shard_map.50.refs_6_), channel_id=1, source_target_pairs={{0,8},{4,12},{8,0},{12,4},{1,9},{5,13},{9,1},{13,5},{2,10},{6,14},... | collective-permute-start | bytes 995336 | tf_op jit(solution)/shard_map/ppermute | solution.py:26
  40.4 0.0 collective-permute-done.1.refs_4_
  40.4 0.0 collective-permute-done.refs_3_
  40.4 0.8 collective-permute-done.6.refs_9_
  41.2 8.0 %collective-permute-done.5.refs_8_ = bf16[144,1152]{1,0:T(8,128)(2,1)} collective-permute-done((bf16[144,1152]{1,0:T(8,128)(2,1)S(1)}, bf16[144,1152]{1,0:T(8,128)(2,1)}, u32[]{:S(2)}, u32[]{:S(2)}) %collective-permute-start.5) | collective-permute-done | bytes 331808 | tf_op jit(solution)/shard_map/ppermute | solution.py:26
  49.2 0.0 collective-permute-done.4.refs_7_
  49.2 8.1 %all-to-all-done = bf16[4,144,1152]{2,1,0:T(8,128)(2,1)S(1)} async-done(((bf16[4,144,1152]{2,1,0:T(8,128)(2,1)}), bf16[4,144,1152]{2,1,0:T(8,128)(2,1)S(1)}, u32[]{:S(2)}, u32[]{:S(2)}) %all-to-all-start) | async-done | bytes 1327136 | tf_op jit(solution)/shard_map/all_to_all | solution.py:217
  57.2 8.8 %shard_map.51 = (bf16[576,1152]{1,0:T(8,128)(2,1)S(1)}, bf16[4,160,1152]{2,1,0:T(8,128)(2,1)}) custom-call(s32[1]{0:T(128)} %bitcast.refs_0_, bf16[576,1152]{1,0:T(8,128)(2,1)S(1)} %bitcast.3, bf16[144,1152]{1,0:T(8,128)(2,1)S(1)} %get-tuple-element.18.refs_2_, bf16[144,1152]{1,0:T(8,128)(2,1)S(1)} %collective-permute-done.refs_3_, ...), custom_call_target="tpu_custom_call" | custom-call | flops 3057647616 | bytes 6782980 | tf_op jit(solution)/shard_map/pallas_call | solution.py:31
  66.1 0.0 copy-start.4
  66.1 1.1 copy-done.4
  67.2 5.1 %all-to-all-start.1 = ((bf16[4,160,1152]{2,1,0:T(8,128)(2,1)}), bf16[4,160,1152]{2,1,0:T(8,128)(2,1)S(1)}, u32[]{:S(2)}, u32[]{:S(2)}) async-start(bf16[4,160,1152]{2,1,0:T(8,128)(2,1)} %get-tuple-element.19), calls=%async_computation.1 | async-start | bytes 2949120 | tf_op jit(solution)/shard_map/all_to_all | solution.py:224
  72.3 0.0 copy-start.5
  72.3 1.3 %copy-done.5 = bf16[576,1152]{1,0:T(8,128)(2,1)S(1)} copy-done((bf16[576,1152]{1,0:T(8,128)(2,1)S(1)}, bf16[576,1152]{1,0:T(8,128)(2,1)}, u32[]{:S(2)}) %copy-start.5) | copy-done | bytes 1327128
  73.6 0.0 copy-start.6
  73.6 1.4 %shard_map.54 = (bf16[144,1152]{1,0:T(8,128)(2,1)S(1)}, bf16[144,1152]{1,0:T(8,128)(2,1)S(1)}, bf16[144,1152]{1,0:T(8,128)(2,1)S(1)}, bf16[144,1152]{1,0:T(8,128)(2,1)S(1)}) custom-call(bf16[576,1152]{1,0:T(8,128)(2,1)S(1)} %copy-done.5, bf16[576,1152]{1,0:T(8,128)(2,1)S(1)} %bitcast.4), custom_call_target="tpu_custom_call" | custom-call | flops 764411904 | bytes 3981312 | tf_op jit(solution)/shard_map/pallas_call | solution.py:31
  75.1 4.7 %collective-permute-start.10 = (bf16[144,1152]{1,0:T(8,128)(2,1)S(1)}, bf16[144,1152]{1,0:T(8,128)(2,1)S(1)}, u32[]{:S(2)}, u32[]{:S(2)}) collective-permute-start(bf16[144,1152]{1,0:T(8,128)(2,1)S(1)} %get-tuple-element.28), channel_id=1, source_target_pairs={{0,8},{4,12},{8,0},{12,4},{1,9},{5,13},{9,1},{13,5},{2,10},{6,14},... | collective-permute-start | bytes 995336 | tf_op jit(solution)/shard_map/ppermute | solution.py:26
  79.7 2.8 %collective-permute-start.11 = (bf16[144,1152]{1,0:T(8,128)(2,1)S(1)}, bf16[144,1152]{1,0:T(8,128)(2,1)S(1)}, u32[]{:S(2)}, u32[]{:S(2)}) collective-permute-start(bf16[144,1152]{1,0:T(8,128)(2,1)S(1)} %get-tuple-element.29), channel_id=1, source_target_pairs={{0,12},{4,0},{8,4},{12,8},{1,13},{5,1},{9,5},{13,9},{2,14},{6,2},{... | collective-permute-start | bytes 995336 | tf_op jit(solution)/shard_map/ppermute | solution.py:26
  82.5 2.5 %collective-permute-start.12 = (bf16[144,1152]{1,0:T(8,128)(2,1)S(1)}, bf16[144,1152]{1,0:T(8,128)(2,1)S(1)}, u32[]{:S(2)}, u32[]{:S(2)}) collective-permute-start(bf16[144,1152]{1,0:T(8,128)(2,1)S(1)} %get-tuple-element.30), channel_id=1, source_target_pairs={{0,4},{4,8},{8,12},{12,0},{1,5},{5,9},{9,13},{13,1},{2,6},{6,10},{... | collective-permute-start | bytes 995336 | tf_op jit(solution)/shard_map/ppermute | solution.py:26
  85.1 0.0 copy-done.6
  85.1 1.4 %shard_map.53 = (bf16[144,1152]{1,0:T(8,128)(2,1)S(1)}, bf16[144,1152]{1,0:T(8,128)(2,1)S(1)}, bf16[144,1152]{1,0:T(8,128)(2,1)S(1)}, bf16[144,1152]{1,0:T(8,128)(2,1)S(1)}) custom-call(bf16[576,1152]{1,0:T(8,128)(2,1)S(1)} %copy-done.6, bf16[576,1152]{1,0:T(8,128)(2,1)S(1)} %bitcast.5), custom_call_target="tpu_custom_call" | custom-call | flops 764411904 | bytes 3981312 | tf_op jit(solution)/shard_map/pallas_call | solution.py:31
  86.5 0.0 copy-start.3
  86.5 2.7 %collective-permute-start.7 = (bf16[144,1152]{1,0:T(8,128)(2,1)S(1)}, bf16[144,1152]{1,0:T(8,128)(2,1)S(1)}, u32[]{:S(2)}, u32[]{:S(2)}) collective-permute-start(bf16[144,1152]{1,0:T(8,128)(2,1)S(1)} %get-tuple-element.24), channel_id=1, source_target_pairs={{0,8},{4,12},{8,0},{12,4},{1,9},{5,13},{9,1},{13,5},{2,10},{6,14},... | collective-permute-start | bytes 995336 | tf_op jit(solution)/shard_map/ppermute | solution.py:26
  89.2 4.0 %collective-permute-start.8 = (bf16[144,1152]{1,0:T(8,128)(2,1)S(1)}, bf16[144,1152]{1,0:T(8,128)(2,1)S(1)}, u32[]{:S(2)}, u32[]{:S(2)}) collective-permute-start(bf16[144,1152]{1,0:T(8,128)(2,1)S(1)} %get-tuple-element.25), channel_id=1, source_target_pairs={{0,12},{4,0},{8,4},{12,8},{1,13},{5,1},{9,5},{13,9},{2,14},{6,2},{... | collective-permute-start | bytes 995336 | tf_op jit(solution)/shard_map/ppermute | solution.py:26
  93.2 0.0 collective-permute-done.10.b
  93.2 1.9 %collective-permute-start.9 = (bf16[144,1152]{1,0:T(8,128)(2,1)S(1)}, bf16[144,1152]{1,0:T(8,128)(2,1)S(1)}, u32[]{:S(2)}, u32[]{:S(2)}) collective-permute-start(bf16[144,1152]{1,0:T(8,128)(2,1)S(1)} %get-tuple-element.26), channel_id=1, source_target_pairs={{0,4},{4,8},{8,12},{12,0},{1,5},{5,9},{9,13},{13,1},{2,6},{6,10},{... | collective-permute-start | bytes 995336 | tf_op jit(solution)/shard_map/ppermute | solution.py:26
  95.1 0.4 collective-permute-done.11.c
  95.5 6.5 %collective-permute-done.12.d = bf16[144,1152]{1,0:T(8,128)(2,1)S(1)} collective-permute-done((bf16[144,1152]{1,0:T(8,128)(2,1)S(1)}, bf16[144,1152]{1,0:T(8,128)(2,1)S(1)}, u32[]{:S(2)}, u32[]{:S(2)}) %collective-permute-start.12) | collective-permute-done | bytes 331808 | tf_op jit(solution)/shard_map/ppermute | solution.py:26
  102.0 0.2 shard_map.55
  102.2 1.9 %collective-permute-start.13 = (bf16[144,1152]{1,0:T(8,128)(2,1)S(1)}, bf16[144,1152]{1,0:T(8,128)(2,1)S(1)}, u32[]{:S(2)}, u32[]{:S(2)}) collective-permute-start(bf16[144,1152]{1,0:T(8,128)(2,1)S(1)} %shard_map.55), channel_id=1, source_target_pairs={{0,752},{16,0},{32,16},{48,32},{64,48},{80,64},{96,80},{112,96},{1... | collective-permute-start | bytes 995336 | tf_op jit(solution)/shard_map/ppermute | solution.py:26
  104.1 0.0 collective-permute-done.7.b
  104.1 5.7 %collective-permute-done.8.c = bf16[144,1152]{1,0:T(8,128)(2,1)S(1)} collective-permute-done((bf16[144,1152]{1,0:T(8,128)(2,1)S(1)}, bf16[144,1152]{1,0:T(8,128)(2,1)S(1)}, u32[]{:S(2)}, u32[]{:S(2)}) %collective-permute-start.8) | collective-permute-done | bytes 331808 | tf_op jit(solution)/shard_map/ppermute | solution.py:26
  109.8 0.0 collective-permute-done.9.d
  109.8 16.9 %collective-permute-done.13.home = bf16[144,1152]{1,0:T(8,128)(2,1)S(1)} collective-permute-done((bf16[144,1152]{1,0:T(8,128)(2,1)S(1)}, bf16[144,1152]{1,0:T(8,128)(2,1)S(1)}, u32[]{:S(2)}, u32[]{:S(2)}) %collective-permute-start.13) | collective-permute-done | bytes 331808 | tf_op jit(solution)/shard_map/ppermute | solution.py:26
  126.7 0.0 copy-done.3
  126.7 0.0 copy-start.1
  126.7 1.3 shard_map.56
  128.0 0.0 all-to-all-done.1.parts_ref
  128.0 0.0 copy-done.1
  128.0 1.2 shard_map.52
Async XLA Ops:
  0.6 30.5 %collective-permute-start.3 = (bf16[144,1152]{1,0:T(8,128)(2,1)}, bf16[144,1152]{1,0:T(8,128)(2,1)S(1)}, u32[]{:S(2)}, u32[]{:S(2)}) collective-permute-start(bf16[144,1152]{1,0:T(8,128)(2,1)} %raw_ref.3), channel_id=1, source_target_pairs={{0,16},{16,32},{32,48},{48,64},{64,80},{80,96},{96,112},{112,128},... | collective-permute-start | bytes 995336 | tf_op jit(solution)/shard_map/ppermute | solution.py:26
  11.8 1.0 copy-start
  12.8 1.0 copy-start.2
  15.1 21.6 %collective-permute-start.2 = (bf16[144,1152]{1,0:T(8,128)(2,1)S(1)}, bf16[144,1152]{1,0:T(8,128)(2,1)S(1)}, u32[]{:S(2)}, u32[]{:S(2)}) collective-permute-start(bf16[144,1152]{1,0:T(8,128)(2,1)S(1)} %get-tuple-element.18.refs_2_), channel_id=1, source_target_pairs={{0,12},{4,0},{8,4},{12,8},{1,13},{5,1},{9,5},{13,9},{2,14},{6,2},{... | collective-permute-start | bytes 995336 | tf_op jit(solution)/shard_map/ppermute | solution.py:26
  19.5 20.9 %collective-permute-start.1 = (bf16[144,1152]{1,0:T(8,128)(2,1)S(1)}, bf16[144,1152]{1,0:T(8,128)(2,1)S(1)}, u32[]{:S(2)}, u32[]{:S(2)}) collective-permute-start(bf16[144,1152]{1,0:T(8,128)(2,1)S(1)} %get-tuple-element.18.refs_2_), channel_id=1, source_target_pairs={{0,4},{4,8},{8,12},{12,0},{1,5},{5,9},{9,13},{13,1},{2,6},{6,10},{... | collective-permute-start | bytes 995336 | tf_op jit(solution)/shard_map/ppermute | solution.py:26
  21.4 19.0 %collective-permute-start = (bf16[144,1152]{1,0:T(8,128)(2,1)S(1)}, bf16[144,1152]{1,0:T(8,128)(2,1)S(1)}, u32[]{:S(2)}, u32[]{:S(2)}) collective-permute-start(bf16[144,1152]{1,0:T(8,128)(2,1)S(1)} %get-tuple-element.18.refs_2_), channel_id=1, source_target_pairs={{0,8},{4,12},{8,0},{12,4},{1,9},{5,13},{9,1},{13,5},{2,10},{6,14},... | collective-permute-start | bytes 995336 | tf_op jit(solution)/shard_map/ppermute | solution.py:26
  25.1 32.2 %all-to-all-start = ((bf16[4,144,1152]{2,1,0:T(8,128)(2,1)}), bf16[4,144,1152]{2,1,0:T(8,128)(2,1)S(1)}, u32[]{:S(2)}, u32[]{:S(2)}) async-start(bf16[4,144,1152]{2,1,0:T(8,128)(2,1)} %get-tuple-element.17), calls=%async_computation | async-start | bytes 2654208 | tf_op jit(solution)/shard_map/all_to_all | solution.py:217
  31.3 9.9 %collective-permute-start.6 = (bf16[144,1152]{1,0:T(8,128)(2,1)S(1)}, bf16[144,1152]{1,0:T(8,128)(2,1)S(1)}, u32[]{:S(2)}, u32[]{:S(2)}) collective-permute-start(bf16[144,1152]{1,0:T(8,128)(2,1)S(1)} %shard_map.50.refs_6_), channel_id=1, source_target_pairs={{0,12},{4,0},{8,4},{12,8},{1,13},{5,1},{9,5},{13,9},{2,14},{6,2},{... | collective-permute-start | bytes 995336 | tf_op jit(solution)/shard_map/ppermute | solution.py:26
  34.2 15.0 %collective-permute-start.5 = (bf16[144,1152]{1,0:T(8,128)(2,1)S(1)}, bf16[144,1152]{1,0:T(8,128)(2,1)}, u32[]{:S(2)}, u32[]{:S(2)}) collective-permute-start(bf16[144,1152]{1,0:T(8,128)(2,1)S(1)} %shard_map.50.refs_6_), channel_id=1, source_target_pairs={{0,4},{4,8},{8,12},{12,0},{1,5},{5,9},{9,13},{13,1},{2,6},{6,10},{... | collective-permute-start | bytes 995336 | tf_op jit(solution)/shard_map/ppermute | solution.py:26
  36.7 12.5 %collective-permute-start.4 = (bf16[144,1152]{1,0:T(8,128)(2,1)S(1)}, bf16[144,1152]{1,0:T(8,128)(2,1)}, u32[]{:S(2)}, u32[]{:S(2)}) collective-permute-start(bf16[144,1152]{1,0:T(8,128)(2,1)S(1)} %shard_map.50.refs_6_), channel_id=1, source_target_pairs={{0,8},{4,12},{8,0},{12,4},{1,9},{5,13},{9,1},{13,5},{2,10},{6,14},... | collective-permute-start | bytes 995336 | tf_op jit(solution)/shard_map/ppermute | solution.py:26
  66.1 1.1 copy-start.4
  67.2 60.8 %all-to-all-start.1 = ((bf16[4,160,1152]{2,1,0:T(8,128)(2,1)}), bf16[4,160,1152]{2,1,0:T(8,128)(2,1)S(1)}, u32[]{:S(2)}, u32[]{:S(2)}) async-start(bf16[4,160,1152]{2,1,0:T(8,128)(2,1)} %get-tuple-element.19), calls=%async_computation.1 | async-start | bytes 2949120 | tf_op jit(solution)/shard_map/all_to_all | solution.py:224
  72.3 1.3 %copy-start.5 = (bf16[576,1152]{1,0:T(8,128)(2,1)S(1)}, bf16[576,1152]{1,0:T(8,128)(2,1)}, u32[]{:S(2)}) copy-start(bf16[576,1152]{1,0:T(8,128)(2,1)} %copy-done.4) | copy-start | bytes 3981316
  73.6 11.4 %copy-start.6 = (bf16[576,1152]{1,0:T(8,128)(2,1)S(1)}, bf16[576,1152]{1,0:T(8,128)(2,1)}, u32[]{:S(2)}) copy-start(bf16[576,1152]{1,0:T(8,128)(2,1)} %copy-done.4) | copy-start | bytes 3981316
  75.1 18.1 %collective-permute-start.10 = (bf16[144,1152]{1,0:T(8,128)(2,1)S(1)}, bf16[144,1152]{1,0:T(8,128)(2,1)S(1)}, u32[]{:S(2)}, u32[]{:S(2)}) collective-permute-start(bf16[144,1152]{1,0:T(8,128)(2,1)S(1)} %get-tuple-element.28), channel_id=1, source_target_pairs={{0,8},{4,12},{8,0},{12,4},{1,9},{5,13},{9,1},{13,5},{2,10},{6,14},... | collective-permute-start | bytes 995336 | tf_op jit(solution)/shard_map/ppermute | solution.py:26
  79.7 15.8 %collective-permute-start.11 = (bf16[144,1152]{1,0:T(8,128)(2,1)S(1)}, bf16[144,1152]{1,0:T(8,128)(2,1)S(1)}, u32[]{:S(2)}, u32[]{:S(2)}) collective-permute-start(bf16[144,1152]{1,0:T(8,128)(2,1)S(1)} %get-tuple-element.29), channel_id=1, source_target_pairs={{0,12},{4,0},{8,4},{12,8},{1,13},{5,1},{9,5},{13,9},{2,14},{6,2},{... | collective-permute-start | bytes 995336 | tf_op jit(solution)/shard_map/ppermute | solution.py:26
  82.5 19.5 %collective-permute-start.12 = (bf16[144,1152]{1,0:T(8,128)(2,1)S(1)}, bf16[144,1152]{1,0:T(8,128)(2,1)S(1)}, u32[]{:S(2)}, u32[]{:S(2)}) collective-permute-start(bf16[144,1152]{1,0:T(8,128)(2,1)S(1)} %get-tuple-element.30), channel_id=1, source_target_pairs={{0,4},{4,8},{8,12},{12,0},{1,5},{5,9},{9,13},{13,1},{2,6},{6,10},{... | collective-permute-start | bytes 995336 | tf_op jit(solution)/shard_map/ppermute | solution.py:26
  86.5 40.2 %copy-start.3 = (bf16[144,1152]{1,0:T(8,128)(2,1)S(1)}, bf16[144,1152]{1,0:T(8,128)(2,1)}, u32[]{:S(2)}) copy-start(bf16[144,1152]{1,0:T(8,128)(2,1)} %raw_ref.3) | copy-start | bytes 995332
  86.5 17.6 %collective-permute-start.7 = (bf16[144,1152]{1,0:T(8,128)(2,1)S(1)}, bf16[144,1152]{1,0:T(8,128)(2,1)S(1)}, u32[]{:S(2)}, u32[]{:S(2)}) collective-permute-start(bf16[144,1152]{1,0:T(8,128)(2,1)S(1)} %get-tuple-element.24), channel_id=1, source_target_pairs={{0,8},{4,12},{8,0},{12,4},{1,9},{5,13},{9,1},{13,5},{2,10},{6,14},... | collective-permute-start | bytes 995336 | tf_op jit(solution)/shard_map/ppermute | solution.py:26
  89.2 20.6 %collective-permute-start.8 = (bf16[144,1152]{1,0:T(8,128)(2,1)S(1)}, bf16[144,1152]{1,0:T(8,128)(2,1)S(1)}, u32[]{:S(2)}, u32[]{:S(2)}) collective-permute-start(bf16[144,1152]{1,0:T(8,128)(2,1)S(1)} %get-tuple-element.25), channel_id=1, source_target_pairs={{0,12},{4,0},{8,4},{12,8},{1,13},{5,1},{9,5},{13,9},{2,14},{6,2},{... | collective-permute-start | bytes 995336 | tf_op jit(solution)/shard_map/ppermute | solution.py:26
  93.2 16.6 %collective-permute-start.9 = (bf16[144,1152]{1,0:T(8,128)(2,1)S(1)}, bf16[144,1152]{1,0:T(8,128)(2,1)S(1)}, u32[]{:S(2)}, u32[]{:S(2)}) collective-permute-start(bf16[144,1152]{1,0:T(8,128)(2,1)S(1)} %get-tuple-element.26), channel_id=1, source_target_pairs={{0,4},{4,8},{8,12},{12,0},{1,5},{5,9},{9,13},{13,1},{2,6},{6,10},{... | collective-permute-start | bytes 995336 | tf_op jit(solution)/shard_map/ppermute | solution.py:26
  102.2 24.6 %collective-permute-start.13 = (bf16[144,1152]{1,0:T(8,128)(2,1)S(1)}, bf16[144,1152]{1,0:T(8,128)(2,1)S(1)}, u32[]{:S(2)}, u32[]{:S(2)}) collective-permute-start(bf16[144,1152]{1,0:T(8,128)(2,1)S(1)} %shard_map.55), channel_id=1, source_target_pairs={{0,752},{16,0},{32,16},{48,32},{64,48},{80,64},{96,80},{112,96},{1... | collective-permute-start | bytes 995336 | tf_op jit(solution)/shard_map/ppermute | solution.py:26
  126.7 1.3 %copy-start.1 = (bf16[144,1152]{1,0:T(8,128)(2,1)S(1)}, bf16[144,1152]{1,0:T(8,128)(2,1)}, u32[]{:S(2)}) copy-start(bf16[144,1152]{1,0:T(8,128)(2,1)} %raw_ref.2) | copy-start | bytes 995332

commit v4 on v3

--- a/solution.py
+++ b/solution.py
@@ -18,7 +18,8 @@
 LOSS_ROWS = 16
 CHUNK = 16
 LANES = 128
-WEIGHT = 60_000_000_000
+WEIGHT = 26_000_000_000
+HOME_WEIGHT = 4_000_000_000
 
 
 def shifted(value, axis, steps):
@@ -186,11 +187,14 @@
     loss_ref[...] = jnp.sum(tail, axis=0, keepdims=True)
 
 
-def text_end_kernel(raw_ref, a, b, c, d, home, grad_ref):
-    grads = a[...].astype(F32) + b[...].astype(F32)
+def text_end_kernel(raw_ref, base, b, c, d, grad_ref):
+    grads = base[...] + b[...].astype(F32)
     grads = grads + c[...].astype(F32) + d[...].astype(F32)
-    grads = grads + home[...].astype(F32)
     grad_ref[...] = project(raw_ref[...], grads)
+
+
+def base_kernel(a, home, out_ref):
+    out_ref[...] = a[...].astype(F32) + home[...].astype(F32)
 
 
 def later_kernel(a, b, c, d, out_ref):
@@ -231,7 +235,8 @@
     image_grad, row_loss = vmem_call(
         image_end_kernel, [images, img_back], [wide, shape((1, own), F32)], 12
     )
-    (text_grad,) = vmem_call(text_end_kernel, [texts] + now_back + [home], [wide], 12)
+    (base,) = vmem_call(base_kernel, [now_back[0], home], [wide], 8, flops=HOME_WEIGHT)
+    (text_grad,) = vmem_call(text_end_kernel, [texts, base] + now_back[1:], [wide], 12)
     return (row_loss.reshape(own), image_grad, text_grad)
 
 

time: 130 us -> 128 us (0.985)
  the two profiles are of different devices: /device:TPU:113 before, /device:TPU:65 now
where the time goes in v4:
time: 128 us; the launch traced here: 127 us
  starting transfers between devices  61 us (48%)
  waiting for transfers between devices  44.2 us (35%)
  Pallas kernels  15.9 us (12%)
  local copies, waits for them, and re-layouts  5.2 us (4%)
    ppermute x14, starting transfers between devices, shifted(): lax.ppermute(value, axis, [(i, (i + steps) % count) for i in range(count)])  50.2 us
    ppermute x14, waiting for transfers between devices, shifted(): lax.ppermute(value, axis, [(i, (i + steps) % count) for i in range(count)])  44.2 us
    pallas_call x9, Pallas kernels, vmem_call(): pl.pallas_call(body, out_shape=list(outs), in_specs=[pl.BlockSpec(memory_...  15.9 us
    all_to_all x1, starting transfers between devices, on_device(): img_all = lax.all_to_all(spread, 'z', 0, 0).reshape(NZ * own, features)  6.06 us
    unnamed x12, local copies, waits for them, and re-layouts  5.2 us
    all_to_all x1, starting transfers between devices, on_device(): img_back = lax.all_to_all(img_parts, 'z', 0, 0)  4.69 us
  transfers between devices with their start and end apart: 16, of which 8 were waited for; matrix products, arithmetic and copies ran while one was open for 0% of the time, Pallas kernels for 5%

profile of v4, /device:TPU:65, one launch (start us, length us, event | category | flops | bytes accessed | tf_op | source)
XLA Modules:
  0.0 127.1 jit_solution(2619316038992930555)
XLA Ops:
  0.6 11.2 %collective-permute-start.3 = (bf16[144,1152]{1,0:T(8,128)(2,1)}, bf16[144,1152]{1,0:T(8,128)(2,1)S(1)}, u32[]{:S(2)}, u32[]{:S(2)}) collective-permute-start(bf16[144,1152]{1,0:T(8,128)(2,1)} %raw_ref.3), channel_id=1, source_target_pairs={{0,16},{16,32},{32,48},{48,64},{64,80},{80,96},{96,112},{112,128},... | collective-permute-start | bytes 995336 | tf_op jit(solution)/shard_map/ppermute | solution.py:27
  11.8 0.0 copy-start
  11.8 1.0 copy-done
  12.8 0.0 copy-start.2
  12.8 1.0 copy-done.2
  13.8 1.3 %shard_map.49 = (bf16[4,144,1152]{2,1,0:T(8,128)(2,1)}, bf16[144,1152]{1,0:T(8,128)(2,1)S(1)}) custom-call(bf16[144,1152]{1,0:T(8,128)(2,1)S(1)} %copy-done, bf16[144,1152]{1,0:T(8,128)(2,1)S(1)} %copy-done.2), custom_call_target="tpu_custom_call" | custom-call | bytes 2322432 | tf_op jit(solution)/shard_map/pallas_call | solution.py:32
  15.1 6.1 %all-to-all-start = ((bf16[4,144,1152]{2,1,0:T(8,128)(2,1)}), bf16[4,144,1152]{2,1,0:T(8,128)(2,1)S(1)}, u32[]{:S(2)}, u32[]{:S(2)}) async-start(bf16[4,144,1152]{2,1,0:T(8,128)(2,1)} %get-tuple-element.17), calls=%async_computation | async-start | bytes 2654208 | tf_op jit(solution)/shard_map/all_to_all | solution.py:221
  21.2 4.4 %collective-permute-start.2 = (bf16[144,1152]{1,0:T(8,128)(2,1)S(1)}, bf16[144,1152]{1,0:T(8,128)(2,1)S(1)}, u32[]{:S(2)}, u32[]{:S(2)}) collective-permute-start(bf16[144,1152]{1,0:T(8,128)(2,1)S(1)} %get-tuple-element.18.refs_2_), channel_id=1, source_target_pairs={{0,12},{4,0},{8,4},{12,8},{1,13},{5,1},{9,5},{13,9},{2,14},{6,2},{... | collective-permute-start | bytes 995336 | tf_op jit(solution)/shard_map/ppermute | solution.py:27
  25.6 1.9 %collective-permute-start.1 = (bf16[144,1152]{1,0:T(8,128)(2,1)S(1)}, bf16[144,1152]{1,0:T(8,128)(2,1)S(1)}, u32[]{:S(2)}, u32[]{:S(2)}) collective-permute-start(bf16[144,1152]{1,0:T(8,128)(2,1)S(1)} %get-tuple-element.18.refs_2_), channel_id=1, source_target_pairs={{0,4},{4,8},{8,12},{12,0},{1,5},{5,9},{9,13},{13,1},{2,6},{6,10},{... | collective-permute-start | bytes 995336 | tf_op jit(solution)/shard_map/ppermute | solution.py:27
  27.5 3.6 %collective-permute-start = (bf16[144,1152]{1,0:T(8,128)(2,1)S(1)}, bf16[144,1152]{1,0:T(8,128)(2,1)S(1)}, u32[]{:S(2)}, u32[]{:S(2)}) collective-permute-start(bf16[144,1152]{1,0:T(8,128)(2,1)S(1)} %get-tuple-element.18.refs_2_), channel_id=1, source_target_pairs={{0,8},{4,12},{8,0},{12,4},{1,9},{5,13},{9,1},{13,5},{2,10},{6,14},... | collective-permute-start | bytes 995336 | tf_op jit(solution)/shard_map/ppermute | solution.py:27
  31.1 0.0 collective-permute-done.3.txt_ref
  31.1 0.2 shard_map.50.refs_6_
  31.3 2.9 %collective-permute-start.6 = (bf16[144,1152]{1,0:T(8,128)(2,1)S(1)}, bf16[144,1152]{1,0:T(8,128)(2,1)S(1)}, u32[]{:S(2)}, u32[]{:S(2)}) collective-permute-start(bf16[144,1152]{1,0:T(8,128)(2,1)S(1)} %shard_map.50.refs_6_), channel_id=1, source_target_pairs={{0,12},{4,0},{8,4},{12,8},{1,13},{5,1},{9,5},{13,9},{2,14},{6,2},{... | collective-permute-start | bytes 995336 | tf_op jit(solution)/shard_map/ppermute | solution.py:27
  34.2 2.5 %collective-permute-start.5 = (bf16[144,1152]{1,0:T(8,128)(2,1)S(1)}, bf16[144,1152]{1,0:T(8,128)(2,1)}, u32[]{:S(2)}, u32[]{:S(2)}) collective-permute-start(bf16[144,1152]{1,0:T(8,128)(2,1)S(1)} %shard_map.50.refs_6_), channel_id=1, source_target_pairs={{0,4},{4,8},{8,12},{12,0},{1,5},{5,9},{9,13},{13,1},{2,6},{6,10},{... | collective-permute-start | bytes 995336 | tf_op jit(solution)/shard_map/ppermute | solution.py:27
  36.7 0.0 collective-permute-done.2.refs_5_
  36.7 3.7 %collective-permute-start.4 = (bf16[144,1152]{1,0:T(8,128)(2,1)S(1)}, bf16[144,1152]{1,0:T(8,128)(2,1)}, u32[]{:S(2)}, u32[]{:S(2)}) collective-permute-start(bf16[144,1152]{1,0:T(8,128)(2,1)S(1)} %shard_map.50.refs_6_), channel_id=1, source_target_pairs={{0,8},{4,12},{8,0},{12,4},{1,9},{5,13},{9,1},{13,5},{2,10},{6,14},... | collective-permute-start | bytes 995336 | tf_op jit(solution)/shard_map/ppermute | solution.py:27
  40.4 0.6 collective-permute-done.1.refs_4_
  41.0 2.7 %collective-permute-done.refs_3_ = bf16[144,1152]{1,0:T(8,128)(2,1)S(1)} collective-permute-done((bf16[144,1152]{1,0:T(8,128)(2,1)S(1)}, bf16[144,1152]{1,0:T(8,128)(2,1)S(1)}, u32[]{:S(2)}, u32[]{:S(2)}) %collective-permute-start) | collective-permute-done | bytes 331808 | tf_op jit(solution)/shard_map/ppermute | solution.py:27
  43.8 4.5 %collective-permute-done.6.refs_9_ = bf16[144,1152]{1,0:T(8,128)(2,1)S(1)} collective-permute-done((bf16[144,1152]{1,0:T(8,128)(2,1)S(1)}, bf16[144,1152]{1,0:T(8,128)(2,1)S(1)}, u32[]{:S(2)}, u32[]{:S(2)}) %collective-permute-start.6) | collective-permute-done | bytes 331808 | tf_op jit(solution)/shard_map/ppermute | solution.py:27
  48.3 7.6 %collective-permute-done.5.refs_8_ = bf16[144,1152]{1,0:T(8,128)(2,1)} collective-permute-done((bf16[144,1152]{1,0:T(8,128)(2,1)S(1)}, bf16[144,1152]{1,0:T(8,128)(2,1)}, u32[]{:S(2)}, u32[]{:S(2)}) %collective-permute-start.5) | collective-permute-done | bytes 331808 | tf_op jit(solution)/shard_map/ppermute | solution.py:27
  55.9 0.0 collective-permute-done.4.refs_7_
  55.9 0.0 all-to-all-done
  55.9 8.8 %shard_map.51 = (bf16[576,1152]{1,0:T(8,128)(2,1)S(1)}, bf16[4,160,1152]{2,1,0:T(8,128)(2,1)}) custom-call(s32[1]{0:T(128)} %bitcast.refs_0_, bf16[576,1152]{1,0:T(8,128)(2,1)S(1)} %bitcast.3, bf16[144,1152]{1,0:T(8,128)(2,1)S(1)} %get-tuple-element.18.refs_2_, bf16[144,1152]{1,0:T(8,128)(2,1)S(1)} %collective-permute-done.refs_3_, ...), custom_call_target="tpu_custom_call" | custom-call | flops 3057647616 | bytes 6782980 | tf_op jit(solution)/shard_map/pallas_call | solution.py:32
  64.8 0.0 copy-start.4
  64.8 1.1 copy-done.4
  65.8 4.7 %all-to-all-start.1 = ((bf16[4,160,1152]{2,1,0:T(8,128)(2,1)}), bf16[4,160,1152]{2,1,0:T(8,128)(2,1)S(1)}, u32[]{:S(2)}, u32[]{:S(2)}) async-start(bf16[4,160,1152]{2,1,0:T(8,128)(2,1)} %get-tuple-element.19), calls=%async_computation.1 | async-start | bytes 2949120 | tf_op jit(solution)/shard_map/all_to_all | solution.py:228
  70.5 0.0 copy-start.5
  70.5 1.3 %copy-done.5 = bf16[576,1152]{1,0:T(8,128)(2,1)S(1)} copy-done((bf16[576,1152]{1,0:T(8,128)(2,1)S(1)}, bf16[576,1152]{1,0:T(8,128)(2,1)}, u32[]{:S(2)}) %copy-start.5) | copy-done | bytes 1327128
  71.8 1.4 %shard_map.54 = (bf16[144,1152]{1,0:T(8,128)(2,1)S(1)}, bf16[144,1152]{1,0:T(8,128)(2,1)S(1)}, bf16[144,1152]{1,0:T(8,128)(2,1)S(1)}, bf16[144,1152]{1,0:T(8,128)(2,1)S(1)}) custom-call(bf16[576,1152]{1,0:T(8,128)(2,1)S(1)} %copy-done.5, bf16[576,1152]{1,0:T(8,128)(2,1)S(1)} %bitcast.4), custom_call_target="tpu_custom_call" | custom-call | flops 764411904 | bytes 3981312 | tf_op jit(solution)/shard_map/pallas_call | solution.py:32
  73.3 3.6 %collective-permute-start.7 = (bf16[144,1152]{1,0:T(8,128)(2,1)S(1)}, bf16[144,1152]{1,0:T(8,128)(2,1)S(1)}, u32[]{:S(2)}, u32[]{:S(2)}) collective-permute-start(bf16[144,1152]{1,0:T(8,128)(2,1)S(1)} %get-tuple-element.25), channel_id=1, source_target_pairs={{0,8},{4,12},{8,0},{12,4},{1,9},{5,13},{9,1},{13,5},{2,10},{6,14},... | collective-permute-start | bytes 995336 | tf_op jit(solution)/shard_map/ppermute | solution.py:27
  76.9 2.8 %collective-permute-start.8 = (bf16[144,1152]{1,0:T(8,128)(2,1)S(1)}, bf16[144,1152]{1,0:T(8,128)(2,1)S(1)}, u32[]{:S(2)}, u32[]{:S(2)}) collective-permute-start(bf16[144,1152]{1,0:T(8,128)(2,1)S(1)} %get-tuple-element.26), channel_id=1, source_target_pairs={{0,12},{4,0},{8,4},{12,8},{1,13},{5,1},{9,5},{13,9},{2,14},{6,2},{... | collective-permute-start | bytes 995336 | tf_op jit(solution)/shard_map/ppermute | solution.py:27
  79.7 2.5 %collective-permute-start.9 = (bf16[144,1152]{1,0:T(8,128)(2,1)S(1)}, bf16[144,1152]{1,0:T(8,128)(2,1)S(1)}, u32[]{:S(2)}, u32[]{:S(2)}) collective-permute-start(bf16[144,1152]{1,0:T(8,128)(2,1)S(1)} %get-tuple-element.27), channel_id=1, source_target_pairs={{0,4},{4,8},{8,12},{12,0},{1,5},{5,9},{9,13},{13,1},{2,6},{6,10},{... | collective-permute-start | bytes 995336 | tf_op jit(solution)/shard_map/ppermute | solution.py:27
  82.2 2.7 %collective-permute-done.7.b = bf16[144,1152]{1,0:T(8,128)(2,1)S(1)} collective-permute-done((bf16[144,1152]{1,0:T(8,128)(2,1)S(1)}, bf16[144,1152]{1,0:T(8,128)(2,1)S(1)}, u32[]{:S(2)}, u32[]{:S(2)}) %collective-permute-start.7) | collective-permute-done | bytes 331808 | tf_op jit(solution)/shard_map/ppermute | solution.py:27
  84.9 7.1 %collective-permute-done.8.c = bf16[144,1152]{1,0:T(8,128)(2,1)S(1)} collective-permute-done((bf16[144,1152]{1,0:T(8,128)(2,1)S(1)}, bf16[144,1152]{1,0:T(8,128)(2,1)S(1)}, u32[]{:S(2)}, u32[]{:S(2)}) %collective-permute-start.8) | collective-permute-done | bytes 331808 | tf_op jit(solution)/shard_map/ppermute | solution.py:27
  92.0 1.6 %collective-permute-done.9.d = bf16[144,1152]{1,0:T(8,128)(2,1)S(1)} collective-permute-done((bf16[144,1152]{1,0:T(8,128)(2,1)S(1)}, bf16[144,1152]{1,0:T(8,128)(2,1)S(1)}, u32[]{:S(2)}, u32[]{:S(2)}) %collective-permute-start.9) | collective-permute-done | bytes 331808 | tf_op jit(solution)/shard_map/ppermute | solution.py:27
  93.6 0.2 shard_map.55
  93.8 2.6 %collective-permute-start.10 = (bf16[144,1152]{1,0:T(8,128)(2,1)S(1)}, bf16[144,1152]{1,0:T(8,128)(2,1)S(1)}, u32[]{:S(2)}, u32[]{:S(2)}) collective-permute-start(bf16[144,1152]{1,0:T(8,128)(2,1)S(1)} %shard_map.55), channel_id=1, source_target_pairs={{0,752},{16,0},{32,16},{48,32},{64,48},{80,64},{96,80},{112,96},{1... | collective-permute-start | bytes 995336 | tf_op jit(solution)/shard_map/ppermute | solution.py:27
  96.4 1.4 %shard_map.53 = (bf16[144,1152]{1,0:T(8,128)(2,1)S(1)}, bf16[144,1152]{1,0:T(8,128)(2,1)S(1)}, bf16[144,1152]{1,0:T(8,128)(2,1)S(1)}, bf16[144,1152]{1,0:T(8,128)(2,1)S(1)}) custom-call(bf16[576,1152]{1,0:T(8,128)(2,1)S(1)} %copy-done.5, bf16[576,1152]{1,0:T(8,128)(2,1)S(1)} %bitcast.5), custom_call_target="tpu_custom_call" | custom-call | flops 764411904 | bytes 3981312 | tf_op jit(solution)/shard_map/pallas_call | solution.py:32
  97.8 3.3 %collective-permute-start.11 = (bf16[144,1152]{1,0:T(8,128)(2,1)S(1)}, bf16[144,1152]{1,0:T(8,128)(2,1)S(1)}, u32[]{:S(2)}, u32[]{:S(2)}) collective-permute-start(bf16[144,1152]{1,0:T(8,128)(2,1)S(1)} %get-tuple-element.28), channel_id=1, source_target_pairs={{0,8},{4,12},{8,0},{12,4},{1,9},{5,13},{9,1},{13,5},{2,10},{6,14},... | collective-permute-start | bytes 995336 | tf_op jit(solution)/shard_map/ppermute | solution.py:27
  101.1 2.8 %collective-permute-start.12 = (bf16[144,1152]{1,0:T(8,128)(2,1)S(1)}, bf16[144,1152]{1,0:T(8,128)(2,1)S(1)}, u32[]{:S(2)}, u32[]{:S(2)}) collective-permute-start(bf16[144,1152]{1,0:T(8,128)(2,1)S(1)} %get-tuple-element.29), channel_id=1, source_target_pairs={{0,12},{4,0},{8,4},{12,8},{1,13},{5,1},{9,5},{13,9},{2,14},{6,2},{... | collective-permute-start | bytes 995336 | tf_op jit(solution)/shard_map/ppermute | solution.py:27
  103.9 2.5 %collective-permute-start.13 = (bf16[144,1152]{1,0:T(8,128)(2,1)S(1)}, bf16[144,1152]{1,0:T(8,128)(2,1)S(1)}, u32[]{:S(2)}, u32[]{:S(2)}) collective-permute-start(bf16[144,1152]{1,0:T(8,128)(2,1)S(1)} %get-tuple-element.30), channel_id=1, source_target_pairs={{0,4},{4,8},{8,12},{12,0},{1,5},{5,9},{9,13},{13,1},{2,6},{6,10},{... | collective-permute-start | bytes 995336 | tf_op jit(solution)/shard_map/ppermute | solution.py:27
  106.4 17.2 %collective-permute-done.10.home = bf16[144,1152]{1,0:T(8,128)(2,1)S(1)} collective-permute-done((bf16[144,1152]{1,0:T(8,128)(2,1)S(1)}, bf16[144,1152]{1,0:T(8,128)(2,1)S(1)}, u32[]{:S(2)}, u32[]{:S(2)}) %collective-permute-start.10) | collective-permute-done | bytes 331808 | tf_op jit(solution)/shard_map/ppermute | solution.py:27
  123.7 0.0 copy-start.3
  123.7 0.1 shard_map.56.base
  123.8 0.0 copy-start.1
  123.8 0.0 collective-permute-done.11.b
  123.8 0.0 collective-permute-done.12.c
  123.8 0.0 collective-permute-done.13.d
  123.8 0.8 copy-done.3
  124.7 1.2 shard_map.57
  125.9 0.0 all-to-all-done.1.parts_ref
  125.9 0.0 copy-done.1
  125.9 1.2 shard_map.52
Async XLA Ops:
  0.6 30.5 %collective-permute-start.3 = (bf16[144,1152]{1,0:T(8,128)(2,1)}, bf16[144,1152]{1,0:T(8,128)(2,1)S(1)}, u32[]{:S(2)}, u32[]{:S(2)}) collective-permute-start(bf16[144,1152]{1,0:T(8,128)(2,1)} %raw_ref.3), channel_id=1, source_target_pairs={{0,16},{16,32},{32,48},{48,64},{64,80},{80,96},{96,112},{112,128},... | collective-permute-start | bytes 995336 | tf_op jit(solution)/shard_map/ppermute | solution.py:27
  11.8 1.0 copy-start
  12.8 1.0 copy-start.2
  15.1 40.8 %all-to-all-start = ((bf16[4,144,1152]{2,1,0:T(8,128)(2,1)}), bf16[4,144,1152]{2,1,0:T(8,128)(2,1)S(1)}, u32[]{:S(2)}, u32[]{:S(2)}) async-start(bf16[4,144,1152]{2,1,0:T(8,128)(2,1)} %get-tuple-element.17), calls=%async_computation | async-start | bytes 2654208 | tf_op jit(solution)/shard_map/all_to_all | solution.py:221
  21.2 15.5 %collective-permute-start.2 = (bf16[144,1152]{1,0:T(8,128)(2,1)S(1)}, bf16[144,1152]{1,0:T(8,128)(2,1)S(1)}, u32[]{:S(2)}, u32[]{:S(2)}) collective-permute-start(bf16[144,1152]{1,0:T(8,128)(2,1)S(1)} %get-tuple-element.18.refs_2_), channel_id=1, source_target_pairs={{0,12},{4,0},{8,4},{12,8},{1,13},{5,1},{9,5},{13,9},{2,14},{6,2},{... | collective-permute-start | bytes 995336 | tf_op jit(solution)/shard_map/ppermute | solution.py:27
  25.6 15.5 %collective-permute-start.1 = (bf16[144,1152]{1,0:T(8,128)(2,1)S(1)}, bf16[144,1152]{1,0:T(8,128)(2,1)S(1)}, u32[]{:S(2)}, u32[]{:S(2)}) collective-permute-start(bf16[144,1152]{1,0:T(8,128)(2,1)S(1)} %get-tuple-element.18.refs_2_), channel_id=1, source_target_pairs={{0,4},{4,8},{8,12},{12,0},{1,5},{5,9},{9,13},{13,1},{2,6},{6,10},{... | collective-permute-start | bytes 995336 | tf_op jit(solution)/shard_map/ppermute | solution.py:27
  27.5 16.3 %collective-permute-start = (bf16[144,1152]{1,0:T(8,128)(2,1)S(1)}, bf16[144,1152]{1,0:T(8,128)(2,1)S(1)}, u32[]{:S(2)}, u32[]{:S(2)}) collective-permute-start(bf16[144,1152]{1,0:T(8,128)(2,1)S(1)} %get-tuple-element.18.refs_2_), channel_id=1, source_target_pairs={{0,8},{4,12},{8,0},{12,4},{1,9},{5,13},{9,1},{13,5},{2,10},{6,14},... | collective-permute-start | bytes 995336 | tf_op jit(solution)/shard_map/ppermute | solution.py:27
  31.3 17.0 %collective-permute-start.6 = (bf16[144,1152]{1,0:T(8,128)(2,1)S(1)}, bf16[144,1152]{1,0:T(8,128)(2,1)S(1)}, u32[]{:S(2)}, u32[]{:S(2)}) collective-permute-start(bf16[144,1152]{1,0:T(8,128)(2,1)S(1)} %shard_map.50.refs_6_), channel_id=1, source_target_pairs={{0,12},{4,0},{8,4},{12,8},{1,13},{5,1},{9,5},{13,9},{2,14},{6,2},{... | collective-permute-start | bytes 995336 | tf_op jit(solution)/shard_map/ppermute | solution.py:27
  34.2 21.7 %collective-permute-start.5 = (bf16[144,1152]{1,0:T(8,128)(2,1)S(1)}, bf16[144,1152]{1,0:T(8,128)(2,1)}, u32[]{:S(2)}, u32[]{:S(2)}) collective-permute-start(bf16[144,1152]{1,0:T(8,128)(2,1)S(1)} %shard_map.50.refs_6_), channel_id=1, source_target_pairs={{0,4},{4,8},{8,12},{12,0},{1,5},{5,9},{9,13},{13,1},{2,6},{6,10},{... | collective-permute-start | bytes 995336 | tf_op jit(solution)/shard_map/ppermute | solution.py:27
  36.7 19.2 %collective-permute-start.4 = (bf16[144,1152]{1,0:T(8,128)(2,1)S(1)}, bf16[144,1152]{1,0:T(8,128)(2,1)}, u32[]{:S(2)}, u32[]{:S(2)}) collective-permute-start(bf16[144,1152]{1,0:T(8,128)(2,1)S(1)} %shard_map.50.refs_6_), channel_id=1, source_target_pairs={{0,8},{4,12},{8,0},{12,4},{1,9},{5,13},{9,1},{13,5},{2,10},{6,14},... | collective-permute-start | bytes 995336 | tf_op jit(solution)/shard_map/ppermute | solution.py:27
  64.8 1.1 copy-start.4
  65.8 60.1 %all-to-all-start.1 = ((bf16[4,160,1152]{2,1,0:T(8,128)(2,1)}), bf16[4,160,1152]{2,1,0:T(8,128)(2,1)S(1)}, u32[]{:S(2)}, u32[]{:S(2)}) async-start(bf16[4,160,1152]{2,1,0:T(8,128)(2,1)} %get-tuple-element.19), calls=%async_computation.1 | async-start | bytes 2949120 | tf_op jit(solution)/shard_map/all_to_all | solution.py:228
  70.5 1.3 %copy-start.5 = (bf16[576,1152]{1,0:T(8,128)(2,1)S(1)}, bf16[576,1152]{1,0:T(8,128)(2,1)}, u32[]{:S(2)}) copy-start(bf16[576,1152]{1,0:T(8,128)(2,1)} %copy-done.4) | copy-start | bytes 3981316
  73.3 11.6 %collective-permute-start.7 = (bf16[144,1152]{1,0:T(8,128)(2,1)S(1)}, bf16[144,1152]{1,0:T(8,128)(2,1)S(1)}, u32[]{:S(2)}, u32[]{:S(2)}) collective-permute-start(bf16[144,1152]{1,0:T(8,128)(2,1)S(1)} %get-tuple-element.25), channel_id=1, source_target_pairs={{0,8},{4,12},{8,0},{12,4},{1,9},{5,13},{9,1},{13,5},{2,10},{6,14},... | collective-permute-start | bytes 995336 | tf_op jit(solution)/shard_map/ppermute | solution.py:27
  76.9 15.1 %collective-permute-start.8 = (bf16[144,1152]{1,0:T(8,128)(2,1)S(1)}, bf16[144,1152]{1,0:T(8,128)(2,1)S(1)}, u32[]{:S(2)}, u32[]{:S(2)}) collective-permute-start(bf16[144,1152]{1,0:T(8,128)(2,1)S(1)} %get-tuple-element.26), channel_id=1, source_target_pairs={{0,12},{4,0},{8,4},{12,8},{1,13},{5,1},{9,5},{13,9},{2,14},{6,2},{... | collective-permute-start | bytes 995336 | tf_op jit(solution)/shard_map/ppermute | solution.py:27
  79.7 13.9 %collective-permute-start.9 = (bf16[144,1152]{1,0:T(8,128)(2,1)S(1)}, bf16[144,1152]{1,0:T(8,128)(2,1)S(1)}, u32[]{:S(2)}, u32[]{:S(2)}) collective-permute-start(bf16[144,1152]{1,0:T(8,128)(2,1)S(1)} %get-tuple-element.27), channel_id=1, source_target_pairs={{0,4},{4,8},{8,12},{12,0},{1,5},{5,9},{9,13},{13,1},{2,6},{6,10},{... | collective-permute-start | bytes 995336 | tf_op jit(solution)/shard_map/ppermute | solution.py:27
  93.8 29.9 %collective-permute-start.10 = (bf16[144,1152]{1,0:T(8,128)(2,1)S(1)}, bf16[144,1152]{1,0:T(8,128)(2,1)S(1)}, u32[]{:S(2)}, u32[]{:S(2)}) collective-permute-start(bf16[144,1152]{1,0:T(8,128)(2,1)S(1)} %shard_map.55), channel_id=1, source_target_pairs={{0,752},{16,0},{32,16},{48,32},{64,48},{80,64},{96,80},{112,96},{1... | collective-permute-start | bytes 995336 | tf_op jit(solution)/shard_map/ppermute | solution.py:27
  97.8 26.0 %collective-permute-start.11 = (bf16[144,1152]{1,0:T(8,128)(2,1)S(1)}, bf16[144,1152]{1,0:T(8,128)(2,1)S(1)}, u32[]{:S(2)}, u32[]{:S(2)}) collective-permute-start(bf16[144,1152]{1,0:T(8,128)(2,1)S(1)} %get-tuple-element.28), channel_id=1, source_target_pairs={{0,8},{4,12},{8,0},{12,4},{1,9},{5,13},{9,1},{13,5},{2,10},{6,14},... | collective-permute-start | bytes 995336 | tf_op jit(solution)/shard_map/ppermute | solution.py:27
  101.1 22.7 %collective-permute-start.12 = (bf16[144,1152]{1,0:T(8,128)(2,1)S(1)}, bf16[144,1152]{1,0:T(8,128)(2,1)S(1)}, u32[]{:S(2)}, u32[]{:S(2)}) collective-permute-start(bf16[144,1152]{1,0:T(8,128)(2,1)S(1)} %get-tuple-element.29), channel_id=1, source_target_pairs={{0,12},{4,0},{8,4},{12,8},{1,13},{5,1},{9,5},{13,9},{2,14},{6,2},{... | collective-permute-start | bytes 995336 | tf_op jit(solution)/shard_map/ppermute | solution.py:27
  103.9 19.9 %collective-permute-start.13 = (bf16[144,1152]{1,0:T(8,128)(2,1)S(1)}, bf16[144,1152]{1,0:T(8,128)(2,1)S(1)}, u32[]{:S(2)}, u32[]{:S(2)}) collective-permute-start(bf16[144,1152]{1,0:T(8,128)(2,1)S(1)} %get-tuple-element.30), channel_id=1, source_target_pairs={{0,4},{4,8},{8,12},{12,0},{1,5},{5,9},{9,13},{13,1},{2,6},{6,10},{... | collective-permute-start | bytes 995336 | tf_op jit(solution)/shard_map/ppermute | solution.py:27
  123.7 1.0 copy-start.3
  123.8 2.1 %copy-start.1 = (bf16[144,1152]{1,0:T(8,128)(2,1)S(1)}, bf16[144,1152]{1,0:T(8,128)(2,1)}, u32[]{:S(2)}) copy-start(bf16[144,1152]{1,0:T(8,128)(2,1)} %raw_ref.2) | copy-start | bytes 995332

commit v5 on v4

--- a/solution.py
+++ b/solution.py
@@ -1,5 +1,3 @@
-import functools
-
 import jax
 import jax.numpy as jnp
 from jax import lax
@@ -18,13 +16,31 @@
 LOSS_ROWS = 16
 CHUNK = 16
 LANES = 128
+HOPS = (2, 1, 3)
 WEIGHT = 26_000_000_000
 HOME_WEIGHT = 4_000_000_000
+FAR_WEIGHT = 10_000_000_000
 
 
 def shifted(value, axis, steps):
     count = lax.axis_size(axis)
     return lax.ppermute(value, axis, [(i, (i + steps) % count) for i in range(count)])
+
+
+def across_z(value, bit):
+    return lax.ppermute(value, "z", [(z, z ^ bit) for z in range(NZ)])
+
+
+def next_group(value, back):
+    count = lax.axis_size("g")
+    pairs = [(2 * g + 1, 2 * ((g + 1) % count)) for g in range(count)]
+    if back:
+        pairs = [(b, a) for a, b in pairs]
+    return lax.ppermute(value, BLK, pairs)
+
+
+def first_core(value, steps):
+    return lax.ppermute(value, ("core", "x"), [(x, (x + steps) % NX) for x in range(NX)])
 
 
 def vmem_call(body, ins, outs, limit, scratch=(), flops=0, transcendentals=0, smem=0):
@@ -68,8 +84,8 @@
 
 def slopes_kernel(*refs):
     place_ref, img_all, texts = refs[0], refs[1], refs[2:10]
-    slopes_ref, out_ref = refs[10:12]
-    txt_all, scores, lanes_ref = refs[12:15]
+    slopes_ref, keep, send = refs[10:13]
+    txt_all, scores, lanes_ref, low, tails = refs[13:18]
     own = img_all.shape[0] // NZ
     first = place_ref[0] * (own // CHUNK)
     for s in range(8):
@@ -111,15 +127,21 @@
         chunk(i, False)
 
     loss_row = jnp.sum(lanes_ref[...].T, axis=0, keepdims=True)
-    grads = jnp.dot(slopes_ref[...], txt_all[...], preferred_element_type=F32).astype(BF16)
+    low[...] = jnp.dot(slopes_ref[...], txt_all[...], preferred_element_type=F32).astype(BF16)
     row = lax.broadcasted_iota(jnp.int32, (LOSS_ROWS, own), 0)
-    for s in range(NZ):
-        out_ref[s, 0:own, :] = grads[s * own : (s + 1) * own, :]
-        loss = loss_row[:, s * own : (s + 1) * own]
+    tails[...] = jnp.zeros(tails.shape, BF16)
+    for z in range(NZ):
+        loss = loss_row[:, z * own : (z + 1) * own]
         main = loss.astype(BF16).astype(F32)
         both = jnp.where(row == 0, main, jnp.where(row == 1, loss - main, 0.0))
-        out_ref[s, own : own + LOSS_ROWS, :] = jnp.zeros((LOSS_ROWS, out_ref.shape[2]), BF16)
-        out_ref[s, own : own + LOSS_ROWS, 0:own] = both.astype(BF16)
+        tails[z, :, 0:own] = both.astype(BF16)
+    tall = own + LOSS_ROWS
+    for s, bits in enumerate((0, 2, 1, 3)):
+        z = place_ref[0] ^ bits
+        out_ref = keep if s < 2 else send
+        at = s % 2 * tall
+        out_ref[at : at + own, :] = low[pl.ds(pl.multiple_of(z * own, CHUNK), own), :]
+        out_ref[at + own : at + tall, :] = tails[z]
 
 
 def slopes_call(place, images, texts):
@@ -129,12 +151,14 @@
     return vmem_call(
         slopes_kernel,
         [place, images] + list(texts),
-        [shape((rows, cols), BF16), shape((NZ, own + LOSS_ROWS, features), BF16)],
+        [shape((rows, cols), BF16)] + [shape((2 * (own + LOSS_ROWS), features), BF16)] * 2,
         18,
         [
             pltpu.VMEM((cols, features), BF16),
             pltpu.VMEM((rows, cols), F32),
             pltpu.VMEM((rows, LANES), F32),
+            pltpu.VMEM((rows, features), BF16),
+            pltpu.VMEM((NZ, LOSS_ROWS, features), BF16),
         ],
         flops=4 * rows * cols * features,
         transcendentals=3 * rows * cols,
@@ -142,32 +166,35 @@
     )
 
 
-def text_kernel(base, slopes_ref, img_all, *parts):
+def text_grads(slopes, images):
+    return lax.dot_general(
+        slopes, images, (((0,), (0,)), ((), ())), preferred_element_type=F32
+    )
+
+
+def later_parts_kernel(slopes_ref, img_all, stack, *parts):
     own = parts[0].shape[0]
-    cols = len(parts) * own
-    wide = slopes_ref.shape[1]
-    start = base * cols // LANES * LANES
-    grads = lax.dot_general(
-        slopes_ref[:, start : wide if base else -(-cols // LANES) * LANES],
-        img_all[...],
-        (((0,), (0,)), ((), ())),
-        preferred_element_type=F32,
-    ).astype(BF16)
-    skip = base * cols - start
+    cols = stack.shape[0]
+    start = cols // LANES * LANES
+    grads = text_grads(slopes_ref[:, start:], img_all[...]).astype(BF16)
+    stack[...] = grads[cols - start :, :]
     for s, part in enumerate(parts):
-        part[...] = grads[skip + s * own : skip + (s + 1) * own, :]
-
-
-def text_call(base, slopes, images):
-    rows, features = images.shape
-    own = rows // NZ
-    return vmem_call(
-        functools.partial(text_kernel, base),
-        [slopes, images],
-        [shape((own, features), BF16)] * NX,
-        12,
-        flops=2 * rows * NX * own * features,
-    )
+        at = cols - start + s * own
+        part[...] = grads[at : at + own, :]
+
+
+def now_parts_kernel(slopes_ref, img_all, other, *parts):
+    own = parts[0].shape[0]
+    cols = other.shape[0]
+    grads = text_grads(slopes_ref[:, 0 : -(-cols // LANES) * LANES], img_all[...])
+    grads = (grads[0:cols, :] + other[...].astype(F32)).astype(BF16)
+    for s, part in enumerate(parts):
+        part[...] = grads[s * own : (s + 1) * own, :]
+
+
+def text_call(body, ins, outs):
+    flops = 2 * ins[0].shape[0] * ins[0].shape[1] * ins[1].shape[1] // 2
+    return vmem_call(body, ins, outs, 12, flops=flops)
 
 
 def project(values, grads):
@@ -176,13 +203,18 @@
     return (grads - unit * radial) / length
 
 
-def image_end_kernel(raw_ref, parts_ref, grad_ref, loss_ref):
+def far_kernel(mine, theirs, out_ref):
+    tall = out_ref.shape[0]
+    out_ref[...] = (mine[tall:, :].astype(F32) + theirs[tall:, :].astype(F32)).astype(BF16)
+
+
+def image_end_kernel(raw_ref, mine, near, far, grad_ref, loss_ref):
     own = raw_ref.shape[0]
-    grads = parts_ref[0, 0:own, :].astype(F32)
-    tail = parts_ref[0, own : own + LOSS_ROWS, 0:own].astype(F32)
-    for z in range(1, NZ):
-        grads = grads + parts_ref[z, 0:own, :].astype(F32)
-        tail = tail + parts_ref[z, own : own + LOSS_ROWS, 0:own].astype(F32)
+    grads = jnp.zeros(raw_ref.shape, F32)
+    tail = jnp.zeros((LOSS_ROWS, own), F32)
+    for part in (mine, near, far):
+        grads = grads + part[0:own, :].astype(F32)
+        tail = tail + part[own : own + LOSS_ROWS, 0:own].astype(F32)
     grad_ref[...] = project(raw_ref[...], grads)
     loss_ref[...] = jnp.sum(tail, axis=0, keepdims=True)
 
@@ -204,11 +236,7 @@
 
 
 def spread_x(value):
-    return [value] + [shifted(value, "x", s) for s in (2, 1, 3)]
-
-
-def return_x(parts):
-    return [parts[0]] + [shifted(p, "x", -s) for p, s in zip(parts[1:], (2, 1, 3))]
+    return [value] + [shifted(value, "x", s) for s in HOPS]
 
 
 def on_device(images, texts):
@@ -224,16 +252,24 @@
     later_slots = spread_x(moved_low)
 
     place = lax.axis_index("z").reshape(1).astype(jnp.int32)
-    slopes, img_parts = slopes_call(place, img_all, now_slots + later_slots)
-    img_back = lax.all_to_all(img_parts, "z", 0, 0)
-    later_back = return_x(text_call(1, slopes, img_all))
+    slopes, keep, send = slopes_call(place, img_all, now_slots + later_slots)
+    back_near = across_z(send, 1)
+    tall = shape((own + LOSS_ROWS, features), BF16)
+    (far_send,) = vmem_call(far_kernel, [keep, back_near], [tall], 8, flops=FAR_WEIGHT)
+    back_far = across_z(far_send, 2)
+    all_x = shape((NX * own, features), BF16)
+    out = text_call(later_parts_kernel, [slopes, img_all], [all_x] + [unit] * NX)
+    across = lax.ppermute(out[0], "core", [(1, 0)])
+    later_back = [out[1]] + [first_core(p, -s) for p, s in zip(out[2:], HOPS)]
     (later,) = vmem_call(later_kernel, later_back, [unit], 8)
-    home = shifted(later, BLK, -1)
-    now_back = return_x(text_call(0, slopes, img_all))
-
+    home = next_group(later, True)
+    parts = text_call(now_parts_kernel, [slopes, img_all, across], [unit] * NX)
+    now_back = [parts[0]] + [shifted(p, "x", -s) for p, s in zip(parts[1:], HOPS)]
+
+    back_far, home, now_back = lax.optimization_barrier((back_far, home, now_back))
     wide = shape((own, features), F32)
     image_grad, row_loss = vmem_call(
-        image_end_kernel, [images, img_back], [wide, shape((1, own), F32)], 12
+        image_end_kernel, [images, keep, back_near, back_far], [wide, shape((1, own), F32)], 12
     )
     (base,) = vmem_call(base_kernel, [now_back[0], home], [wide], 8, flops=HOME_WEIGHT)
     (text_grad,) = vmem_call(text_end_kernel, [texts, base] + now_back[1:], [wide], 12)

time: 128 us -> 123 us (0.961)
  the two profiles are of different devices: /device:TPU:65 before, /device:TPU:32 now
where the time goes in v5:
time: 123 us; the launch traced here: 122 us
  starting transfers between devices  64 us (52%)
  waiting for transfers between devices  39.4 us (32%)
  Pallas kernels  14.9 us (12%)
  local copies, waits for them, and re-layouts  2.84 us (2%)
    ppermute x10, starting transfers between devices, shifted(): lax.ppermute(value, axis, [(i, (i + steps) % count) for i in range(count)])  30.8 us
    ppermute x2, waiting for transfers between devices, across_z(): return lax.ppermute(value, 'z', [(z, z ^ bit) for z in range(NZ)])  18 us
    pallas_call x10, Pallas kernels, vmem_call(): pl.pallas_call(body, out_shape=list(outs), in_specs=[pl.BlockSpec(memory_...  14.9 us
    ppermute x10, waiting for transfers between devices, shifted(): lax.ppermute(value, axis, [(i, (i + steps) % count) for i in range(count)])  14 us
    ppermute x2, starting transfers between devices, across_z(): return lax.ppermute(value, 'z', [(z, z ^ bit) for z in range(NZ)])  12.5 us
    ppermute x3, starting transfers between devices, first_core(): lax.ppermute(value, ('core', 'x'), [(x, (x + steps) % NX) for x in range(...  10.8 us
    ppermute x3, waiting for transfers between devices, first_core(): lax.ppermute(value, ('core', 'x'), [(x, (x + steps) % NX) for x in range(...  7.41 us
    all_to_all x1, starting transfers between devices, on_device(): img_all = lax.all_to_all(spread, 'z', 0, 0).reshape(NZ * own, features)  7.26 us
  transfers between devices with their start and end apart: 18, of which 6 were waited for; matrix products, arithmetic and copies ran while one was open for 0% of the time, Pallas kernels for 4%

profile of v5, /device:TPU:32, one launch (start us, length us, event | category | flops | bytes accessed | tf_op | source)
XLA Modules:
  0.0 122.1 jit_solution(9977161836542769634)
XLA Ops:
  0.6 1.9 %collective-permute-start.3 = (bf16[144,1152]{1,0:T(8,128)(2,1)}, bf16[144,1152]{1,0:T(8,128)(2,1)S(1)}, u32[]{:S(2)}, u32[]{:S(2)}) collective-permute-start(bf16[144,1152]{1,0:T(8,128)(2,1)} %raw_ref.3), channel_id=1, source_target_pairs={{0,16},{16,32},{32,48},{48,64},{64,80},{80,96},{96,112},{112,128},... | collective-permute-start | bytes 995336 | tf_op jit(solution)/shard_map/ppermute | solution.py:27
  2.6 0.0 copy-start
  2.6 1.0 copy-done
  3.5 0.0 copy-start.2
  3.5 1.0 copy-done.2
  4.5 1.3 %shard_map.49 = (bf16[4,144,1152]{2,1,0:T(8,128)(2,1)}, bf16[144,1152]{1,0:T(8,128)(2,1)S(1)}) custom-call(bf16[144,1152]{1,0:T(8,128)(2,1)S(1)} %copy-done.2, bf16[144,1152]{1,0:T(8,128)(2,1)S(1)} %copy-done), custom_call_target="tpu_custom_call" | custom-call | bytes 2322432 | tf_op jit(solution)/shard_map/pallas_call | solution.py:48
  5.8 7.3 %all-to-all-start = ((bf16[4,144,1152]{2,1,0:T(8,128)(2,1)}), bf16[4,144,1152]{2,1,0:T(8,128)(2,1)S(1)}, u32[]{:S(2)}, u32[]{:S(2)}) async-start(bf16[4,144,1152]{2,1,0:T(8,128)(2,1)} %get-tuple-element.25), calls=%async_computation | async-start | bytes 2654208 | tf_op jit(solution)/shard_map/all_to_all | solution.py:249
  13.1 4.7 %collective-permute-start.2 = (bf16[144,1152]{1,0:T(8,128)(2,1)S(1)}, bf16[144,1152]{1,0:T(8,128)(2,1)S(1)}, u32[]{:S(2)}, u32[]{:S(2)}) collective-permute-start(bf16[144,1152]{1,0:T(8,128)(2,1)S(1)} %get-tuple-element.26.refs_2_), channel_id=1, source_target_pairs={{0,12},{4,0},{8,4},{12,8},{1,13},{5,1},{9,5},{13,9},{2,14},{6,2},{... | collective-permute-start | bytes 995336 | tf_op jit(solution)/shard_map/ppermute | solution.py:27
  17.7 1.9 %collective-permute-start.1 = (bf16[144,1152]{1,0:T(8,128)(2,1)S(1)}, bf16[144,1152]{1,0:T(8,128)(2,1)S(1)}, u32[]{:S(2)}, u32[]{:S(2)}) collective-permute-start(bf16[144,1152]{1,0:T(8,128)(2,1)S(1)} %get-tuple-element.26.refs_2_), channel_id=1, source_target_pairs={{0,4},{4,8},{8,12},{12,0},{1,5},{5,9},{9,13},{13,1},{2,6},{6,10},{... | collective-permute-start | bytes 995336 | tf_op jit(solution)/shard_map/ppermute | solution.py:27
  19.7 4.2 %collective-permute-start = (bf16[144,1152]{1,0:T(8,128)(2,1)S(1)}, bf16[144,1152]{1,0:T(8,128)(2,1)S(1)}, u32[]{:S(2)}, u32[]{:S(2)}) collective-permute-start(bf16[144,1152]{1,0:T(8,128)(2,1)S(1)} %get-tuple-element.26.refs_2_), channel_id=1, source_target_pairs={{0,8},{4,12},{8,0},{12,4},{1,9},{5,13},{9,1},{13,5},{2,10},{6,14},... | collective-permute-start | bytes 995336 | tf_op jit(solution)/shard_map/ppermute | solution.py:27
  23.9 0.0 collective-permute-done.3.txt_ref
  23.9 0.2 shard_map.50.refs_6_
  24.0 3.0 %collective-permute-start.6 = (bf16[144,1152]{1,0:T(8,128)(2,1)S(1)}, bf16[144,1152]{1,0:T(8,128)(2,1)S(1)}, u32[]{:S(2)}, u32[]{:S(2)}) collective-permute-start(bf16[144,1152]{1,0:T(8,128)(2,1)S(1)} %shard_map.50.refs_6_), channel_id=1, source_target_pairs={{0,12},{4,0},{8,4},{12,8},{1,13},{5,1},{9,5},{13,9},{2,14},{6,2},{... | collective-permute-start | bytes 995336 | tf_op jit(solution)/shard_map/ppermute | solution.py:27
  27.1 2.8 %collective-permute-start.5 = (bf16[144,1152]{1,0:T(8,128)(2,1)S(1)}, bf16[144,1152]{1,0:T(8,128)(2,1)}, u32[]{:S(2)}, u32[]{:S(2)}) collective-permute-start(bf16[144,1152]{1,0:T(8,128)(2,1)S(1)} %shard_map.50.refs_6_), channel_id=1, source_target_pairs={{0,4},{4,8},{8,12},{12,0},{1,5},{5,9},{9,13},{13,1},{2,6},{6,10},{... | collective-permute-start | bytes 995336 | tf_op jit(solution)/shard_map/ppermute | solution.py:27
  29.9 0.0 collective-permute-done.2.refs_5_
  29.9 3.8 %collective-permute-start.4 = (bf16[144,1152]{1,0:T(8,128)(2,1)S(1)}, bf16[144,1152]{1,0:T(8,128)(2,1)}, u32[]{:S(2)}, u32[]{:S(2)}) collective-permute-start(bf16[144,1152]{1,0:T(8,128)(2,1)S(1)} %shard_map.50.refs_6_), channel_id=1, source_target_pairs={{0,8},{4,12},{8,0},{12,4},{1,9},{5,13},{9,1},{13,5},{2,10},{6,14},... | collective-permute-start | bytes 995336 | tf_op jit(solution)/shard_map/ppermute | solution.py:27
  33.7 0.0 collective-permute-done.1.refs_4_
  33.7 0.0 collective-permute-done.refs_3_
  33.7 10.4 %collective-permute-done.6.refs_9_ = bf16[144,1152]{1,0:T(8,128)(2,1)S(1)} collective-permute-done((bf16[144,1152]{1,0:T(8,128)(2,1)S(1)}, bf16[144,1152]{1,0:T(8,128)(2,1)S(1)}, u32[]{:S(2)}, u32[]{:S(2)}) %collective-permute-start.6) | collective-permute-done | bytes 331808 | tf_op jit(solution)/shard_map/ppermute | solution.py:27
  44.1 2.1 %collective-permute-done.5.refs_8_ = bf16[144,1152]{1,0:T(8,128)(2,1)} collective-permute-done((bf16[144,1152]{1,0:T(8,128)(2,1)S(1)}, bf16[144,1152]{1,0:T(8,128)(2,1)}, u32[]{:S(2)}, u32[]{:S(2)}) %collective-permute-start.5) | collective-permute-done | bytes 331808 | tf_op jit(solution)/shard_map/ppermute | solution.py:27
  46.2 1.5 %collective-permute-done.4.refs_7_ = bf16[144,1152]{1,0:T(8,128)(2,1)} collective-permute-done((bf16[144,1152]{1,0:T(8,128)(2,1)S(1)}, bf16[144,1152]{1,0:T(8,128)(2,1)}, u32[]{:S(2)}, u32[]{:S(2)}) %collective-permute-start.4) | collective-permute-done | bytes 331808 | tf_op jit(solution)/shard_map/ppermute | solution.py:27
  47.7 0.0 all-to-all-done
  47.7 7.8 %shard_map.51 = (bf16[576,1152]{1,0:T(8,128)(2,1)S(1)}, bf16[320,1152]{1,0:T(8,128)(2,1)S(1)}, bf16[320,1152]{1,0:T(8,128)(2,1)S(1)}) custom-call(s32[1]{0:T(128)} %bitcast.refs_0_, bf16[576,1152]{1,0:T(8,128)(2,1)S(1)} %bitcast.3, bf16[144,1152]{1,0:T(8,128)(2,1)S(1)} %get-tuple-element.26.refs_2_, bf16[144,1152]{1,0:T(8,128)(2,1)S(1)} %collective-permute-done.refs_3_, ...), custom_call_target="tpu_custom_call" | custom-call | flops 3057647616 | bytes 6782980 | tf_op jit(solution)/shard_map/pallas_call | solution.py:48
  55.5 7.4 %collective-permute-start.7 = (bf16[320,1152]{1,0:T(8,128)(2,1)S(1)}, bf16[320,1152]{1,0:T(8,128)(2,1)S(1)}, u32[]{:S(2)}, u32[]{:S(2)}) collective-permute-start(bf16[320,1152]{1,0:T(8,128)(2,1)S(1)} %get-tuple-element.28), channel_id=1, source_target_pairs={{0,1},{1,0},{2,3},{3,2},{4,5},{5,4},{6,7},{7,6},{8,9},{9,8},{10,11... | collective-permute-start | bytes 2211848 | tf_op jit(solution)/shard_map/ppermute | solution.py:31
  62.9 1.4 %shard_map.53 = (bf16[576,1152]{1,0:T(8,128)(2,1)S(1)}, bf16[144,1152]{1,0:T(8,128)(2,1)S(1)}, bf16[144,1152]{1,0:T(8,128)(2,1)S(1)}, bf16[144,1152]{1,0:T(8,128)(2,1)S(1)}, bf16[144,1152]{1,0:T(8,128)(2,1)S(1)}) custom-call(bf16[576,1152]{1,0:T(8,128)(2,1)S(1)} %get-tuple-element.29.slopes_ref, bf16[576,1152]{1,0:T(8,128)(2,1)S(1)} %bitcast.4), custom_call_target="tpu_custom_call" | custom-call | flops 764411904 | bytes 5308416 | tf_op jit(solution)/shard_map/pallas_call | solution.py:48
  64.3 1.3 %collective-permute-start.13 = (bf16[576,1152]{1,0:T(8,128)(2,1)S(1)}, bf16[576,1152]{1,0:T(8,128)(2,1)S(1)}, u32[]{:S(2)}, u32[]{:S(2)}) collective-permute-start(bf16[576,1152]{1,0:T(8,128)(2,1)S(1)} %get-tuple-element.34), channel_id=1, source_target_pairs={{16,0},{17,1},{18,2},{19,3},{20,4},{21,5},{22,6},{23,7},{24,8},{25... | collective-permute-start | bytes 3981320 | tf_op jit(solution)/shard_map/ppermute | solution.py:262
  65.6 4.9 %collective-permute-start.9 = (bf16[144,1152]{1,0:T(8,128)(2,1)S(1)}, bf16[144,1152]{1,0:T(8,128)(2,1)S(1)}, u32[]{:S(2)}, u32[]{:S(2)}) collective-permute-start(bf16[144,1152]{1,0:T(8,128)(2,1)S(1)} %get-tuple-element.31), channel_id=1, source_target_pairs={{0,8},{4,12},{8,0},{12,4},{1,9},{5,13},{9,1},{13,5},{2,10},{6,14},... | collective-permute-start | bytes 995336 | tf_op jit(solution)/shard_map/ppermute | solution.py:43
  70.6 3.0 %collective-permute-start.10 = (bf16[144,1152]{1,0:T(8,128)(2,1)S(1)}, bf16[144,1152]{1,0:T(8,128)(2,1)S(1)}, u32[]{:S(2)}, u32[]{:S(2)}) collective-permute-start(bf16[144,1152]{1,0:T(8,128)(2,1)S(1)} %get-tuple-element.32), channel_id=1, source_target_pairs={{0,12},{4,0},{8,4},{12,8},{1,13},{5,1},{9,5},{13,9},{2,14},{6,2},{... | collective-permute-start | bytes 995336 | tf_op jit(solution)/shard_map/ppermute | solution.py:43
  73.6 2.8 %collective-permute-start.11 = (bf16[144,1152]{1,0:T(8,128)(2,1)S(1)}, bf16[144,1152]{1,0:T(8,128)(2,1)S(1)}, u32[]{:S(2)}, u32[]{:S(2)}) collective-permute-start(bf16[144,1152]{1,0:T(8,128)(2,1)S(1)} %get-tuple-element.33), channel_id=1, source_target_pairs={{0,4},{4,8},{8,12},{12,0},{1,5},{5,9},{9,13},{13,1},{2,6},{6,10},{... | collective-permute-start | bytes 995336 | tf_op jit(solution)/shard_map/ppermute | solution.py:43
  76.4 0.0 collective-permute-done.9.b
  76.5 3.3 %collective-permute-done.10.c = bf16[144,1152]{1,0:T(8,128)(2,1)S(1)} collective-permute-done((bf16[144,1152]{1,0:T(8,128)(2,1)S(1)}, bf16[144,1152]{1,0:T(8,128)(2,1)S(1)}, u32[]{:S(2)}, u32[]{:S(2)}) %collective-permute-start.10) | collective-permute-done | bytes 331808 | tf_op jit(solution)/shard_map/ppermute | solution.py:43
  79.8 4.1 %collective-permute-done.11.d = bf16[144,1152]{1,0:T(8,128)(2,1)S(1)} collective-permute-done((bf16[144,1152]{1,0:T(8,128)(2,1)S(1)}, bf16[144,1152]{1,0:T(8,128)(2,1)S(1)}, u32[]{:S(2)}, u32[]{:S(2)}) %collective-permute-start.11) | collective-permute-done | bytes 331808 | tf_op jit(solution)/shard_map/ppermute | solution.py:43
  83.9 0.2 shard_map.54
  84.0 1.3 %collective-permute-start.12 = (bf16[144,1152]{1,0:T(8,128)(2,1)S(1)}, bf16[144,1152]{1,0:T(8,128)(2,1)S(1)}, u32[]{:S(2)}, u32[]{:S(2)}) collective-permute-start(bf16[144,1152]{1,0:T(8,128)(2,1)S(1)} %shard_map.54), channel_id=1, source_target_pairs={{32,16},{64,48},{96,80},{128,112},{160,144},{192,176},{224,208},{2... | collective-permute-start | bytes 995336 | tf_op jit(solution)/shard_map/ppermute | solution.py:39
  85.4 0.0 collective-permute-done.7.theirs.near
  85.4 0.1 shard_map.52
  85.5 5.2 %collective-permute-start.8 = (bf16[160,1152]{1,0:T(8,128)(2,1)S(1)}, bf16[160,1152]{1,0:T(8,128)(2,1)S(1)}, u32[]{:S(2)}, u32[]{:S(2)}) collective-permute-start(bf16[160,1152]{1,0:T(8,128)(2,1)S(1)} %shard_map.52), channel_id=1, source_target_pairs={{0,2},{1,3},{2,0},{3,1},{4,6},{5,7},{6,4},{7,5},{8,10},{9,11},{10,... | collective-permute-start | bytes 1105928 | tf_op jit(solution)/shard_map/ppermute | solution.py:31
  90.7 0.0 collective-permute-done.13.other
  90.7 1.4 %shard_map.55 = (bf16[144,1152]{1,0:T(8,128)(2,1)S(1)}, bf16[144,1152]{1,0:T(8,128)(2,1)S(1)}, bf16[144,1152]{1,0:T(8,128)(2,1)S(1)}, bf16[144,1152]{1,0:T(8,128)(2,1)S(1)}) custom-call(bf16[576,1152]{1,0:T(8,128)(2,1)S(1)} %get-tuple-element.29.slopes_ref, bf16[576,1152]{1,0:T(8,128)(2,1)S(1)} %bitcast.5, bf16[576,1152]{1,0:T(8,128)(2,1)S(1)} %collective-permute-done.13.other), custom_call_target="tpu_custom_call" | custom-call | flops 764411904 | bytes 5308416 | tf_op jit(solution)/shard_map/pallas_call | solution.py:48
  92.1 2.4 %collective-permute-start.14 = (bf16[144,1152]{1,0:T(8,128)(2,1)S(1)}, bf16[144,1152]{1,0:T(8,128)(2,1)S(1)}, u32[]{:S(2)}, u32[]{:S(2)}) collective-permute-start(bf16[144,1152]{1,0:T(8,128)(2,1)S(1)} %get-tuple-element.36), channel_id=1, source_target_pairs={{0,8},{4,12},{8,0},{12,4},{1,9},{5,13},{9,1},{13,5},{2,10},{6,14},... | collective-permute-start | bytes 995336 | tf_op jit(solution)/shard_map/ppermute | solution.py:27
  94.5 4.2 %collective-permute-start.15 = (bf16[144,1152]{1,0:T(8,128)(2,1)S(1)}, bf16[144,1152]{1,0:T(8,128)(2,1)S(1)}, u32[]{:S(2)}, u32[]{:S(2)}) collective-permute-start(bf16[144,1152]{1,0:T(8,128)(2,1)S(1)} %get-tuple-element.37), channel_id=1, source_target_pairs={{0,12},{4,0},{8,4},{12,8},{1,13},{5,1},{9,5},{13,9},{2,14},{6,2},{... | collective-permute-start | bytes 995336 | tf_op jit(solution)/shard_map/ppermute | solution.py:27
  98.7 1.9 %collective-permute-start.16 = (bf16[144,1152]{1,0:T(8,128)(2,1)S(1)}, bf16[144,1152]{1,0:T(8,128)(2,1)S(1)}, u32[]{:S(2)}, u32[]{:S(2)}) collective-permute-start(bf16[144,1152]{1,0:T(8,128)(2,1)S(1)} %get-tuple-element.38), channel_id=1, source_target_pairs={{0,4},{4,8},{8,12},{12,0},{1,5},{5,9},{9,13},{13,1},{2,6},{6,10},{... | collective-permute-start | bytes 995336 | tf_op jit(solution)/shard_map/ppermute | solution.py:27
  100.7 0.0 collective-permute-done.12.home
  100.7 18.0 %collective-permute-done.8.far = bf16[160,1152]{1,0:T(8,128)(2,1)S(1)} collective-permute-done((bf16[160,1152]{1,0:T(8,128)(2,1)S(1)}, bf16[160,1152]{1,0:T(8,128)(2,1)S(1)}, u32[]{:S(2)}, u32[]{:S(2)}) %collective-permute-start.8) | collective-permute-done | bytes 368672 | tf_op jit(solution)/shard_map/ppermute | solution.py:31
  118.6 0.0 collective-permute-done.14.b
  118.6 0.0 collective-permute-done.15.c
  118.6 0.0 collective-permute-done.16.d
  118.6 0.0 copy-start.1
  118.7 0.1 shard_map.57.base
  118.7 0.9 copy-done.1
  119.6 0.0 copy-start.3
  119.6 1.2 %shard_map.58 = f32[144,1152]{1,0:T(8,128)} custom-call(bf16[144,1152]{1,0:T(8,128)(2,1)S(1)} %copy-done.1, f32[144,1152]{1,0:T(8,128)S(1)} %shard_map.57.base, bf16[144,1152]{1,0:T(8,128)(2,1)S(1)} %collective-permute-done.14.b, bf16[144,1152]{1,0:T(8,128)(2,1)S(1)} %collective-permute-done.15.c, bf16[144,1152]{1,0:T(8,128)(2,1)S(1)} %collective-permute-done.16.d), custom_call_target="tpu_custom_call" | custom-call | bytes 2654208 | tf_op jit(solution)/shard_map/pallas_call | solution.py:48
  120.9 0.0 copy-done.3
  120.9 1.2 shard_map.56
Async XLA Ops:
  0.6 23.2 %collective-permute-start.3 = (bf16[144,1152]{1,0:T(8,128)(2,1)}, bf16[144,1152]{1,0:T(8,128)(2,1)S(1)}, u32[]{:S(2)}, u32[]{:S(2)}) collective-permute-start(bf16[144,1152]{1,0:T(8,128)(2,1)} %raw_ref.3), channel_id=1, source_target_pairs={{0,16},{16,32},{32,48},{48,64},{64,80},{80,96},{96,112},{112,128},... | collective-permute-start | bytes 995336 | tf_op jit(solution)/shard_map/ppermute | solution.py:27
  2.6 1.0 copy-start
  3.5 1.0 copy-start.2
  5.8 41.9 %all-to-all-start = ((bf16[4,144,1152]{2,1,0:T(8,128)(2,1)}), bf16[4,144,1152]{2,1,0:T(8,128)(2,1)S(1)}, u32[]{:S(2)}, u32[]{:S(2)}) async-start(bf16[4,144,1152]{2,1,0:T(8,128)(2,1)} %get-tuple-element.25), calls=%async_computation | async-start | bytes 2654208 | tf_op jit(solution)/shard_map/all_to_all | solution.py:249
  13.1 16.8 %collective-permute-start.2 = (bf16[144,1152]{1,0:T(8,128)(2,1)S(1)}, bf16[144,1152]{1,0:T(8,128)(2,1)S(1)}, u32[]{:S(2)}, u32[]{:S(2)}) collective-permute-start(bf16[144,1152]{1,0:T(8,128)(2,1)S(1)} %get-tuple-element.26.refs_2_), channel_id=1, source_target_pairs={{0,12},{4,0},{8,4},{12,8},{1,13},{5,1},{9,5},{13,9},{2,14},{6,2},{... | collective-permute-start | bytes 995336 | tf_op jit(solution)/shard_map/ppermute | solution.py:27
  17.7 16.0 %collective-permute-start.1 = (bf16[144,1152]{1,0:T(8,128)(2,1)S(1)}, bf16[144,1152]{1,0:T(8,128)(2,1)S(1)}, u32[]{:S(2)}, u32[]{:S(2)}) collective-permute-start(bf16[144,1152]{1,0:T(8,128)(2,1)S(1)} %get-tuple-element.26.refs_2_), channel_id=1, source_target_pairs={{0,4},{4,8},{8,12},{12,0},{1,5},{5,9},{9,13},{13,1},{2,6},{6,10},{... | collective-permute-start | bytes 995336 | tf_op jit(solution)/shard_map/ppermute | solution.py:27
  19.7 14.0 %collective-permute-start = (bf16[144,1152]{1,0:T(8,128)(2,1)S(1)}, bf16[144,1152]{1,0:T(8,128)(2,1)S(1)}, u32[]{:S(2)}, u32[]{:S(2)}) collective-permute-start(bf16[144,1152]{1,0:T(8,128)(2,1)S(1)} %get-tuple-element.26.refs_2_), channel_id=1, source_target_pairs={{0,8},{4,12},{8,0},{12,4},{1,9},{5,13},{9,1},{13,5},{2,10},{6,14},... | collective-permute-start | bytes 995336 | tf_op jit(solution)/shard_map/ppermute | solution.py:27
  24.0 20.0 %collective-permute-start.6 = (bf16[144,1152]{1,0:T(8,128)(2,1)S(1)}, bf16[144,1152]{1,0:T(8,128)(2,1)S(1)}, u32[]{:S(2)}, u32[]{:S(2)}) collective-permute-start(bf16[144,1152]{1,0:T(8,128)(2,1)S(1)} %shard_map.50.refs_6_), channel_id=1, source_target_pairs={{0,12},{4,0},{8,4},{12,8},{1,13},{5,1},{9,5},{13,9},{2,14},{6,2},{... | collective-permute-start | bytes 995336 | tf_op jit(solution)/shard_map/ppermute | solution.py:27
  27.1 19.1 %collective-permute-start.5 = (bf16[144,1152]{1,0:T(8,128)(2,1)S(1)}, bf16[144,1152]{1,0:T(8,128)(2,1)}, u32[]{:S(2)}, u32[]{:S(2)}) collective-permute-start(bf16[144,1152]{1,0:T(8,128)(2,1)S(1)} %shard_map.50.refs_6_), channel_id=1, source_target_pairs={{0,4},{4,8},{8,12},{12,0},{1,5},{5,9},{9,13},{13,1},{2,6},{6,10},{... | collective-permute-start | bytes 995336 | tf_op jit(solution)/shard_map/ppermute | solution.py:27
  29.9 17.8 %collective-permute-start.4 = (bf16[144,1152]{1,0:T(8,128)(2,1)S(1)}, bf16[144,1152]{1,0:T(8,128)(2,1)}, u32[]{:S(2)}, u32[]{:S(2)}) collective-permute-start(bf16[144,1152]{1,0:T(8,128)(2,1)S(1)} %shard_map.50.refs_6_), channel_id=1, source_target_pairs={{0,8},{4,12},{8,0},{12,4},{1,9},{5,13},{9,1},{13,5},{2,10},{6,14},... | collective-permute-start | bytes 995336 | tf_op jit(solution)/shard_map/ppermute | solution.py:27
  55.5 29.8 %collective-permute-start.7 = (bf16[320,1152]{1,0:T(8,128)(2,1)S(1)}, bf16[320,1152]{1,0:T(8,128)(2,1)S(1)}, u32[]{:S(2)}, u32[]{:S(2)}) collective-permute-start(bf16[320,1152]{1,0:T(8,128)(2,1)S(1)} %get-tuple-element.28), channel_id=1, source_target_pairs={{0,1},{1,0},{2,3},{3,2},{4,5},{5,4},{6,7},{7,6},{8,9},{9,8},{10,11... | collective-permute-start | bytes 2211848 | tf_op jit(solution)/shard_map/ppermute | solution.py:31
  64.3 26.3 %collective-permute-start.13 = (bf16[576,1152]{1,0:T(8,128)(2,1)S(1)}, bf16[576,1152]{1,0:T(8,128)(2,1)S(1)}, u32[]{:S(2)}, u32[]{:S(2)}) collective-permute-start(bf16[576,1152]{1,0:T(8,128)(2,1)S(1)} %get-tuple-element.34), channel_id=1, source_target_pairs={{16,0},{17,1},{18,2},{19,3},{20,4},{21,5},{22,6},{23,7},{24,8},{25... | collective-permute-start | bytes 3981320 | tf_op jit(solution)/shard_map/ppermute | solution.py:262
  65.6 10.8 %collective-permute-start.9 = (bf16[144,1152]{1,0:T(8,128)(2,1)S(1)}, bf16[144,1152]{1,0:T(8,128)(2,1)S(1)}, u32[]{:S(2)}, u32[]{:S(2)}) collective-permute-start(bf16[144,1152]{1,0:T(8,128)(2,1)S(1)} %get-tuple-element.31), channel_id=1, source_target_pairs={{0,8},{4,12},{8,0},{12,4},{1,9},{5,13},{9,1},{13,5},{2,10},{6,14},... | collective-permute-start | bytes 995336 | tf_op jit(solution)/shard_map/ppermute | solution.py:43
  70.6 9.2 %collective-permute-start.10 = (bf16[144,1152]{1,0:T(8,128)(2,1)S(1)}, bf16[144,1152]{1,0:T(8,128)(2,1)S(1)}, u32[]{:S(2)}, u32[]{:S(2)}) collective-permute-start(bf16[144,1152]{1,0:T(8,128)(2,1)S(1)} %get-tuple-element.32), channel_id=1, source_target_pairs={{0,12},{4,0},{8,4},{12,8},{1,13},{5,1},{9,5},{13,9},{2,14},{6,2},{... | collective-permute-start | bytes 995336 | tf_op jit(solution)/shard_map/ppermute | solution.py:43
  73.6 10.2 %collective-permute-start.11 = (bf16[144,1152]{1,0:T(8,128)(2,1)S(1)}, bf16[144,1152]{1,0:T(8,128)(2,1)S(1)}, u32[]{:S(2)}, u32[]{:S(2)}) collective-permute-start(bf16[144,1152]{1,0:T(8,128)(2,1)S(1)} %get-tuple-element.33), channel_id=1, source_target_pairs={{0,4},{4,8},{8,12},{12,0},{1,5},{5,9},{9,13},{13,1},{2,6},{6,10},{... | collective-permute-start | bytes 995336 | tf_op jit(solution)/shard_map/ppermute | solution.py:43
  84.0 16.6 %collective-permute-start.12 = (bf16[144,1152]{1,0:T(8,128)(2,1)S(1)}, bf16[144,1152]{1,0:T(8,128)(2,1)S(1)}, u32[]{:S(2)}, u32[]{:S(2)}) collective-permute-start(bf16[144,1152]{1,0:T(8,128)(2,1)S(1)} %shard_map.54), channel_id=1, source_target_pairs={{32,16},{64,48},{96,80},{128,112},{160,144},{192,176},{224,208},{2... | collective-permute-start | bytes 995336 | tf_op jit(solution)/shard_map/ppermute | solution.py:39
  85.5 33.2 %collective-permute-start.8 = (bf16[160,1152]{1,0:T(8,128)(2,1)S(1)}, bf16[160,1152]{1,0:T(8,128)(2,1)S(1)}, u32[]{:S(2)}, u32[]{:S(2)}) collective-permute-start(bf16[160,1152]{1,0:T(8,128)(2,1)S(1)} %shard_map.52), channel_id=1, source_target_pairs={{0,2},{1,3},{2,0},{3,1},{4,6},{5,7},{6,4},{7,5},{8,10},{9,11},{10,... | collective-permute-start | bytes 1105928 | tf_op jit(solution)/shard_map/ppermute | solution.py:31
  92.1 26.5 %collective-permute-start.14 = (bf16[144,1152]{1,0:T(8,128)(2,1)S(1)}, bf16[144,1152]{1,0:T(8,128)(2,1)S(1)}, u32[]{:S(2)}, u32[]{:S(2)}) collective-permute-start(bf16[144,1152]{1,0:T(8,128)(2,1)S(1)} %get-tuple-element.36), channel_id=1, source_target_pairs={{0,8},{4,12},{8,0},{12,4},{1,9},{5,13},{9,1},{13,5},{2,10},{6,14},... | collective-permute-start | bytes 995336 | tf_op jit(solution)/shard_map/ppermute | solution.py:27
  94.5 24.1 %collective-permute-start.15 = (bf16[144,1152]{1,0:T(8,128)(2,1)S(1)}, bf16[144,1152]{1,0:T(8,128)(2,1)S(1)}, u32[]{:S(2)}, u32[]{:S(2)}) collective-permute-start(bf16[144,1152]{1,0:T(8,128)(2,1)S(1)} %get-tuple-element.37), channel_id=1, source_target_pairs={{0,12},{4,0},{8,4},{12,8},{1,13},{5,1},{9,5},{13,9},{2,14},{6,2},{... | collective-permute-start | bytes 995336 | tf_op jit(solution)/shard_map/ppermute | solution.py:27
  98.7 19.9 %collective-permute-start.16 = (bf16[144,1152]{1,0:T(8,128)(2,1)S(1)}, bf16[144,1152]{1,0:T(8,128)(2,1)S(1)}, u32[]{:S(2)}, u32[]{:S(2)}) collective-permute-start(bf16[144,1152]{1,0:T(8,128)(2,1)S(1)} %get-tuple-element.38), channel_id=1, source_target_pairs={{0,4},{4,8},{8,12},{12,0},{1,5},{5,9},{9,13},{13,1},{2,6},{6,10},{... | collective-permute-start | bytes 995336 | tf_op jit(solution)/shard_map/ppermute | solution.py:27
  118.6 1.0 copy-start.1
  119.6 1.2 %copy-start.3 = (bf16[144,1152]{1,0:T(8,128)(2,1)S(1)}, bf16[144,1152]{1,0:T(8,128)(2,1)}, u32[]{:S(2)}) copy-start(bf16[144,1152]{1,0:T(8,128)(2,1)} %raw_ref.2) | copy-start | bytes 995332

commit v6 on v5

--- a/solution.py
+++ b/solution.py
@@ -27,8 +27,12 @@
     return lax.ppermute(value, axis, [(i, (i + steps) % count) for i in range(count)])
 
 
-def across_z(value, bit):
-    return lax.ppermute(value, "z", [(z, z ^ bit) for z in range(NZ)])
+def across_z(value, step):
+    pairs = []
+    for core in range(CORES):
+        bit = 1 if step == core else 2
+        pairs += [(core * NZ + z, core * NZ + (z ^ bit)) for z in range(NZ)]
+    return lax.ppermute(value, ("core", "z"), pairs)
 
 
 def next_group(value, back):
@@ -136,7 +140,8 @@
         both = jnp.where(row == 0, main, jnp.where(row == 1, loss - main, 0.0))
         tails[z, :, 0:own] = both.astype(BF16)
     tall = own + LOSS_ROWS
-    for s, bits in enumerate((0, 2, 1, 3)):
+    core = place_ref[1]
+    for s, bits in enumerate((0, 2 - core, 1 + core, 3)):
         z = place_ref[0] ^ bits
         out_ref = keep if s < 2 else send
         at = s % 2 * tall
@@ -251,12 +256,12 @@
     (moved_low,) = vmem_call(moved_kernel, [moved], [unit], 8, flops=WEIGHT)
     later_slots = spread_x(moved_low)
 
-    place = lax.axis_index("z").reshape(1).astype(jnp.int32)
+    place = jnp.stack([lax.axis_index("z"), lax.axis_index("core")]).astype(jnp.int32)
     slopes, keep, send = slopes_call(place, img_all, now_slots + later_slots)
-    back_near = across_z(send, 1)
+    back_near = across_z(send, 0)
     tall = shape((own + LOSS_ROWS, features), BF16)
     (far_send,) = vmem_call(far_kernel, [keep, back_near], [tall], 8, flops=FAR_WEIGHT)
-    back_far = across_z(far_send, 2)
+    back_far = across_z(far_send, 1)
     all_x = shape((NX * own, features), BF16)
     out = text_call(later_parts_kernel, [slopes, img_all], [all_x] + [unit] * NX)
     across = lax.ppermute(out[0], "core", [(1, 0)])

time: 123 us -> 116 us (0.943)
  the two profiles are of different devices: /device:TPU:32 before, /device:TPU:1 now
where the time goes in v6:
time: 116 us; the launch traced here: 115 us
  starting transfers between devices  61.2 us (53%)
  waiting for transfers between devices  34.7 us (30%)
  Pallas kernels  14.9 us (13%)
  local copies, waits for them, and re-layouts  2.85 us (2%)
    ppermute x10, starting transfers between devices, shifted(): lax.ppermute(value, axis, [(i, (i + steps) % count) for i in range(count)])  39.5 us
    ppermute x2, waiting for transfers between devices, across_z(): return lax.ppermute(value, ('core', 'z'), pairs)  16.7 us
    pallas_call x10, Pallas kernels, vmem_call(): pl.pallas_call(body, out_shape=list(outs), in_specs=[pl.BlockSpec(memory_...  14.9 us
    ppermute x10, waiting for transfers between devices, shifted(): lax.ppermute(value, axis, [(i, (i + steps) % count) for i in range(count)])  12.2 us
    ppermute x2, starting transfers between devices, across_z(): return lax.ppermute(value, ('core', 'z'), pairs)  9.72 us
    all_to_all x1, starting transfers between devices, on_device(): img_all = lax.all_to_all(spread, 'z', 0, 0).reshape(NZ * own, features)  6.68 us
    ppermute x1, waiting for transfers between devices, next_group(): return lax.ppermute(value, BLK, pairs)  5.83 us
    unnamed x8, local copies, waits for them, and re-layouts  2.85 us
  transfers between devices with their start and end apart: 18, of which 6 were waited for; matrix products, arithmetic and copies ran while one was open for 0% of the time, Pallas kernels for 4%

profile of v6, /device:TPU:1, one launch (start us, length us, event | category | flops | bytes accessed | tf_op | source)
XLA Modules:
  0.0 114.7 jit_solution(12960097420230044924)
XLA Ops:
  0.6 12.0 %collective-permute-start.3 = (bf16[144,1152]{1,0:T(8,128)(2,1)}, bf16[144,1152]{1,0:T(8,128)(2,1)S(1)}, u32[]{:S(2)}, u32[]{:S(2)}) collective-permute-start(bf16[144,1152]{1,0:T(8,128)(2,1)} %raw_ref.3), channel_id=1, source_target_pairs={{0,16},{16,32},{32,48},{48,64},{64,80},{80,96},{96,112},{112,128},... | collective-permute-start | bytes 995336 | tf_op jit(solution)/shard_map/ppermute | solution.py:27
  12.7 0.0 copy-start
  12.7 1.0 copy-done
  13.7 0.0 copy-start.2
  13.7 1.0 copy-done.2
  14.6 1.3 %shard_map.49 = (bf16[4,144,1152]{2,1,0:T(8,128)(2,1)}, bf16[144,1152]{1,0:T(8,128)(2,1)S(1)}) custom-call(bf16[144,1152]{1,0:T(8,128)(2,1)S(1)} %copy-done.2, bf16[144,1152]{1,0:T(8,128)(2,1)S(1)} %copy-done), custom_call_target="tpu_custom_call" | custom-call | bytes 2322432 | tf_op jit(solution)/shard_map/pallas_call | solution.py:52
  15.9 6.7 %all-to-all-start = ((bf16[4,144,1152]{2,1,0:T(8,128)(2,1)}), bf16[4,144,1152]{2,1,0:T(8,128)(2,1)S(1)}, u32[]{:S(2)}, u32[]{:S(2)}) async-start(bf16[4,144,1152]{2,1,0:T(8,128)(2,1)} %get-tuple-element.25), calls=%async_computation | async-start | bytes 2654208 | tf_op jit(solution)/shard_map/all_to_all | solution.py:254
  22.6 4.6 %collective-permute-start = (bf16[144,1152]{1,0:T(8,128)(2,1)S(1)}, bf16[144,1152]{1,0:T(8,128)(2,1)S(1)}, u32[]{:S(2)}, u32[]{:S(2)}) collective-permute-start(bf16[144,1152]{1,0:T(8,128)(2,1)S(1)} %get-tuple-element.26.refs_2_), channel_id=1, source_target_pairs={{0,8},{4,12},{8,0},{12,4},{1,9},{5,13},{9,1},{13,5},{2,10},{6,14},... | collective-permute-start | bytes 995336 | tf_op jit(solution)/shard_map/ppermute | solution.py:27
  27.3 2.2 %collective-permute-start.1 = (bf16[144,1152]{1,0:T(8,128)(2,1)S(1)}, bf16[144,1152]{1,0:T(8,128)(2,1)S(1)}, u32[]{:S(2)}, u32[]{:S(2)}) collective-permute-start(bf16[144,1152]{1,0:T(8,128)(2,1)S(1)} %get-tuple-element.26.refs_2_), channel_id=1, source_target_pairs={{0,4},{4,8},{8,12},{12,0},{1,5},{5,9},{9,13},{13,1},{2,6},{6,10},{... | collective-permute-start | bytes 995336 | tf_op jit(solution)/shard_map/ppermute | solution.py:27
  29.5 4.3 %collective-permute-start.2 = (bf16[144,1152]{1,0:T(8,128)(2,1)S(1)}, bf16[144,1152]{1,0:T(8,128)(2,1)S(1)}, u32[]{:S(2)}, u32[]{:S(2)}) collective-permute-start(bf16[144,1152]{1,0:T(8,128)(2,1)S(1)} %get-tuple-element.26.refs_2_), channel_id=1, source_target_pairs={{0,12},{4,0},{8,4},{12,8},{1,13},{5,1},{9,5},{13,9},{2,14},{6,2},{... | collective-permute-start | bytes 995336 | tf_op jit(solution)/shard_map/ppermute | solution.py:27
  33.8 0.0 collective-permute-done.3.txt_ref
  33.8 0.2 shard_map.50.refs_6_
  34.0 1.9 %collective-permute-start.4 = (bf16[144,1152]{1,0:T(8,128)(2,1)S(1)}, bf16[144,1152]{1,0:T(8,128)(2,1)S(1)}, u32[]{:S(2)}, u32[]{:S(2)}) collective-permute-start(bf16[144,1152]{1,0:T(8,128)(2,1)S(1)} %shard_map.50.refs_6_), channel_id=1, source_target_pairs={{0,8},{4,12},{8,0},{12,4},{1,9},{5,13},{9,1},{13,5},{2,10},{6,14},... | collective-permute-start | bytes 995336 | tf_op jit(solution)/shard_map/ppermute | solution.py:27
  35.9 2.5 %collective-permute-start.5 = (bf16[144,1152]{1,0:T(8,128)(2,1)S(1)}, bf16[144,1152]{1,0:T(8,128)(2,1)}, u32[]{:S(2)}, u32[]{:S(2)}) collective-permute-start(bf16[144,1152]{1,0:T(8,128)(2,1)S(1)} %shard_map.50.refs_6_), channel_id=1, source_target_pairs={{0,4},{4,8},{8,12},{12,0},{1,5},{5,9},{9,13},{13,1},{2,6},{6,10},{... | collective-permute-start | bytes 995336 | tf_op jit(solution)/shard_map/ppermute | solution.py:27
  38.4 0.0 collective-permute-done.refs_3_
  38.4 4.0 %collective-permute-start.6 = (bf16[144,1152]{1,0:T(8,128)(2,1)S(1)}, bf16[144,1152]{1,0:T(8,128)(2,1)}, u32[]{:S(2)}, u32[]{:S(2)}) collective-permute-start(bf16[144,1152]{1,0:T(8,128)(2,1)S(1)} %shard_map.50.refs_6_), channel_id=1, source_target_pairs={{0,12},{4,0},{8,4},{12,8},{1,13},{5,1},{9,5},{13,9},{2,14},{6,2},{... | collective-permute-start | bytes 995336 | tf_op jit(solution)/shard_map/ppermute | solution.py:27
  42.4 0.1 pad_add_fusion.refs_0_
  42.5 5.0 %collective-permute-done.1.refs_4_ = bf16[144,1152]{1,0:T(8,128)(2,1)S(1)} collective-permute-done((bf16[144,1152]{1,0:T(8,128)(2,1)S(1)}, bf16[144,1152]{1,0:T(8,128)(2,1)S(1)}, u32[]{:S(2)}, u32[]{:S(2)}) %collective-permute-start.1) | collective-permute-done | bytes 331808 | tf_op jit(solution)/shard_map/ppermute | solution.py:27
  47.5 0.0 collective-permute-done.2.refs_5_
  47.5 2.4 %collective-permute-done.4.refs_7_ = bf16[144,1152]{1,0:T(8,128)(2,1)S(1)} collective-permute-done((bf16[144,1152]{1,0:T(8,128)(2,1)S(1)}, bf16[144,1152]{1,0:T(8,128)(2,1)S(1)}, u32[]{:S(2)}, u32[]{:S(2)}) %collective-permute-start.4) | collective-permute-done | bytes 331808 | tf_op jit(solution)/shard_map/ppermute | solution.py:27
  49.9 4.8 %collective-permute-done.5.refs_8_ = bf16[144,1152]{1,0:T(8,128)(2,1)} collective-permute-done((bf16[144,1152]{1,0:T(8,128)(2,1)S(1)}, bf16[144,1152]{1,0:T(8,128)(2,1)}, u32[]{:S(2)}, u32[]{:S(2)}) %collective-permute-start.5) | collective-permute-done | bytes 331808 | tf_op jit(solution)/shard_map/ppermute | solution.py:27
  54.7 0.0 collective-permute-done.6.refs_9_
  54.7 0.0 all-to-all-done
  54.7 7.8 %shard_map.51 = (bf16[576,1152]{1,0:T(8,128)(2,1)S(1)}, bf16[320,1152]{1,0:T(8,128)(2,1)S(1)}, bf16[320,1152]{1,0:T(8,128)(2,1)S(1)}) custom-call(s32[2]{0:T(128)S(1)} %pad_add_fusion.refs_0_, bf16[576,1152]{1,0:T(8,128)(2,1)S(1)} %bitcast.4, bf16[144,1152]{1,0:T(8,128)(2,1)S(1)} %get-tuple-element.26.refs_2_, ...), custom_call_target="tpu_custom_call" | custom-call | flops 3057647616 | bytes 6782984 | tf_op jit(solution)/shard_map/pallas_call | solution.py:52
  62.5 3.8 %collective-permute-start.7 = (bf16[320,1152]{1,0:T(8,128)(2,1)S(1)}, bf16[320,1152]{1,0:T(8,128)(2,1)S(1)}, u32[]{:S(2)}, u32[]{:S(2)}) collective-permute-start(bf16[320,1152]{1,0:T(8,128)(2,1)S(1)} %get-tuple-element.28), channel_id=1, source_target_pairs={{0,1},{1,0},{2,3},{3,2},{16,18},{17,19},{18,16},{19,17},{4,5},{5,4... | collective-permute-start | bytes 2211848 | tf_op jit(solution)/shard_map/ppermute | solution.py:35
  66.4 1.4 %shard_map.53 = (bf16[576,1152]{1,0:T(8,128)(2,1)S(1)}, bf16[144,1152]{1,0:T(8,128)(2,1)S(1)}, bf16[144,1152]{1,0:T(8,128)(2,1)S(1)}, bf16[144,1152]{1,0:T(8,128)(2,1)S(1)}, bf16[144,1152]{1,0:T(8,128)(2,1)S(1)}) custom-call(bf16[576,1152]{1,0:T(8,128)(2,1)S(1)} %get-tuple-element.29.slopes_ref, bf16[576,1152]{1,0:T(8,128)(2,1)S(1)} %bitcast.5), custom_call_target="tpu_custom_call" | custom-call | flops 764411904 | bytes 5308416 | tf_op jit(solution)/shard_map/pallas_call | solution.py:52
  67.8 1.9 %collective-permute-start.13 = (bf16[576,1152]{1,0:T(8,128)(2,1)S(1)}, bf16[576,1152]{1,0:T(8,128)(2,1)S(1)}, u32[]{:S(2)}, u32[]{:S(2)}) collective-permute-start(bf16[576,1152]{1,0:T(8,128)(2,1)S(1)} %get-tuple-element.34), channel_id=1, source_target_pairs={{16,0},{17,1},{18,2},{19,3},{20,4},{21,5},{22,6},{23,7},{24,8},{25... | collective-permute-start | bytes 3981320 | tf_op jit(solution)/shard_map/ppermute | solution.py:267
  69.8 0.7 collective-permute-start.10
  70.5 0.7 collective-permute-start.11
  71.2 0.7 collective-permute-start.9
  71.8 0.0 collective-permute-done.10.c
  71.9 0.0 collective-permute-done.11.d
  71.9 0.0 collective-permute-done.9.b
  71.9 0.2 shard_map.54
  72.0 1.3 %collective-permute-start.12 = (bf16[144,1152]{1,0:T(8,128)(2,1)S(1)}, bf16[144,1152]{1,0:T(8,128)(2,1)S(1)}, u32[]{:S(2)}, u32[]{:S(2)}) collective-permute-start(bf16[144,1152]{1,0:T(8,128)(2,1)S(1)} %shard_map.54), channel_id=1, source_target_pairs={{32,16},{64,48},{96,80},{128,112},{160,144},{192,176},{224,208},{2... | collective-permute-start | bytes 995336 | tf_op jit(solution)/shard_map/ppermute | solution.py:43
  73.3 9.2 %collective-permute-done.7.theirs.near = bf16[320,1152]{1,0:T(8,128)(2,1)S(1)} collective-permute-done((bf16[320,1152]{1,0:T(8,128)(2,1)S(1)}, bf16[320,1152]{1,0:T(8,128)(2,1)S(1)}, u32[]{:S(2)}, u32[]{:S(2)}) %collective-permute-start.7) | collective-permute-done | bytes 737312 | tf_op jit(solution)/shard_map/ppermute | solution.py:35
  82.5 0.1 shard_map.52
  82.6 5.9 %collective-permute-start.8 = (bf16[160,1152]{1,0:T(8,128)(2,1)S(1)}, bf16[160,1152]{1,0:T(8,128)(2,1)S(1)}, u32[]{:S(2)}, u32[]{:S(2)}) collective-permute-start(bf16[160,1152]{1,0:T(8,128)(2,1)S(1)} %shard_map.52), channel_id=1, source_target_pairs={{0,2},{1,3},{2,0},{3,1},{16,17},{17,16},{18,19},{19,18},{4,6},{5,7... | collective-permute-start | bytes 1105928 | tf_op jit(solution)/shard_map/ppermute | solution.py:35
  88.5 0.0 collective-permute-done.13.other
  88.5 1.4 %shard_map.55 = (bf16[144,1152]{1,0:T(8,128)(2,1)S(1)}, bf16[144,1152]{1,0:T(8,128)(2,1)S(1)}, bf16[144,1152]{1,0:T(8,128)(2,1)S(1)}, bf16[144,1152]{1,0:T(8,128)(2,1)S(1)}) custom-call(bf16[576,1152]{1,0:T(8,128)(2,1)S(1)} %get-tuple-element.29.slopes_ref, bf16[576,1152]{1,0:T(8,128)(2,1)S(1)} %bitcast.6, bf16[576,1152]{1,0:T(8,128)(2,1)S(1)} %collective-permute-done.13.other), custom_call_target="tpu_custom_call" | custom-call | flops 764411904 | bytes 5308416 | tf_op jit(solution)/shard_map/pallas_call | solution.py:52
  90.0 2.4 %collective-permute-start.14 = (bf16[144,1152]{1,0:T(8,128)(2,1)S(1)}, bf16[144,1152]{1,0:T(8,128)(2,1)S(1)}, u32[]{:S(2)}, u32[]{:S(2)}) collective-permute-start(bf16[144,1152]{1,0:T(8,128)(2,1)S(1)} %get-tuple-element.36), channel_id=1, source_target_pairs={{0,8},{4,12},{8,0},{12,4},{1,9},{5,13},{9,1},{13,5},{2,10},{6,14},... | collective-permute-start | bytes 995336 | tf_op jit(solution)/shard_map/ppermute | solution.py:27
  92.3 3.7 %collective-permute-start.15 = (bf16[144,1152]{1,0:T(8,128)(2,1)S(1)}, bf16[144,1152]{1,0:T(8,128)(2,1)S(1)}, u32[]{:S(2)}, u32[]{:S(2)}) collective-permute-start(bf16[144,1152]{1,0:T(8,128)(2,1)S(1)} %get-tuple-element.37), channel_id=1, source_target_pairs={{0,12},{4,0},{8,4},{12,8},{1,13},{5,1},{9,5},{13,9},{2,14},{6,2},{... | collective-permute-start | bytes 995336 | tf_op jit(solution)/shard_map/ppermute | solution.py:27
  96.0 1.9 %collective-permute-start.16 = (bf16[144,1152]{1,0:T(8,128)(2,1)S(1)}, bf16[144,1152]{1,0:T(8,128)(2,1)S(1)}, u32[]{:S(2)}, u32[]{:S(2)}) collective-permute-start(bf16[144,1152]{1,0:T(8,128)(2,1)S(1)} %get-tuple-element.38), channel_id=1, source_target_pairs={{0,4},{4,8},{8,12},{12,0},{1,5},{5,9},{9,13},{13,1},{2,6},{6,10},{... | collective-permute-start | bytes 995336 | tf_op jit(solution)/shard_map/ppermute | solution.py:27
  97.9 5.8 %collective-permute-done.12.home = bf16[144,1152]{1,0:T(8,128)(2,1)S(1)} collective-permute-done((bf16[144,1152]{1,0:T(8,128)(2,1)S(1)}, bf16[144,1152]{1,0:T(8,128)(2,1)S(1)}, u32[]{:S(2)}, u32[]{:S(2)}) %collective-permute-start.12) | collective-permute-done | bytes 331808 | tf_op jit(solution)/shard_map/ppermute | solution.py:43
  103.8 7.5 %collective-permute-done.8.far = bf16[160,1152]{1,0:T(8,128)(2,1)S(1)} collective-permute-done((bf16[160,1152]{1,0:T(8,128)(2,1)S(1)}, bf16[160,1152]{1,0:T(8,128)(2,1)S(1)}, u32[]{:S(2)}, u32[]{:S(2)}) %collective-permute-start.8) | collective-permute-done | bytes 368672 | tf_op jit(solution)/shard_map/ppermute | solution.py:35
  111.2 0.0 collective-permute-done.14.b
  111.2 0.0 collective-permute-done.15.c
  111.2 0.0 collective-permute-done.16.d
  111.2 0.0 copy-start.1
  111.3 0.1 shard_map.57.base
  111.3 0.9 copy-done.1
  112.2 0.0 copy-start.3
  112.2 1.2 %shard_map.58 = f32[144,1152]{1,0:T(8,128)} custom-call(bf16[144,1152]{1,0:T(8,128)(2,1)S(1)} %copy-done.1, f32[144,1152]{1,0:T(8,128)S(1)} %shard_map.57.base, bf16[144,1152]{1,0:T(8,128)(2,1)S(1)} %collective-permute-done.14.b, bf16[144,1152]{1,0:T(8,128)(2,1)S(1)} %collective-permute-done.15.c, bf16[144,1152]{1,0:T(8,128)(2,1)S(1)} %collective-permute-done.16.d), custom_call_target="tpu_custom_call" | custom-call | bytes 2654208 | tf_op jit(solution)/shard_map/pallas_call | solution.py:52
  113.5 0.0 copy-done.3
  113.5 1.2 %shard_map.56 = (f32[144,1152]{1,0:T(8,128)}, f32[1,144]{1,0:T(1,128)}) custom-call(bf16[144,1152]{1,0:T(8,128)(2,1)S(1)} %copy-done.3, bf16[320,1152]{1,0:T(8,128)(2,1)S(1)} %get-tuple-element.27.mine, bf16[320,1152]{1,0:T(8,128)(2,1)S(1)} %collective-permute-done.7.theirs.near, bf16[160,1152]{1,0:T(8,128)(2,1)S(1)} %collective-permute-done.8.far), custom_call_target="tpu_custom_call" | custom-call | bytes 2839104 | tf_op jit(solution)/shard_map/pallas_call | solution.py:52
Async XLA Ops:
  0.6 33.2 %collective-permute-start.3 = (bf16[144,1152]{1,0:T(8,128)(2,1)}, bf16[144,1152]{1,0:T(8,128)(2,1)S(1)}, u32[]{:S(2)}, u32[]{:S(2)}) collective-permute-start(bf16[144,1152]{1,0:T(8,128)(2,1)} %raw_ref.3), channel_id=1, source_target_pairs={{0,16},{16,32},{32,48},{48,64},{64,80},{80,96},{96,112},{112,128},... | collective-permute-start | bytes 995336 | tf_op jit(solution)/shard_map/ppermute | solution.py:27
  12.7 1.0 copy-start
  13.7 1.0 copy-start.2
  15.9 38.8 %all-to-all-start = ((bf16[4,144,1152]{2,1,0:T(8,128)(2,1)}), bf16[4,144,1152]{2,1,0:T(8,128)(2,1)S(1)}, u32[]{:S(2)}, u32[]{:S(2)}) async-start(bf16[4,144,1152]{2,1,0:T(8,128)(2,1)} %get-tuple-element.25), calls=%async_computation | async-start | bytes 2654208 | tf_op jit(solution)/shard_map/all_to_all | solution.py:254
  22.6 15.8 %collective-permute-start = (bf16[144,1152]{1,0:T(8,128)(2,1)S(1)}, bf16[144,1152]{1,0:T(8,128)(2,1)S(1)}, u32[]{:S(2)}, u32[]{:S(2)}) collective-permute-start(bf16[144,1152]{1,0:T(8,128)(2,1)S(1)} %get-tuple-element.26.refs_2_), channel_id=1, source_target_pairs={{0,8},{4,12},{8,0},{12,4},{1,9},{5,13},{9,1},{13,5},{2,10},{6,14},... | collective-permute-start | bytes 995336 | tf_op jit(solution)/shard_map/ppermute | solution.py:27
  27.3 20.2 %collective-permute-start.1 = (bf16[144,1152]{1,0:T(8,128)(2,1)S(1)}, bf16[144,1152]{1,0:T(8,128)(2,1)S(1)}, u32[]{:S(2)}, u32[]{:S(2)}) collective-permute-start(bf16[144,1152]{1,0:T(8,128)(2,1)S(1)} %get-tuple-element.26.refs_2_), channel_id=1, source_target_pairs={{0,4},{4,8},{8,12},{12,0},{1,5},{5,9},{9,13},{13,1},{2,6},{6,10},{... | collective-permute-start | bytes 995336 | tf_op jit(solution)/shard_map/ppermute | solution.py:27
  29.5 18.0 %collective-permute-start.2 = (bf16[144,1152]{1,0:T(8,128)(2,1)S(1)}, bf16[144,1152]{1,0:T(8,128)(2,1)S(1)}, u32[]{:S(2)}, u32[]{:S(2)}) collective-permute-start(bf16[144,1152]{1,0:T(8,128)(2,1)S(1)} %get-tuple-element.26.refs_2_), channel_id=1, source_target_pairs={{0,12},{4,0},{8,4},{12,8},{1,13},{5,1},{9,5},{13,9},{2,14},{6,2},{... | collective-permute-start | bytes 995336 | tf_op jit(solution)/shard_map/ppermute | solution.py:27
  34.0 15.9 %collective-permute-start.4 = (bf16[144,1152]{1,0:T(8,128)(2,1)S(1)}, bf16[144,1152]{1,0:T(8,128)(2,1)S(1)}, u32[]{:S(2)}, u32[]{:S(2)}) collective-permute-start(bf16[144,1152]{1,0:T(8,128)(2,1)S(1)} %shard_map.50.refs_6_), channel_id=1, source_target_pairs={{0,8},{4,12},{8,0},{12,4},{1,9},{5,13},{9,1},{13,5},{2,10},{6,14},... | collective-permute-start | bytes 995336 | tf_op jit(solution)/shard_map/ppermute | solution.py:27
  35.9 18.8 %collective-permute-start.5 = (bf16[144,1152]{1,0:T(8,128)(2,1)S(1)}, bf16[144,1152]{1,0:T(8,128)(2,1)}, u32[]{:S(2)}, u32[]{:S(2)}) collective-permute-start(bf16[144,1152]{1,0:T(8,128)(2,1)S(1)} %shard_map.50.refs_6_), channel_id=1, source_target_pairs={{0,4},{4,8},{8,12},{12,0},{1,5},{5,9},{9,13},{13,1},{2,6},{6,10},{... | collective-permute-start | bytes 995336 | tf_op jit(solution)/shard_map/ppermute | solution.py:27
  38.4 16.3 %collective-permute-start.6 = (bf16[144,1152]{1,0:T(8,128)(2,1)S(1)}, bf16[144,1152]{1,0:T(8,128)(2,1)}, u32[]{:S(2)}, u32[]{:S(2)}) collective-permute-start(bf16[144,1152]{1,0:T(8,128)(2,1)S(1)} %shard_map.50.refs_6_), channel_id=1, source_target_pairs={{0,12},{4,0},{8,4},{12,8},{1,13},{5,1},{9,5},{13,9},{2,14},{6,2},{... | collective-permute-start | bytes 995336 | tf_op jit(solution)/shard_map/ppermute | solution.py:27
  62.5 20.0 %collective-permute-start.7 = (bf16[320,1152]{1,0:T(8,128)(2,1)S(1)}, bf16[320,1152]{1,0:T(8,128)(2,1)S(1)}, u32[]{:S(2)}, u32[]{:S(2)}) collective-permute-start(bf16[320,1152]{1,0:T(8,128)(2,1)S(1)} %get-tuple-element.28), channel_id=1, source_target_pairs={{0,1},{1,0},{2,3},{3,2},{16,18},{17,19},{18,16},{19,17},{4,5},{5,4... | collective-permute-start | bytes 2211848 | tf_op jit(solution)/shard_map/ppermute | solution.py:35
  67.8 20.7 %collective-permute-start.13 = (bf16[576,1152]{1,0:T(8,128)(2,1)S(1)}, bf16[576,1152]{1,0:T(8,128)(2,1)S(1)}, u32[]{:S(2)}, u32[]{:S(2)}) collective-permute-start(bf16[576,1152]{1,0:T(8,128)(2,1)S(1)} %get-tuple-element.34), channel_id=1, source_target_pairs={{16,0},{17,1},{18,2},{19,3},{20,4},{21,5},{22,6},{23,7},{24,8},{25... | collective-permute-start | bytes 3981320 | tf_op jit(solution)/shard_map/ppermute | solution.py:267
  69.8 2.1 %collective-permute-start.10 = (bf16[144,1152]{1,0:T(8,128)(2,1)S(1)}, bf16[144,1152]{1,0:T(8,128)(2,1)S(1)}, u32[]{:S(2)}, u32[]{:S(2)}) collective-permute-start(bf16[144,1152]{1,0:T(8,128)(2,1)S(1)} %get-tuple-element.32), channel_id=1, source_target_pairs={{0,12},{4,0},{8,4},{12,8},{1,13},{5,1},{9,5},{13,9},{2,14},{6,2},{... | collective-permute-start | bytes 995336 | tf_op jit(solution)/shard_map/ppermute | solution.py:47
  70.5 1.4 %collective-permute-start.11 = (bf16[144,1152]{1,0:T(8,128)(2,1)S(1)}, bf16[144,1152]{1,0:T(8,128)(2,1)S(1)}, u32[]{:S(2)}, u32[]{:S(2)}) collective-permute-start(bf16[144,1152]{1,0:T(8,128)(2,1)S(1)} %get-tuple-element.33), channel_id=1, source_target_pairs={{0,4},{4,8},{8,12},{12,0},{1,5},{5,9},{9,13},{13,1},{2,6},{6,10},{... | collective-permute-start | bytes 995336 | tf_op jit(solution)/shard_map/ppermute | solution.py:47
  71.2 0.7 collective-permute-start.9
  72.0 31.7 %collective-permute-start.12 = (bf16[144,1152]{1,0:T(8,128)(2,1)S(1)}, bf16[144,1152]{1,0:T(8,128)(2,1)S(1)}, u32[]{:S(2)}, u32[]{:S(2)}) collective-permute-start(bf16[144,1152]{1,0:T(8,128)(2,1)S(1)} %shard_map.54), channel_id=1, source_target_pairs={{32,16},{64,48},{96,80},{128,112},{160,144},{192,176},{224,208},{2... | collective-permute-start | bytes 995336 | tf_op jit(solution)/shard_map/ppermute | solution.py:43
  82.6 28.6 %collective-permute-start.8 = (bf16[160,1152]{1,0:T(8,128)(2,1)S(1)}, bf16[160,1152]{1,0:T(8,128)(2,1)S(1)}, u32[]{:S(2)}, u32[]{:S(2)}) collective-permute-start(bf16[160,1152]{1,0:T(8,128)(2,1)S(1)} %shard_map.52), channel_id=1, source_target_pairs={{0,2},{1,3},{2,0},{3,1},{16,17},{17,16},{18,19},{19,18},{4,6},{5,7... | collective-permute-start | bytes 1105928 | tf_op jit(solution)/shard_map/ppermute | solution.py:35
  90.0 21.3 %collective-permute-start.14 = (bf16[144,1152]{1,0:T(8,128)(2,1)S(1)}, bf16[144,1152]{1,0:T(8,128)(2,1)S(1)}, u32[]{:S(2)}, u32[]{:S(2)}) collective-permute-start(bf16[144,1152]{1,0:T(8,128)(2,1)S(1)} %get-tuple-element.36), channel_id=1, source_target_pairs={{0,8},{4,12},{8,0},{12,4},{1,9},{5,13},{9,1},{13,5},{2,10},{6,14},... | collective-permute-start | bytes 995336 | tf_op jit(solution)/shard_map/ppermute | solution.py:27
  92.3 18.9 %collective-permute-start.15 = (bf16[144,1152]{1,0:T(8,128)(2,1)S(1)}, bf16[144,1152]{1,0:T(8,128)(2,1)S(1)}, u32[]{:S(2)}, u32[]{:S(2)}) collective-permute-start(bf16[144,1152]{1,0:T(8,128)(2,1)S(1)} %get-tuple-element.37), channel_id=1, source_target_pairs={{0,12},{4,0},{8,4},{12,8},{1,13},{5,1},{9,5},{13,9},{2,14},{6,2},{... | collective-permute-start | bytes 995336 | tf_op jit(solution)/shard_map/ppermute | solution.py:27
  96.0 15.2 %collective-permute-start.16 = (bf16[144,1152]{1,0:T(8,128)(2,1)S(1)}, bf16[144,1152]{1,0:T(8,128)(2,1)S(1)}, u32[]{:S(2)}, u32[]{:S(2)}) collective-permute-start(bf16[144,1152]{1,0:T(8,128)(2,1)S(1)} %get-tuple-element.38), channel_id=1, source_target_pairs={{0,4},{4,8},{8,12},{12,0},{1,5},{5,9},{9,13},{13,1},{2,6},{6,10},{... | collective-permute-start | bytes 995336 | tf_op jit(solution)/shard_map/ppermute | solution.py:27
  111.2 1.0 copy-start.1
  112.2 1.2 %copy-start.3 = (bf16[144,1152]{1,0:T(8,128)(2,1)S(1)}, bf16[144,1152]{1,0:T(8,128)(2,1)}, u32[]{:S(2)}) copy-start(bf16[144,1152]{1,0:T(8,128)(2,1)} %raw_ref.2) | copy-start | bytes 995332

commit v7 on v6

--- a/solution.py
+++ b/solution.py
@@ -18,7 +18,8 @@
 LANES = 128
 HOPS = (2, 1, 3)
 WEIGHT = 26_000_000_000
-HOME_WEIGHT = 4_000_000_000
+HOME_WEIGHT = 2_000_000_000
+END_WEIGHT = 3_000_000_000
 FAR_WEIGHT = 10_000_000_000
 
 
@@ -41,6 +42,14 @@
     if back:
         pairs = [(b, a) for a, b in pairs]
     return lax.ppermute(value, BLK, pairs)
+
+
+def turned(value, steps):
+    pairs = []
+    for core in range(CORES):
+        by = steps if core == 0 else -steps
+        pairs += [(core * NX + x, core * NX + (x + by) % NX) for x in range(NX)]
+    return lax.ppermute(value, ("core", "x"), pairs)
 
 
 def first_core(value, steps):
@@ -252,7 +261,9 @@
         low_kernel, [images, texts], [shape((NZ, own, features), BF16), unit], 8
     )
     img_all = lax.all_to_all(spread, "z", 0, 0).reshape(NZ * own, features)
-    now_slots = spread_x(txt_low)
+    after, before = turned(txt_low, 1), turned(txt_low, -1)
+    beyond = turned(after, 1)
+    now_slots = [txt_low, beyond, after, before]
     (moved_low,) = vmem_call(moved_kernel, [moved], [unit], 8, flops=WEIGHT)
     later_slots = spread_x(moved_low)
 
@@ -269,13 +280,13 @@
     (later,) = vmem_call(later_kernel, later_back, [unit], 8)
     home = next_group(later, True)
     parts = text_call(now_parts_kernel, [slopes, img_all, across], [unit] * NX)
-    now_back = [parts[0]] + [shifted(p, "x", -s) for p, s in zip(parts[1:], HOPS)]
-
-    back_far, home, now_back = lax.optimization_barrier((back_far, home, now_back))
+    now_back = [parts[0]] + [turned(p, -s) for p, s in zip(parts[1:], HOPS)]
+
     wide = shape((own, features), F32)
     image_grad, row_loss = vmem_call(
-        image_end_kernel, [images, keep, back_near, back_far], [wide, shape((1, own), F32)], 12
-    )
+        image_end_kernel, [images, keep, back_near, back_far], [wide, shape((1, own), F32)], 12, flops=END_WEIGHT
+    )
+    home, image_grad = lax.optimization_barrier((home, image_grad))
     (base,) = vmem_call(base_kernel, [now_back[0], home], [wide], 8, flops=HOME_WEIGHT)
     (text_grad,) = vmem_call(text_end_kernel, [texts, base] + now_back[1:], [wide], 12)
     return (row_loss.reshape(own), image_grad, text_grad)

time: 116 us -> 118 us (1.017)
  the two profiles are of different devices: /device:TPU:1 before, /device:TPU:127 now
where the time goes in v7:
time: 118 us; the launch traced here: 117 us
  starting transfers between devices  53.2 us (45%)
  waiting for transfers between devices  45.2 us (38%)
  Pallas kernels  14.9 us (13%)
  local copies, waits for them, and re-layouts  2.83 us (2%)
    ppermute x4, starting transfers between devices, shifted(): lax.ppermute(value, axis, [(i, (i + steps) % count) for i in range(count)])  19.6 us
    ppermute x1, waiting for transfers between devices, next_group(): return lax.ppermute(value, BLK, pairs)  17.3 us
    ppermute x6, starting transfers between devices, turned(): return lax.ppermute(value, ('core', 'x'), pairs)  16.1 us
    pallas_call x10, Pallas kernels, vmem_call(): pl.pallas_call(body, out_shape=list(outs), in_specs=[pl.BlockSpec(memory_...  14.9 us
    ppermute x2, waiting for transfers between devices, across_z(): return lax.ppermute(value, ('core', 'z'), pairs)  11.4 us
    ppermute x4, waiting for transfers between devices, shifted(): lax.ppermute(value, axis, [(i, (i + steps) % count) for i in range(count)])  9.93 us
    ppermute x2, starting transfers between devices, across_z(): return lax.ppermute(value, ('core', 'z'), pairs)  6.53 us
    all_to_all x1, starting transfers between devices, on_device(): img_all = lax.all_to_all(spread, 'z', 0, 0).reshape(NZ * own, features)  6.06 us
  transfers between devices with their start and end apart: 18, of which 6 were waited for; matrix products, arithmetic and copies ran while one was open for 0% of the time, Pallas kernels for 5%

profile of v7, /device:TPU:127, one launch (start us, length us, event | category | flops | bytes accessed | tf_op | source)
XLA Modules:
  0.0 117.1 jit_solution(14354149410724635385)
XLA Ops:
  0.6 11.2 %collective-permute-start.3 = (bf16[144,1152]{1,0:T(8,128)(2,1)}, bf16[144,1152]{1,0:T(8,128)(2,1)S(1)}, u32[]{:S(2)}, u32[]{:S(2)}) collective-permute-start(bf16[144,1152]{1,0:T(8,128)(2,1)} %raw_ref.3), channel_id=1, source_target_pairs={{0,16},{16,32},{32,48},{48,64},{64,80},{80,96},{96,112},{112,128},... | collective-permute-start | bytes 995336 | tf_op jit(solution)/shard_map/ppermute | solution.py:28
  11.8 0.0 copy-start
  11.8 1.0 copy-done
  12.8 0.0 copy-start.2
  12.8 1.0 copy-done.2
  13.8 1.3 %shard_map.49 = (bf16[4,144,1152]{2,1,0:T(8,128)(2,1)}, bf16[144,1152]{1,0:T(8,128)(2,1)S(1)}) custom-call(bf16[144,1152]{1,0:T(8,128)(2,1)S(1)} %copy-done.2, bf16[144,1152]{1,0:T(8,128)(2,1)S(1)} %copy-done), custom_call_target="tpu_custom_call" | custom-call | bytes 2322432 | tf_op jit(solution)/shard_map/pallas_call | solution.py:61
  15.1 6.1 %all-to-all-start = ((bf16[4,144,1152]{2,1,0:T(8,128)(2,1)}), bf16[4,144,1152]{2,1,0:T(8,128)(2,1)S(1)}, u32[]{:S(2)}, u32[]{:S(2)}) async-start(bf16[4,144,1152]{2,1,0:T(8,128)(2,1)} %get-tuple-element.21), calls=%async_computation | async-start | bytes 2654208 | tf_op jit(solution)/shard_map/all_to_all | solution.py:263
  21.2 2.1 %collective-permute-start.2 = (bf16[144,1152]{1,0:T(8,128)(2,1)S(1)}, bf16[144,1152]{1,0:T(8,128)(2,1)S(1)}, u32[]{:S(2)}, u32[]{:S(2)}) collective-permute-start(bf16[144,1152]{1,0:T(8,128)(2,1)S(1)} %get-tuple-element.22.refs_2_), channel_id=1, source_target_pairs={{0,12},{4,0},{8,4},{12,8},{16,20},{20,24},{24,28},{28,16},{1,13},{... | collective-permute-start | bytes 995336 | tf_op jit(solution)/shard_map/ppermute | solution.py:52
  23.3 3.2 %collective-permute-start = (bf16[144,1152]{1,0:T(8,128)(2,1)S(1)}, bf16[144,1152]{1,0:T(8,128)(2,1)S(1)}, u32[]{:S(2)}, u32[]{:S(2)}) collective-permute-start(bf16[144,1152]{1,0:T(8,128)(2,1)S(1)} %get-tuple-element.22.refs_2_), channel_id=1, source_target_pairs={{0,4},{4,8},{8,12},{12,0},{16,28},{20,16},{24,20},{28,24},{1,5},{5... | collective-permute-start | bytes 995336 | tf_op jit(solution)/shard_map/ppermute | solution.py:52
  26.4 0.0 collective-permute-done.3.txt_ref
  26.5 0.2 shard_map.50.refs_6_
  26.6 2.5 %collective-permute-start.6 = (bf16[144,1152]{1,0:T(8,128)(2,1)S(1)}, bf16[144,1152]{1,0:T(8,128)(2,1)S(1)}, u32[]{:S(2)}, u32[]{:S(2)}) collective-permute-start(bf16[144,1152]{1,0:T(8,128)(2,1)S(1)} %shard_map.50.refs_6_), channel_id=1, source_target_pairs={{0,12},{4,0},{8,4},{12,8},{1,13},{5,1},{9,5},{13,9},{2,14},{6,2},{... | collective-permute-start | bytes 995336 | tf_op jit(solution)/shard_map/ppermute | solution.py:28
  29.1 4.0 %collective-permute-start.5 = (bf16[144,1152]{1,0:T(8,128)(2,1)S(1)}, bf16[144,1152]{1,0:T(8,128)(2,1)S(1)}, u32[]{:S(2)}, u32[]{:S(2)}) collective-permute-start(bf16[144,1152]{1,0:T(8,128)(2,1)S(1)} %shard_map.50.refs_6_), channel_id=1, source_target_pairs={{0,4},{4,8},{8,12},{12,0},{1,5},{5,9},{9,13},{13,1},{2,6},{6,10},{... | collective-permute-start | bytes 995336 | tf_op jit(solution)/shard_map/ppermute | solution.py:28
  33.1 1.9 %collective-permute-start.4 = (bf16[144,1152]{1,0:T(8,128)(2,1)S(1)}, bf16[144,1152]{1,0:T(8,128)(2,1)}, u32[]{:S(2)}, u32[]{:S(2)}) collective-permute-start(bf16[144,1152]{1,0:T(8,128)(2,1)S(1)} %shard_map.50.refs_6_), channel_id=1, source_target_pairs={{0,8},{4,12},{8,0},{12,4},{1,9},{5,13},{9,1},{13,5},{2,10},{6,14},... | collective-permute-start | bytes 995336 | tf_op jit(solution)/shard_map/ppermute | solution.py:28
  35.1 0.0 collective-permute-done.refs_4_
  35.1 2.7 %collective-permute-start.1 = (bf16[144,1152]{1,0:T(8,128)(2,1)S(1)}, bf16[144,1152]{1,0:T(8,128)(2,1)}, u32[]{:S(2)}, u32[]{:S(2)}) collective-permute-start(bf16[144,1152]{1,0:T(8,128)(2,1)S(1)} %collective-permute-done.refs_4_), channel_id=1, source_target_pairs={{0,4},{4,8},{8,12},{12,0},{16,28},{20,16},{24,20},{28,24},{1,5},{5... | collective-permute-start | bytes 995336 | tf_op jit(solution)/shard_map/ppermute | solution.py:52
  37.8 0.1 pad_add_fusion.refs_0_
  37.8 0.0 collective-permute-done.2.refs_5_
  37.8 8.7 %collective-permute-done.6.refs_9_ = bf16[144,1152]{1,0:T(8,128)(2,1)S(1)} collective-permute-done((bf16[144,1152]{1,0:T(8,128)(2,1)S(1)}, bf16[144,1152]{1,0:T(8,128)(2,1)S(1)}, u32[]{:S(2)}, u32[]{:S(2)}) %collective-permute-start.6) | collective-permute-done | bytes 331808 | tf_op jit(solution)/shard_map/ppermute | solution.py:28
  46.6 1.2 %collective-permute-done.5.refs_8_ = bf16[144,1152]{1,0:T(8,128)(2,1)S(1)} collective-permute-done((bf16[144,1152]{1,0:T(8,128)(2,1)S(1)}, bf16[144,1152]{1,0:T(8,128)(2,1)S(1)}, u32[]{:S(2)}, u32[]{:S(2)}) %collective-permute-start.5) | collective-permute-done | bytes 331808 | tf_op jit(solution)/shard_map/ppermute | solution.py:28
  47.8 0.0 collective-permute-done.4.refs_7_
  47.8 2.4 %collective-permute-done.1.refs_3_ = bf16[144,1152]{1,0:T(8,128)(2,1)} collective-permute-done((bf16[144,1152]{1,0:T(8,128)(2,1)S(1)}, bf16[144,1152]{1,0:T(8,128)(2,1)}, u32[]{:S(2)}, u32[]{:S(2)}) %collective-permute-start.1) | collective-permute-done | bytes 331808 | tf_op jit(solution)/shard_map/ppermute | solution.py:52
  50.2 4.2 %all-to-all-done = bf16[4,144,1152]{2,1,0:T(8,128)(2,1)S(1)} async-done(((bf16[4,144,1152]{2,1,0:T(8,128)(2,1)}), bf16[4,144,1152]{2,1,0:T(8,128)(2,1)S(1)}, u32[]{:S(2)}, u32[]{:S(2)}) %all-to-all-start) | async-done | bytes 1327136 | tf_op jit(solution)/shard_map/all_to_all | solution.py:263
  54.4 7.8 %shard_map.51 = (bf16[576,1152]{1,0:T(8,128)(2,1)S(1)}, bf16[320,1152]{1,0:T(8,128)(2,1)S(1)}, bf16[320,1152]{1,0:T(8,128)(2,1)S(1)}) custom-call(s32[2]{0:T(128)S(1)} %pad_add_fusion.refs_0_, bf16[576,1152]{1,0:T(8,128)(2,1)S(1)} %bitcast.4, bf16[144,1152]{1,0:T(8,128)(2,1)S(1)} %get-tuple-element.22.refs_2_, ...), custom_call_target="tpu_custom_call" | custom-call | flops 3057647616 | bytes 6782984 | tf_op jit(solution)/shard_map/pallas_call | solution.py:61
  62.2 4.6 %collective-permute-start.7 = (bf16[320,1152]{1,0:T(8,128)(2,1)S(1)}, bf16[320,1152]{1,0:T(8,128)(2,1)S(1)}, u32[]{:S(2)}, u32[]{:S(2)}) collective-permute-start(bf16[320,1152]{1,0:T(8,128)(2,1)S(1)} %get-tuple-element.24), channel_id=1, source_target_pairs={{0,1},{1,0},{2,3},{3,2},{16,18},{17,19},{18,16},{19,17},{4,5},{5,4... | collective-permute-start | bytes 2211848 | tf_op jit(solution)/shard_map/ppermute | solution.py:36
  66.8 1.4 %shard_map.54 = (bf16[576,1152]{1,0:T(8,128)(2,1)S(1)}, bf16[144,1152]{1,0:T(8,128)(2,1)S(1)}, bf16[144,1152]{1,0:T(8,128)(2,1)S(1)}, bf16[144,1152]{1,0:T(8,128)(2,1)S(1)}, bf16[144,1152]{1,0:T(8,128)(2,1)S(1)}) custom-call(bf16[576,1152]{1,0:T(8,128)(2,1)S(1)} %get-tuple-element.26.slopes_ref, bf16[576,1152]{1,0:T(8,128)(2,1)S(1)} %bitcast.5), custom_call_target="tpu_custom_call" | custom-call | flops 764411904 | bytes 5308416 | tf_op jit(solution)/shard_map/pallas_call | solution.py:61
  68.3 1.4 %collective-permute-start.13 = (bf16[576,1152]{1,0:T(8,128)(2,1)S(1)}, bf16[576,1152]{1,0:T(8,128)(2,1)S(1)}, u32[]{:S(2)}, u32[]{:S(2)}) collective-permute-start(bf16[576,1152]{1,0:T(8,128)(2,1)S(1)} %get-tuple-element.33), channel_id=1, source_target_pairs={{16,0},{17,1},{18,2},{19,3},{20,4},{21,5},{22,6},{23,7},{24,8},{25... | collective-permute-start | bytes 3981320 | tf_op jit(solution)/shard_map/ppermute | solution.py:278
  69.7 0.7 collective-permute-start.9
  70.3 0.7 collective-permute-start.10
  71.0 0.7 collective-permute-start.11
  71.7 11.4 %collective-permute-done.7.theirs.near = bf16[320,1152]{1,0:T(8,128)(2,1)S(1)} collective-permute-done((bf16[320,1152]{1,0:T(8,128)(2,1)S(1)}, bf16[320,1152]{1,0:T(8,128)(2,1)S(1)}, u32[]{:S(2)}, u32[]{:S(2)}) %collective-permute-start.7) | collective-permute-done | bytes 737312 | tf_op jit(solution)/shard_map/ppermute | solution.py:36
  83.1 0.1 shard_map.52
  83.2 1.9 %collective-permute-start.8 = (bf16[160,1152]{1,0:T(8,128)(2,1)S(1)}, bf16[160,1152]{1,0:T(8,128)(2,1)S(1)}, u32[]{:S(2)}, u32[]{:S(2)}) collective-permute-start(bf16[160,1152]{1,0:T(8,128)(2,1)S(1)} %shard_map.52), channel_id=1, source_target_pairs={{0,2},{1,3},{2,0},{3,1},{16,17},{17,16},{18,19},{19,18},{4,6},{5,7... | collective-permute-start | bytes 1105928 | tf_op jit(solution)/shard_map/ppermute | solution.py:36
  85.1 0.0 collective-permute-done.9.b
  85.1 0.0 collective-permute-done.10.c
  85.2 0.0 collective-permute-done.11.d
  85.2 0.2 shard_map.55
  85.3 0.0 copy-start.3
  85.4 1.4 %collective-permute-start.12 = (bf16[144,1152]{1,0:T(8,128)(2,1)S(1)}, bf16[144,1152]{1,0:T(8,128)(2,1)S(1)}, u32[]{:S(2)}, u32[]{:S(2)}) collective-permute-start(bf16[144,1152]{1,0:T(8,128)(2,1)S(1)} %shard_map.55), channel_id=1, source_target_pairs={{32,16},{64,48},{96,80},{128,112},{160,144},{192,176},{224,208},{2... | collective-permute-start | bytes 995336 | tf_op jit(solution)/shard_map/ppermute | solution.py:44
  86.8 0.0 collective-permute-done.13.other
  86.8 1.4 %shard_map.56 = (bf16[144,1152]{1,0:T(8,128)(2,1)S(1)}, bf16[144,1152]{1,0:T(8,128)(2,1)S(1)}, bf16[144,1152]{1,0:T(8,128)(2,1)S(1)}, bf16[144,1152]{1,0:T(8,128)(2,1)S(1)}) custom-call(bf16[576,1152]{1,0:T(8,128)(2,1)S(1)} %get-tuple-element.26.slopes_ref, bf16[576,1152]{1,0:T(8,128)(2,1)S(1)} %bitcast.6, bf16[576,1152]{1,0:T(8,128)(2,1)S(1)} %collective-permute-done.13.other), custom_call_target="tpu_custom_call" | custom-call | flops 764411904 | bytes 5308416 | tf_op jit(solution)/shard_map/pallas_call | solution.py:61
  88.2 2.2 %collective-permute-start.14 = (bf16[144,1152]{1,0:T(8,128)(2,1)S(1)}, bf16[144,1152]{1,0:T(8,128)(2,1)S(1)}, u32[]{:S(2)}, u32[]{:S(2)}) collective-permute-start(bf16[144,1152]{1,0:T(8,128)(2,1)S(1)} %get-tuple-element.36), channel_id=1, source_target_pairs={{0,8},{4,12},{8,0},{12,4},{16,24},{20,28},{24,16},{28,20},{1,9},{5... | collective-permute-start | bytes 995336 | tf_op jit(solution)/shard_map/ppermute | solution.py:52
  90.4 4.1 %collective-permute-start.15 = (bf16[144,1152]{1,0:T(8,128)(2,1)S(1)}, bf16[144,1152]{1,0:T(8,128)(2,1)S(1)}, u32[]{:S(2)}, u32[]{:S(2)}) collective-permute-start(bf16[144,1152]{1,0:T(8,128)(2,1)S(1)} %get-tuple-element.37), channel_id=1, source_target_pairs={{0,12},{4,0},{8,4},{12,8},{16,20},{20,24},{24,28},{28,16},{1,13},{... | collective-permute-start | bytes 995336 | tf_op jit(solution)/shard_map/ppermute | solution.py:52
  94.5 1.9 %collective-permute-start.16 = (bf16[144,1152]{1,0:T(8,128)(2,1)S(1)}, bf16[144,1152]{1,0:T(8,128)(2,1)S(1)}, u32[]{:S(2)}, u32[]{:S(2)}) collective-permute-start(bf16[144,1152]{1,0:T(8,128)(2,1)S(1)} %get-tuple-element.38), channel_id=1, source_target_pairs={{0,4},{4,8},{8,12},{12,0},{16,28},{20,16},{24,20},{28,24},{1,5},{5... | collective-permute-start | bytes 995336 | tf_op jit(solution)/shard_map/ppermute | solution.py:52
  96.5 0.0 collective-permute-done.8.far
  96.5 0.0 copy-done.3
  96.5 1.2 %shard_map.53 = (f32[144,1152]{1,0:T(8,128)}, f32[1,144]{1,0:T(1,128)}) custom-call(bf16[144,1152]{1,0:T(8,128)(2,1)S(1)} %copy-done.3, bf16[320,1152]{1,0:T(8,128)(2,1)S(1)} %get-tuple-element.23.mine, bf16[320,1152]{1,0:T(8,128)(2,1)S(1)} %collective-permute-done.7.theirs.near, bf16[160,1152]{1,0:T(8,128)(2,1)S(1)} %collective-permute-done.8.far), custom_call_target="tpu_custom_call" | custom-call | flops 3000000000 | bytes 2839104 | tf_op jit(solution)/shard_map/pallas_call | solution.py:61
  97.7 17.3 %collective-permute-done.12.home = bf16[144,1152]{1,0:T(8,128)(2,1)S(1)} collective-permute-done((bf16[144,1152]{1,0:T(8,128)(2,1)S(1)}, bf16[144,1152]{1,0:T(8,128)(2,1)S(1)}, u32[]{:S(2)}, u32[]{:S(2)}) %collective-permute-start.12) | collective-permute-done | bytes 331808 | tf_op jit(solution)/shard_map/ppermute | solution.py:44
  114.9 0.0 copy-start.1
  114.9 0.1 shard_map.57.base
  115.0 0.0 collective-permute-done.14.b
  115.0 0.0 collective-permute-done.15.c
  115.0 0.0 collective-permute-done.16.d
  115.0 0.9 copy-done.1
  115.9 1.2 %shard_map.58 = f32[144,1152]{1,0:T(8,128)} custom-call(bf16[144,1152]{1,0:T(8,128)(2,1)S(1)} %copy-done.1, f32[144,1152]{1,0:T(8,128)S(1)} %shard_map.57.base, bf16[144,1152]{1,0:T(8,128)(2,1)S(1)} %collective-permute-done.14.b, bf16[144,1152]{1,0:T(8,128)(2,1)S(1)} %collective-permute-done.15.c, bf16[144,1152]{1,0:T(8,128)(2,1)S(1)} %collective-permute-done.16.d), custom_call_target="tpu_custom_call" | custom-call | bytes 2654208 | tf_op jit(solution)/shard_map/pallas_call | solution.py:61
Async XLA Ops:
  0.6 25.8 %collective-permute-start.3 = (bf16[144,1152]{1,0:T(8,128)(2,1)}, bf16[144,1152]{1,0:T(8,128)(2,1)S(1)}, u32[]{:S(2)}, u32[]{:S(2)}) collective-permute-start(bf16[144,1152]{1,0:T(8,128)(2,1)} %raw_ref.3), channel_id=1, source_target_pairs={{0,16},{16,32},{32,48},{48,64},{64,80},{80,96},{96,112},{112,128},... | collective-permute-start | bytes 995336 | tf_op jit(solution)/shard_map/ppermute | solution.py:28
  11.8 1.0 copy-start
  12.8 1.0 copy-start.2
  15.1 39.3 %all-to-all-start = ((bf16[4,144,1152]{2,1,0:T(8,128)(2,1)}), bf16[4,144,1152]{2,1,0:T(8,128)(2,1)S(1)}, u32[]{:S(2)}, u32[]{:S(2)}) async-start(bf16[4,144,1152]{2,1,0:T(8,128)(2,1)} %get-tuple-element.21), calls=%async_computation | async-start | bytes 2654208 | tf_op jit(solution)/shard_map/all_to_all | solution.py:263
  21.2 16.7 %collective-permute-start.2 = (bf16[144,1152]{1,0:T(8,128)(2,1)S(1)}, bf16[144,1152]{1,0:T(8,128)(2,1)S(1)}, u32[]{:S(2)}, u32[]{:S(2)}) collective-permute-start(bf16[144,1152]{1,0:T(8,128)(2,1)S(1)} %get-tuple-element.22.refs_2_), channel_id=1, source_target_pairs={{0,12},{4,0},{8,4},{12,8},{16,20},{20,24},{24,28},{28,16},{1,13},{... | collective-permute-start | bytes 995336 | tf_op jit(solution)/shard_map/ppermute | solution.py:52
  23.3 11.8 %collective-permute-start = (bf16[144,1152]{1,0:T(8,128)(2,1)S(1)}, bf16[144,1152]{1,0:T(8,128)(2,1)S(1)}, u32[]{:S(2)}, u32[]{:S(2)}) collective-permute-start(bf16[144,1152]{1,0:T(8,128)(2,1)S(1)} %get-tuple-element.22.refs_2_), channel_id=1, source_target_pairs={{0,4},{4,8},{8,12},{12,0},{16,28},{20,16},{24,20},{28,24},{1,5},{5... | collective-permute-start | bytes 995336 | tf_op jit(solution)/shard_map/ppermute | solution.py:52
  26.6 19.9 %collective-permute-start.6 = (bf16[144,1152]{1,0:T(8,128)(2,1)S(1)}, bf16[144,1152]{1,0:T(8,128)(2,1)S(1)}, u32[]{:S(2)}, u32[]{:S(2)}) collective-permute-start(bf16[144,1152]{1,0:T(8,128)(2,1)S(1)} %shard_map.50.refs_6_), channel_id=1, source_target_pairs={{0,12},{4,0},{8,4},{12,8},{1,13},{5,1},{9,5},{13,9},{2,14},{6,2},{... | collective-permute-start | bytes 995336 | tf_op jit(solution)/shard_map/ppermute | solution.py:28
  29.1 18.7 %collective-permute-start.5 = (bf16[144,1152]{1,0:T(8,128)(2,1)S(1)}, bf16[144,1152]{1,0:T(8,128)(2,1)S(1)}, u32[]{:S(2)}, u32[]{:S(2)}) collective-permute-start(bf16[144,1152]{1,0:T(8,128)(2,1)S(1)} %shard_map.50.refs_6_), channel_id=1, source_target_pairs={{0,4},{4,8},{8,12},{12,0},{1,5},{5,9},{9,13},{13,1},{2,6},{6,10},{... | collective-permute-start | bytes 995336 | tf_op jit(solution)/shard_map/ppermute | solution.py:28
  33.1 14.6 %collective-permute-start.4 = (bf16[144,1152]{1,0:T(8,128)(2,1)S(1)}, bf16[144,1152]{1,0:T(8,128)(2,1)}, u32[]{:S(2)}, u32[]{:S(2)}) collective-permute-start(bf16[144,1152]{1,0:T(8,128)(2,1)S(1)} %shard_map.50.refs_6_), channel_id=1, source_target_pairs={{0,8},{4,12},{8,0},{12,4},{1,9},{5,13},{9,1},{13,5},{2,10},{6,14},... | collective-permute-start | bytes 995336 | tf_op jit(solution)/shard_map/ppermute | solution.py:28
  35.1 15.1 %collective-permute-start.1 = (bf16[144,1152]{1,0:T(8,128)(2,1)S(1)}, bf16[144,1152]{1,0:T(8,128)(2,1)}, u32[]{:S(2)}, u32[]{:S(2)}) collective-permute-start(bf16[144,1152]{1,0:T(8,128)(2,1)S(1)} %collective-permute-done.refs_4_), channel_id=1, source_target_pairs={{0,4},{4,8},{8,12},{12,0},{16,28},{20,16},{24,20},{28,24},{1,5},{5... | collective-permute-start | bytes 995336 | tf_op jit(solution)/shard_map/ppermute | solution.py:52
  62.2 20.9 %collective-permute-start.7 = (bf16[320,1152]{1,0:T(8,128)(2,1)S(1)}, bf16[320,1152]{1,0:T(8,128)(2,1)S(1)}, u32[]{:S(2)}, u32[]{:S(2)}) collective-permute-start(bf16[320,1152]{1,0:T(8,128)(2,1)S(1)} %get-tuple-element.24), channel_id=1, source_target_pairs={{0,1},{1,0},{2,3},{3,2},{16,18},{17,19},{18,16},{19,17},{4,5},{5,4... | collective-permute-start | bytes 2211848 | tf_op jit(solution)/shard_map/ppermute | solution.py:36
  68.3 18.5 %collective-permute-start.13 = (bf16[576,1152]{1,0:T(8,128)(2,1)S(1)}, bf16[576,1152]{1,0:T(8,128)(2,1)S(1)}, u32[]{:S(2)}, u32[]{:S(2)}) collective-permute-start(bf16[576,1152]{1,0:T(8,128)(2,1)S(1)} %get-tuple-element.33), channel_id=1, source_target_pairs={{16,0},{17,1},{18,2},{19,3},{20,4},{21,5},{22,6},{23,7},{24,8},{25... | collective-permute-start | bytes 3981320 | tf_op jit(solution)/shard_map/ppermute | solution.py:278
  69.7 15.5 %collective-permute-start.9 = (bf16[144,1152]{1,0:T(8,128)(2,1)S(1)}, bf16[144,1152]{1,0:T(8,128)(2,1)S(1)}, u32[]{:S(2)}, u32[]{:S(2)}) collective-permute-start(bf16[144,1152]{1,0:T(8,128)(2,1)S(1)} %get-tuple-element.28), channel_id=1, source_target_pairs={{0,8},{4,12},{8,0},{12,4},{1,9},{5,13},{9,1},{13,5},{2,10},{6,14},... | collective-permute-start | bytes 995336 | tf_op jit(solution)/shard_map/ppermute | solution.py:56
  70.3 14.8 %collective-permute-start.10 = (bf16[144,1152]{1,0:T(8,128)(2,1)S(1)}, bf16[144,1152]{1,0:T(8,128)(2,1)S(1)}, u32[]{:S(2)}, u32[]{:S(2)}) collective-permute-start(bf16[144,1152]{1,0:T(8,128)(2,1)S(1)} %get-tuple-element.29), channel_id=1, source_target_pairs={{0,12},{4,0},{8,4},{12,8},{1,13},{5,1},{9,5},{13,9},{2,14},{6,2},{... | collective-permute-start | bytes 995336 | tf_op jit(solution)/shard_map/ppermute | solution.py:56
  71.0 14.1 %collective-permute-start.11 = (bf16[144,1152]{1,0:T(8,128)(2,1)S(1)}, bf16[144,1152]{1,0:T(8,128)(2,1)S(1)}, u32[]{:S(2)}, u32[]{:S(2)}) collective-permute-start(bf16[144,1152]{1,0:T(8,128)(2,1)S(1)} %get-tuple-element.30), channel_id=1, source_target_pairs={{0,4},{4,8},{8,12},{12,0},{1,5},{5,9},{9,13},{13,1},{2,6},{6,10},{... | collective-permute-start | bytes 995336 | tf_op jit(solution)/shard_map/ppermute | solution.py:56
  83.2 13.3 %collective-permute-start.8 = (bf16[160,1152]{1,0:T(8,128)(2,1)S(1)}, bf16[160,1152]{1,0:T(8,128)(2,1)S(1)}, u32[]{:S(2)}, u32[]{:S(2)}) collective-permute-start(bf16[160,1152]{1,0:T(8,128)(2,1)S(1)} %shard_map.52), channel_id=1, source_target_pairs={{0,2},{1,3},{2,0},{3,1},{16,17},{17,16},{18,19},{19,18},{4,6},{5,7... | collective-permute-start | bytes 1105928 | tf_op jit(solution)/shard_map/ppermute | solution.py:36
  85.3 11.1 %copy-start.3 = (bf16[144,1152]{1,0:T(8,128)(2,1)S(1)}, bf16[144,1152]{1,0:T(8,128)(2,1)}, u32[]{:S(2)}) copy-start(bf16[144,1152]{1,0:T(8,128)(2,1)} %raw_ref.2) | copy-start | bytes 995332
  85.4 29.6 %collective-permute-start.12 = (bf16[144,1152]{1,0:T(8,128)(2,1)S(1)}, bf16[144,1152]{1,0:T(8,128)(2,1)S(1)}, u32[]{:S(2)}, u32[]{:S(2)}) collective-permute-start(bf16[144,1152]{1,0:T(8,128)(2,1)S(1)} %shard_map.55), channel_id=1, source_target_pairs={{32,16},{64,48},{96,80},{128,112},{160,144},{192,176},{224,208},{2... | collective-permute-start | bytes 995336 | tf_op jit(solution)/shard_map/ppermute | solution.py:44
  88.2 26.8 %collective-permute-start.14 = (bf16[144,1152]{1,0:T(8,128)(2,1)S(1)}, bf16[144,1152]{1,0:T(8,128)(2,1)S(1)}, u32[]{:S(2)}, u32[]{:S(2)}) collective-permute-start(bf16[144,1152]{1,0:T(8,128)(2,1)S(1)} %get-tuple-element.36), channel_id=1, source_target_pairs={{0,8},{4,12},{8,0},{12,4},{16,24},{20,28},{24,16},{28,20},{1,9},{5... | collective-permute-start | bytes 995336 | tf_op jit(solution)/shard_map/ppermute | solution.py:52
  90.4 24.6 %collective-permute-start.15 = (bf16[144,1152]{1,0:T(8,128)(2,1)S(1)}, bf16[144,1152]{1,0:T(8,128)(2,1)S(1)}, u32[]{:S(2)}, u32[]{:S(2)}) collective-permute-start(bf16[144,1152]{1,0:T(8,128)(2,1)S(1)} %get-tuple-element.37), channel_id=1, source_target_pairs={{0,12},{4,0},{8,4},{12,8},{16,20},{20,24},{24,28},{28,16},{1,13},{... | collective-permute-start | bytes 995336 | tf_op jit(solution)/shard_map/ppermute | solution.py:52
  94.5 20.5 %collective-permute-start.16 = (bf16[144,1152]{1,0:T(8,128)(2,1)S(1)}, bf16[144,1152]{1,0:T(8,128)(2,1)S(1)}, u32[]{:S(2)}, u32[]{:S(2)}) collective-permute-start(bf16[144,1152]{1,0:T(8,128)(2,1)S(1)} %get-tuple-element.38), channel_id=1, source_target_pairs={{0,4},{4,8},{8,12},{12,0},{16,28},{20,16},{24,20},{28,24},{1,5},{5... | collective-permute-start | bytes 995336 | tf_op jit(solution)/shard_map/ppermute | solution.py:52
  114.9 1.0 copy-start.1

commit v8 on v6

--- a/solution.py
+++ b/solution.py
@@ -16,6 +16,7 @@
 LOSS_ROWS = 16
 CHUNK = 16
 LANES = 128
+GROUP = 384
 HOPS = (2, 1, 3)
 WEIGHT = 26_000_000_000
 HOME_WEIGHT = 4_000_000_000
@@ -101,21 +102,23 @@
 
     def chunk(i, paired):
         rows = pl.ds(pl.multiple_of(i * CHUNK, CHUNK), CHUNK)
-        logits = scores[rows, :] * SCALE + SHIFT
-        if paired:
-            row = lax.broadcasted_iota(jnp.int32, logits.shape, 0) + (i - first) * CHUNK
-            col = lax.broadcasted_iota(jnp.int32, logits.shape, 1)
-            match = row == col
-            logits = jnp.where(match, -logits, logits)
-        grown = jnp.exp(logits)
-        losses = jnp.log1p(grown)
-        slopes = SCALE * grown / (1.0 + grown)
-        if paired:
-            slopes = jnp.where(match, -slopes, slopes)
-        slopes_ref[rows, :] = slopes.astype(BF16)
-        total = losses[:, 0:LANES]
-        for c in range(LANES, width, LANES):
-            total = total + losses[:, c : c + LANES]
+        total = jnp.zeros((CHUNK, LANES), F32)
+        for c in range(0, width, GROUP):
+            logits = scores[rows, c : c + GROUP] * SCALE + SHIFT
+            masked = paired and c == 0
+            if masked:
+                row = lax.broadcasted_iota(jnp.int32, logits.shape, 0) + (i - first) * CHUNK
+                col = lax.broadcasted_iota(jnp.int32, logits.shape, 1)
+                match = row == col
+                logits = jnp.where(match, -logits, logits)
+            grown = jnp.exp(logits)
+            losses = jnp.log1p(grown)
+            slopes = SCALE * grown / (1.0 + grown)
+            if masked:
+                slopes = jnp.where(match, -slopes, slopes)
+            slopes_ref[rows, c : c + GROUP] = slopes.astype(BF16)
+            for at in range(0, GROUP, LANES):
+                total = total + losses[:, at : at + LANES]
         lanes_ref[rows, :] = total
 
     @pl.loop(0, first)

time: 116 us -> 116 us (level)
  no operation moved by 1% of the time
where the time goes in v8:
time: 116 us; the launch traced here: 115 us
  starting transfers between devices  61.2 us (53%)
  waiting for transfers between devices  34.7 us (30%)
  Pallas kernels  14.9 us (13%)
  local copies, waits for them, and re-layouts  2.85 us (2%)
    ppermute x10, starting transfers between devices, shifted(): lax.ppermute(value, axis, [(i, (i + steps) % count) for i in range(count)])  39.5 us
    ppermute x2, waiting for transfers between devices, across_z(): return lax.ppermute(value, ('core', 'z'), pairs)  16.7 us
    pallas_call x10, Pallas kernels, vmem_call(): pl.pallas_call(body, out_shape=list(outs), in_specs=[pl.BlockSpec(memory_...  14.9 us
    ppermute x10, waiting for transfers between devices, shifted(): lax.ppermute(value, axis, [(i, (i + steps) % count) for i in range(count)])  12.2 us
    ppermute x2, starting transfers between devices, across_z(): return lax.ppermute(value, ('core', 'z'), pairs)  9.73 us
    all_to_all x1, starting transfers between devices, on_device(): img_all = lax.all_to_all(spread, 'z', 0, 0).reshape(NZ * own, features)  6.68 us
    ppermute x1, waiting for transfers between devices, next_group(): return lax.ppermute(value, BLK, pairs)  5.81 us
    unnamed x8, local copies, waits for them, and re-layouts  2.85 us
  transfers between devices with their start and end apart: 18, of which 6 were waited for; matrix products, arithmetic and copies ran while one was open for 0% of the time, Pallas kernels for 4%

profile of v8, /device:TPU:1, one launch (start us, length us, event | category | flops | bytes accessed | tf_op | source)
XLA Modules:
  0.0 114.6 jit_solution(10107426422772158593)
XLA Ops:
  0.6 12.0 %collective-permute-start.3 = (bf16[144,1152]{1,0:T(8,128)(2,1)}, bf16[144,1152]{1,0:T(8,128)(2,1)S(1)}, u32[]{:S(2)}, u32[]{:S(2)}) collective-permute-start(bf16[144,1152]{1,0:T(8,128)(2,1)} %raw_ref.3), channel_id=1, source_target_pairs={{0,16},{16,32},{32,48},{48,64},{64,80},{80,96},{96,112},{112,128},... | collective-permute-start | bytes 995336 | tf_op jit(solution)/shard_map/ppermute | solution.py:28
  12.7 0.0 copy-start
  12.7 1.0 copy-done
  13.7 0.0 copy-start.2
  13.7 1.0 copy-done.2
  14.6 1.3 %shard_map.49 = (bf16[4,144,1152]{2,1,0:T(8,128)(2,1)}, bf16[144,1152]{1,0:T(8,128)(2,1)S(1)}) custom-call(bf16[144,1152]{1,0:T(8,128)(2,1)S(1)} %copy-done.2, bf16[144,1152]{1,0:T(8,128)(2,1)S(1)} %copy-done), custom_call_target="tpu_custom_call" | custom-call | bytes 2322432 | tf_op jit(solution)/shard_map/pallas_call | solution.py:53
  15.9 6.7 %all-to-all-start = ((bf16[4,144,1152]{2,1,0:T(8,128)(2,1)}), bf16[4,144,1152]{2,1,0:T(8,128)(2,1)S(1)}, u32[]{:S(2)}, u32[]{:S(2)}) async-start(bf16[4,144,1152]{2,1,0:T(8,128)(2,1)} %get-tuple-element.25), calls=%async_computation | async-start | bytes 2654208 | tf_op jit(solution)/shard_map/all_to_all | solution.py:257
  22.6 4.6 %collective-permute-start = (bf16[144,1152]{1,0:T(8,128)(2,1)S(1)}, bf16[144,1152]{1,0:T(8,128)(2,1)S(1)}, u32[]{:S(2)}, u32[]{:S(2)}) collective-permute-start(bf16[144,1152]{1,0:T(8,128)(2,1)S(1)} %get-tuple-element.26.refs_2_), channel_id=1, source_target_pairs={{0,8},{4,12},{8,0},{12,4},{1,9},{5,13},{9,1},{13,5},{2,10},{6,14},... | collective-permute-start | bytes 995336 | tf_op jit(solution)/shard_map/ppermute | solution.py:28
  27.3 2.2 %collective-permute-start.1 = (bf16[144,1152]{1,0:T(8,128)(2,1)S(1)}, bf16[144,1152]{1,0:T(8,128)(2,1)S(1)}, u32[]{:S(2)}, u32[]{:S(2)}) collective-permute-start(bf16[144,1152]{1,0:T(8,128)(2,1)S(1)} %get-tuple-element.26.refs_2_), channel_id=1, source_target_pairs={{0,4},{4,8},{8,12},{12,0},{1,5},{5,9},{9,13},{13,1},{2,6},{6,10},{... | collective-permute-start | bytes 995336 | tf_op jit(solution)/shard_map/ppermute | solution.py:28
  29.5 4.3 %collective-permute-start.2 = (bf16[144,1152]{1,0:T(8,128)(2,1)S(1)}, bf16[144,1152]{1,0:T(8,128)(2,1)S(1)}, u32[]{:S(2)}, u32[]{:S(2)}) collective-permute-start(bf16[144,1152]{1,0:T(8,128)(2,1)S(1)} %get-tuple-element.26.refs_2_), channel_id=1, source_target_pairs={{0,12},{4,0},{8,4},{12,8},{1,13},{5,1},{9,5},{13,9},{2,14},{6,2},{... | collective-permute-start | bytes 995336 | tf_op jit(solution)/shard_map/ppermute | solution.py:28
  33.8 0.0 collective-permute-done.3.txt_ref
  33.8 0.2 shard_map.50.refs_6_
  34.0 1.9 %collective-permute-start.4 = (bf16[144,1152]{1,0:T(8,128)(2,1)S(1)}, bf16[144,1152]{1,0:T(8,128)(2,1)S(1)}, u32[]{:S(2)}, u32[]{:S(2)}) collective-permute-start(bf16[144,1152]{1,0:T(8,128)(2,1)S(1)} %shard_map.50.refs_6_), channel_id=1, source_target_pairs={{0,8},{4,12},{8,0},{12,4},{1,9},{5,13},{9,1},{13,5},{2,10},{6,14},... | collective-permute-start | bytes 995336 | tf_op jit(solution)/shard_map/ppermute | solution.py:28
  35.9 2.5 %collective-permute-start.5 = (bf16[144,1152]{1,0:T(8,128)(2,1)S(1)}, bf16[144,1152]{1,0:T(8,128)(2,1)}, u32[]{:S(2)}, u32[]{:S(2)}) collective-permute-start(bf16[144,1152]{1,0:T(8,128)(2,1)S(1)} %shard_map.50.refs_6_), channel_id=1, source_target_pairs={{0,4},{4,8},{8,12},{12,0},{1,5},{5,9},{9,13},{13,1},{2,6},{6,10},{... | collective-permute-start | bytes 995336 | tf_op jit(solution)/shard_map/ppermute | solution.py:28
  38.4 0.0 collective-permute-done.refs_3_
  38.4 4.0 %collective-permute-start.6 = (bf16[144,1152]{1,0:T(8,128)(2,1)S(1)}, bf16[144,1152]{1,0:T(8,128)(2,1)}, u32[]{:S(2)}, u32[]{:S(2)}) collective-permute-start(bf16[144,1152]{1,0:T(8,128)(2,1)S(1)} %shard_map.50.refs_6_), channel_id=1, source_target_pairs={{0,12},{4,0},{8,4},{12,8},{1,13},{5,1},{9,5},{13,9},{2,14},{6,2},{... | collective-permute-start | bytes 995336 | tf_op jit(solution)/shard_map/ppermute | solution.py:28
  42.4 0.1 pad_add_fusion.refs_0_
  42.5 5.0 %collective-permute-done.1.refs_4_ = bf16[144,1152]{1,0:T(8,128)(2,1)S(1)} collective-permute-done((bf16[144,1152]{1,0:T(8,128)(2,1)S(1)}, bf16[144,1152]{1,0:T(8,128)(2,1)S(1)}, u32[]{:S(2)}, u32[]{:S(2)}) %collective-permute-start.1) | collective-permute-done | bytes 331808 | tf_op jit(solution)/shard_map/ppermute | solution.py:28
  47.5 0.0 collective-permute-done.2.refs_5_
  47.5 2.4 %collective-permute-done.4.refs_7_ = bf16[144,1152]{1,0:T(8,128)(2,1)S(1)} collective-permute-done((bf16[144,1152]{1,0:T(8,128)(2,1)S(1)}, bf16[144,1152]{1,0:T(8,128)(2,1)S(1)}, u32[]{:S(2)}, u32[]{:S(2)}) %collective-permute-start.4) | collective-permute-done | bytes 331808 | tf_op jit(solution)/shard_map/ppermute | solution.py:28
  49.9 4.8 %collective-permute-done.5.refs_8_ = bf16[144,1152]{1,0:T(8,128)(2,1)} collective-permute-done((bf16[144,1152]{1,0:T(8,128)(2,1)S(1)}, bf16[144,1152]{1,0:T(8,128)(2,1)}, u32[]{:S(2)}, u32[]{:S(2)}) %collective-permute-start.5) | collective-permute-done | bytes 331808 | tf_op jit(solution)/shard_map/ppermute | solution.py:28
  54.7 0.0 collective-permute-done.6.refs_9_
  54.7 0.0 all-to-all-done
  54.7 7.8 %shard_map.51 = (bf16[576,1152]{1,0:T(8,128)(2,1)S(1)}, bf16[320,1152]{1,0:T(8,128)(2,1)S(1)}, bf16[320,1152]{1,0:T(8,128)(2,1)S(1)}) custom-call(s32[2]{0:T(128)S(1)} %pad_add_fusion.refs_0_, bf16[576,1152]{1,0:T(8,128)(2,1)S(1)} %bitcast.4, bf16[144,1152]{1,0:T(8,128)(2,1)S(1)} %get-tuple-element.26.refs_2_, ...), custom_call_target="tpu_custom_call" | custom-call | flops 3057647616 | bytes 6782984 | tf_op jit(solution)/shard_map/pallas_call | solution.py:53
  62.5 3.8 %collective-permute-start.7 = (bf16[320,1152]{1,0:T(8,128)(2,1)S(1)}, bf16[320,1152]{1,0:T(8,128)(2,1)S(1)}, u32[]{:S(2)}, u32[]{:S(2)}) collective-permute-start(bf16[320,1152]{1,0:T(8,128)(2,1)S(1)} %get-tuple-element.28), channel_id=1, source_target_pairs={{0,1},{1,0},{2,3},{3,2},{16,18},{17,19},{18,16},{19,17},{4,5},{5,4... | collective-permute-start | bytes 2211848 | tf_op jit(solution)/shard_map/ppermute | solution.py:36
  66.3 1.4 %shard_map.53 = (bf16[576,1152]{1,0:T(8,128)(2,1)S(1)}, bf16[144,1152]{1,0:T(8,128)(2,1)S(1)}, bf16[144,1152]{1,0:T(8,128)(2,1)S(1)}, bf16[144,1152]{1,0:T(8,128)(2,1)S(1)}, bf16[144,1152]{1,0:T(8,128)(2,1)S(1)}) custom-call(bf16[576,1152]{1,0:T(8,128)(2,1)S(1)} %get-tuple-element.29.slopes_ref, bf16[576,1152]{1,0:T(8,128)(2,1)S(1)} %bitcast.5), custom_call_target="tpu_custom_call" | custom-call | flops 764411904 | bytes 5308416 | tf_op jit(solution)/shard_map/pallas_call | solution.py:53
  67.8 1.9 %collective-permute-start.13 = (bf16[576,1152]{1,0:T(8,128)(2,1)S(1)}, bf16[576,1152]{1,0:T(8,128)(2,1)S(1)}, u32[]{:S(2)}, u32[]{:S(2)}) collective-permute-start(bf16[576,1152]{1,0:T(8,128)(2,1)S(1)} %get-tuple-element.34), channel_id=1, source_target_pairs={{16,0},{17,1},{18,2},{19,3},{20,4},{21,5},{22,6},{23,7},{24,8},{25... | collective-permute-start | bytes 3981320 | tf_op jit(solution)/shard_map/ppermute | solution.py:270
  69.7 0.7 collective-permute-start.10
  70.4 0.7 collective-permute-start.11
  71.1 0.7 collective-permute-start.9
  71.8 0.0 collective-permute-done.10.c
  71.8 0.0 collective-permute-done.11.d
  71.8 0.0 collective-permute-done.9.b
  71.8 0.2 shard_map.54
  72.0 1.3 %collective-permute-start.12 = (bf16[144,1152]{1,0:T(8,128)(2,1)S(1)}, bf16[144,1152]{1,0:T(8,128)(2,1)S(1)}, u32[]{:S(2)}, u32[]{:S(2)}) collective-permute-start(bf16[144,1152]{1,0:T(8,128)(2,1)S(1)} %shard_map.54), channel_id=1, source_target_pairs={{32,16},{64,48},{96,80},{128,112},{160,144},{192,176},{224,208},{2... | collective-permute-start | bytes 995336 | tf_op jit(solution)/shard_map/ppermute | solution.py:44
  73.3 9.2 %collective-permute-done.7.theirs.near = bf16[320,1152]{1,0:T(8,128)(2,1)S(1)} collective-permute-done((bf16[320,1152]{1,0:T(8,128)(2,1)S(1)}, bf16[320,1152]{1,0:T(8,128)(2,1)S(1)}, u32[]{:S(2)}, u32[]{:S(2)}) %collective-permute-start.7) | collective-permute-done | bytes 737312 | tf_op jit(solution)/shard_map/ppermute | solution.py:36
  82.5 0.1 shard_map.52
  82.6 5.9 %collective-permute-start.8 = (bf16[160,1152]{1,0:T(8,128)(2,1)S(1)}, bf16[160,1152]{1,0:T(8,128)(2,1)S(1)}, u32[]{:S(2)}, u32[]{:S(2)}) collective-permute-start(bf16[160,1152]{1,0:T(8,128)(2,1)S(1)} %shard_map.52), channel_id=1, source_target_pairs={{0,2},{1,3},{2,0},{3,1},{16,17},{17,16},{18,19},{19,18},{4,6},{5,7... | collective-permute-start | bytes 1105928 | tf_op jit(solution)/shard_map/ppermute | solution.py:36
  88.5 0.0 collective-permute-done.13.other
  88.5 1.4 %shard_map.55 = (bf16[144,1152]{1,0:T(8,128)(2,1)S(1)}, bf16[144,1152]{1,0:T(8,128)(2,1)S(1)}, bf16[144,1152]{1,0:T(8,128)(2,1)S(1)}, bf16[144,1152]{1,0:T(8,128)(2,1)S(1)}) custom-call(bf16[576,1152]{1,0:T(8,128)(2,1)S(1)} %get-tuple-element.29.slopes_ref, bf16[576,1152]{1,0:T(8,128)(2,1)S(1)} %bitcast.6, bf16[576,1152]{1,0:T(8,128)(2,1)S(1)} %collective-permute-done.13.other), custom_call_target="tpu_custom_call" | custom-call | flops 764411904 | bytes 5308416 | tf_op jit(solution)/shard_map/pallas_call | solution.py:53
  89.9 2.4 %collective-permute-start.14 = (bf16[144,1152]{1,0:T(8,128)(2,1)S(1)}, bf16[144,1152]{1,0:T(8,128)(2,1)S(1)}, u32[]{:S(2)}, u32[]{:S(2)}) collective-permute-start(bf16[144,1152]{1,0:T(8,128)(2,1)S(1)} %get-tuple-element.36), channel_id=1, source_target_pairs={{0,8},{4,12},{8,0},{12,4},{1,9},{5,13},{9,1},{13,5},{2,10},{6,14},... | collective-permute-start | bytes 995336 | tf_op jit(solution)/shard_map/ppermute | solution.py:28
  92.3 3.7 %collective-permute-start.15 = (bf16[144,1152]{1,0:T(8,128)(2,1)S(1)}, bf16[144,1152]{1,0:T(8,128)(2,1)S(1)}, u32[]{:S(2)}, u32[]{:S(2)}) collective-permute-start(bf16[144,1152]{1,0:T(8,128)(2,1)S(1)} %get-tuple-element.37), channel_id=1, source_target_pairs={{0,12},{4,0},{8,4},{12,8},{1,13},{5,1},{9,5},{13,9},{2,14},{6,2},{... | collective-permute-start | bytes 995336 | tf_op jit(solution)/shard_map/ppermute | solution.py:28
  95.9 1.9 %collective-permute-start.16 = (bf16[144,1152]{1,0:T(8,128)(2,1)S(1)}, bf16[144,1152]{1,0:T(8,128)(2,1)S(1)}, u32[]{:S(2)}, u32[]{:S(2)}) collective-permute-start(bf16[144,1152]{1,0:T(8,128)(2,1)S(1)} %get-tuple-element.38), channel_id=1, source_target_pairs={{0,4},{4,8},{8,12},{12,0},{1,5},{5,9},{9,13},{13,1},{2,6},{6,10},{... | collective-permute-start | bytes 995336 | tf_op jit(solution)/shard_map/ppermute | solution.py:28
  97.9 5.8 %collective-permute-done.12.home = bf16[144,1152]{1,0:T(8,128)(2,1)S(1)} collective-permute-done((bf16[144,1152]{1,0:T(8,128)(2,1)S(1)}, bf16[144,1152]{1,0:T(8,128)(2,1)S(1)}, u32[]{:S(2)}, u32[]{:S(2)}) %collective-permute-start.12) | collective-permute-done | bytes 331808 | tf_op jit(solution)/shard_map/ppermute | solution.py:44
  103.7 7.5 %collective-permute-done.8.far = bf16[160,1152]{1,0:T(8,128)(2,1)S(1)} collective-permute-done((bf16[160,1152]{1,0:T(8,128)(2,1)S(1)}, bf16[160,1152]{1,0:T(8,128)(2,1)S(1)}, u32[]{:S(2)}, u32[]{:S(2)}) %collective-permute-start.8) | collective-permute-done | bytes 368672 | tf_op jit(solution)/shard_map/ppermute | solution.py:36
  111.2 0.0 collective-permute-done.14.b
  111.2 0.0 collective-permute-done.15.c
  111.2 0.0 collective-permute-done.16.d
  111.2 0.0 copy-start.1
  111.2 0.1 shard_map.57.base
  111.3 0.9 copy-done.1
  112.2 0.0 copy-start.3
  112.2 1.2 %shard_map.58 = f32[144,1152]{1,0:T(8,128)} custom-call(bf16[144,1152]{1,0:T(8,128)(2,1)S(1)} %copy-done.1, f32[144,1152]{1,0:T(8,128)S(1)} %shard_map.57.base, bf16[144,1152]{1,0:T(8,128)(2,1)S(1)} %collective-permute-done.14.b, bf16[144,1152]{1,0:T(8,128)(2,1)S(1)} %collective-permute-done.15.c, bf16[144,1152]{1,0:T(8,128)(2,1)S(1)} %collective-permute-done.16.d), custom_call_target="tpu_custom_call" | custom-call | bytes 2654208 | tf_op jit(solution)/shard_map/pallas_call | solution.py:53
  113.4 0.0 copy-done.3
  113.4 1.2 %shard_map.56 = (f32[144,1152]{1,0:T(8,128)}, f32[1,144]{1,0:T(1,128)}) custom-call(bf16[144,1152]{1,0:T(8,128)(2,1)S(1)} %copy-done.3, bf16[320,1152]{1,0:T(8,128)(2,1)S(1)} %get-tuple-element.27.mine, bf16[320,1152]{1,0:T(8,128)(2,1)S(1)} %collective-permute-done.7.theirs.near, bf16[160,1152]{1,0:T(8,128)(2,1)S(1)} %collective-permute-done.8.far), custom_call_target="tpu_custom_call" | custom-call | bytes 2839104 | tf_op jit(solution)/shard_map/pallas_call | solution.py:53
Async XLA Ops:
  0.6 33.2 %collective-permute-start.3 = (bf16[144,1152]{1,0:T(8,128)(2,1)}, bf16[144,1152]{1,0:T(8,128)(2,1)S(1)}, u32[]{:S(2)}, u32[]{:S(2)}) collective-permute-start(bf16[144,1152]{1,0:T(8,128)(2,1)} %raw_ref.3), channel_id=1, source_target_pairs={{0,16},{16,32},{32,48},{48,64},{64,80},{80,96},{96,112},{112,128},... | collective-permute-start | bytes 995336 | tf_op jit(solution)/shard_map/ppermute | solution.py:28
  12.7 1.0 copy-start
  13.7 1.0 copy-start.2
  15.9 38.8 %all-to-all-start = ((bf16[4,144,1152]{2,1,0:T(8,128)(2,1)}), bf16[4,144,1152]{2,1,0:T(8,128)(2,1)S(1)}, u32[]{:S(2)}, u32[]{:S(2)}) async-start(bf16[4,144,1152]{2,1,0:T(8,128)(2,1)} %get-tuple-element.25), calls=%async_computation | async-start | bytes 2654208 | tf_op jit(solution)/shard_map/all_to_all | solution.py:257
  22.6 15.8 %collective-permute-start = (bf16[144,1152]{1,0:T(8,128)(2,1)S(1)}, bf16[144,1152]{1,0:T(8,128)(2,1)S(1)}, u32[]{:S(2)}, u32[]{:S(2)}) collective-permute-start(bf16[144,1152]{1,0:T(8,128)(2,1)S(1)} %get-tuple-element.26.refs_2_), channel_id=1, source_target_pairs={{0,8},{4,12},{8,0},{12,4},{1,9},{5,13},{9,1},{13,5},{2,10},{6,14},... | collective-permute-start | bytes 995336 | tf_op jit(solution)/shard_map/ppermute | solution.py:28
  27.3 20.2 %collective-permute-start.1 = (bf16[144,1152]{1,0:T(8,128)(2,1)S(1)}, bf16[144,1152]{1,0:T(8,128)(2,1)S(1)}, u32[]{:S(2)}, u32[]{:S(2)}) collective-permute-start(bf16[144,1152]{1,0:T(8,128)(2,1)S(1)} %get-tuple-element.26.refs_2_), channel_id=1, source_target_pairs={{0,4},{4,8},{8,12},{12,0},{1,5},{5,9},{9,13},{13,1},{2,6},{6,10},{... | collective-permute-start | bytes 995336 | tf_op jit(solution)/shard_map/ppermute | solution.py:28
  29.5 18.0 %collective-permute-start.2 = (bf16[144,1152]{1,0:T(8,128)(2,1)S(1)}, bf16[144,1152]{1,0:T(8,128)(2,1)S(1)}, u32[]{:S(2)}, u32[]{:S(2)}) collective-permute-start(bf16[144,1152]{1,0:T(8,128)(2,1)S(1)} %get-tuple-element.26.refs_2_), channel_id=1, source_target_pairs={{0,12},{4,0},{8,4},{12,8},{1,13},{5,1},{9,5},{13,9},{2,14},{6,2},{... | collective-permute-start | bytes 995336 | tf_op jit(solution)/shard_map/ppermute | solution.py:28
  34.0 15.9 %collective-permute-start.4 = (bf16[144,1152]{1,0:T(8,128)(2,1)S(1)}, bf16[144,1152]{1,0:T(8,128)(2,1)S(1)}, u32[]{:S(2)}, u32[]{:S(2)}) collective-permute-start(bf16[144,1152]{1,0:T(8,128)(2,1)S(1)} %shard_map.50.refs_6_), channel_id=1, source_target_pairs={{0,8},{4,12},{8,0},{12,4},{1,9},{5,13},{9,1},{13,5},{2,10},{6,14},... | collective-permute-start | bytes 995336 | tf_op jit(solution)/shard_map/ppermute | solution.py:28
  35.9 18.8 %collective-permute-start.5 = (bf16[144,1152]{1,0:T(8,128)(2,1)S(1)}, bf16[144,1152]{1,0:T(8,128)(2,1)}, u32[]{:S(2)}, u32[]{:S(2)}) collective-permute-start(bf16[144,1152]{1,0:T(8,128)(2,1)S(1)} %shard_map.50.refs_6_), channel_id=1, source_target_pairs={{0,4},{4,8},{8,12},{12,0},{1,5},{5,9},{9,13},{13,1},{2,6},{6,10},{... | collective-permute-start | bytes 995336 | tf_op jit(solution)/shard_map/ppermute | solution.py:28
  38.4 16.3 %collective-permute-start.6 = (bf16[144,1152]{1,0:T(8,128)(2,1)S(1)}, bf16[144,1152]{1,0:T(8,128)(2,1)}, u32[]{:S(2)}, u32[]{:S(2)}) collective-permute-start(bf16[144,1152]{1,0:T(8,128)(2,1)S(1)} %shard_map.50.refs_6_), channel_id=1, source_target_pairs={{0,12},{4,0},{8,4},{12,8},{1,13},{5,1},{9,5},{13,9},{2,14},{6,2},{... | collective-permute-start | bytes 995336 | tf_op jit(solution)/shard_map/ppermute | solution.py:28
  62.5 20.0 %collective-permute-start.7 = (bf16[320,1152]{1,0:T(8,128)(2,1)S(1)}, bf16[320,1152]{1,0:T(8,128)(2,1)S(1)}, u32[]{:S(2)}, u32[]{:S(2)}) collective-permute-start(bf16[320,1152]{1,0:T(8,128)(2,1)S(1)} %get-tuple-element.28), channel_id=1, source_target_pairs={{0,1},{1,0},{2,3},{3,2},{16,18},{17,19},{18,16},{19,17},{4,5},{5,4... | collective-permute-start | bytes 2211848 | tf_op jit(solution)/shard_map/ppermute | solution.py:36
  67.8 20.7 %collective-permute-start.13 = (bf16[576,1152]{1,0:T(8,128)(2,1)S(1)}, bf16[576,1152]{1,0:T(8,128)(2,1)S(1)}, u32[]{:S(2)}, u32[]{:S(2)}) collective-permute-start(bf16[576,1152]{1,0:T(8,128)(2,1)S(1)} %get-tuple-element.34), channel_id=1, source_target_pairs={{16,0},{17,1},{18,2},{19,3},{20,4},{21,5},{22,6},{23,7},{24,8},{25... | collective-permute-start | bytes 3981320 | tf_op jit(solution)/shard_map/ppermute | solution.py:270
  69.7 2.1 %collective-permute-start.10 = (bf16[144,1152]{1,0:T(8,128)(2,1)S(1)}, bf16[144,1152]{1,0:T(8,128)(2,1)S(1)}, u32[]{:S(2)}, u32[]{:S(2)}) collective-permute-start(bf16[144,1152]{1,0:T(8,128)(2,1)S(1)} %get-tuple-element.32), channel_id=1, source_target_pairs={{0,12},{4,0},{8,4},{12,8},{1,13},{5,1},{9,5},{13,9},{2,14},{6,2},{... | collective-permute-start | bytes 995336 | tf_op jit(solution)/shard_map/ppermute | solution.py:48
  70.4 1.4 %collective-permute-start.11 = (bf16[144,1152]{1,0:T(8,128)(2,1)S(1)}, bf16[144,1152]{1,0:T(8,128)(2,1)S(1)}, u32[]{:S(2)}, u32[]{:S(2)}) collective-permute-start(bf16[144,1152]{1,0:T(8,128)(2,1)S(1)} %get-tuple-element.33), channel_id=1, source_target_pairs={{0,4},{4,8},{8,12},{12,0},{1,5},{5,9},{9,13},{13,1},{2,6},{6,10},{... | collective-permute-start | bytes 995336 | tf_op jit(solution)/shard_map/ppermute | solution.py:48
  71.1 0.7 collective-permute-start.9
  72.0 31.7 %collective-permute-start.12 = (bf16[144,1152]{1,0:T(8,128)(2,1)S(1)}, bf16[144,1152]{1,0:T(8,128)(2,1)S(1)}, u32[]{:S(2)}, u32[]{:S(2)}) collective-permute-start(bf16[144,1152]{1,0:T(8,128)(2,1)S(1)} %shard_map.54), channel_id=1, source_target_pairs={{32,16},{64,48},{96,80},{128,112},{160,144},{192,176},{224,208},{2... | collective-permute-start | bytes 995336 | tf_op jit(solution)/shard_map/ppermute | solution.py:44
  82.6 28.6 %collective-permute-start.8 = (bf16[160,1152]{1,0:T(8,128)(2,1)S(1)}, bf16[160,1152]{1,0:T(8,128)(2,1)S(1)}, u32[]{:S(2)}, u32[]{:S(2)}) collective-permute-start(bf16[160,1152]{1,0:T(8,128)(2,1)S(1)} %shard_map.52), channel_id=1, source_target_pairs={{0,2},{1,3},{2,0},{3,1},{16,17},{17,16},{18,19},{19,18},{4,6},{5,7... | collective-permute-start | bytes 1105928 | tf_op jit(solution)/shard_map/ppermute | solution.py:36
  89.9 21.3 %collective-permute-start.14 = (bf16[144,1152]{1,0:T(8,128)(2,1)S(1)}, bf16[144,1152]{1,0:T(8,128)(2,1)S(1)}, u32[]{:S(2)}, u32[]{:S(2)}) collective-permute-start(bf16[144,1152]{1,0:T(8,128)(2,1)S(1)} %get-tuple-element.36), channel_id=1, source_target_pairs={{0,8},{4,12},{8,0},{12,4},{1,9},{5,13},{9,1},{13,5},{2,10},{6,14},... | collective-permute-start | bytes 995336 | tf_op jit(solution)/shard_map/ppermute | solution.py:28
  92.3 18.9 %collective-permute-start.15 = (bf16[144,1152]{1,0:T(8,128)(2,1)S(1)}, bf16[144,1152]{1,0:T(8,128)(2,1)S(1)}, u32[]{:S(2)}, u32[]{:S(2)}) collective-permute-start(bf16[144,1152]{1,0:T(8,128)(2,1)S(1)} %get-tuple-element.37), channel_id=1, source_target_pairs={{0,12},{4,0},{8,4},{12,8},{1,13},{5,1},{9,5},{13,9},{2,14},{6,2},{... | collective-permute-start | bytes 995336 | tf_op jit(solution)/shard_map/ppermute | solution.py:28
  95.9 15.2 %collective-permute-start.16 = (bf16[144,1152]{1,0:T(8,128)(2,1)S(1)}, bf16[144,1152]{1,0:T(8,128)(2,1)S(1)}, u32[]{:S(2)}, u32[]{:S(2)}) collective-permute-start(bf16[144,1152]{1,0:T(8,128)(2,1)S(1)} %get-tuple-element.38), channel_id=1, source_target_pairs={{0,4},{4,8},{8,12},{12,0},{1,5},{5,9},{9,13},{13,1},{2,6},{6,10},{... | collective-permute-start | bytes 995336 | tf_op jit(solution)/shard_map/ppermute | solution.py:28
  111.2 1.0 copy-start.1
  112.2 1.2 %copy-start.3 = (bf16[144,1152]{1,0:T(8,128)(2,1)S(1)}, bf16[144,1152]{1,0:T(8,128)(2,1)}, u32[]{:S(2)}) copy-start(bf16[144,1152]{1,0:T(8,128)(2,1)} %raw_ref.2) | copy-start | bytes 995332

commit v9 on v8

--- a/solution.py
+++ b/solution.py
@@ -274,13 +274,13 @@
     parts = text_call(now_parts_kernel, [slopes, img_all, across], [unit] * NX)
     now_back = [parts[0]] + [shifted(p, "x", -s) for p, s in zip(parts[1:], HOPS)]
 
-    back_far, home, now_back = lax.optimization_barrier((back_far, home, now_back))
     wide = shape((own, features), F32)
+    (base,) = vmem_call(base_kernel, [now_back[0], home], [wide], 8, flops=HOME_WEIGHT)
+    (text_grad,) = vmem_call(text_end_kernel, [texts, base] + now_back[1:], [wide], 12)
+    back_far, text_grad = lax.optimization_barrier((back_far, text_grad))
     image_grad, row_loss = vmem_call(
         image_end_kernel, [images, keep, back_near, back_far], [wide, shape((1, own), F32)], 12
     )
-    (base,) = vmem_call(base_kernel, [now_back[0], home], [wide], 8, flops=HOME_WEIGHT)
-    (text_grad,) = vmem_call(text_end_kernel, [texts, base] + now_back[1:], [wide], 12)
     return (row_loss.reshape(own), image_grad, text_grad)
 
 

time: 116 us -> 116 us (level)
  the two profiles are of different devices: /device:TPU:1 before, /device:TPU:105 now
where the time goes in v9:
time: 116 us; the launch traced here: 115 us
  starting transfers between devices  56.6 us (49%)
  waiting for transfers between devices  39.8 us (34%)
  Pallas kernels  14.9 us (13%)
  local copies, waits for them, and re-layouts  2.82 us (2%)
    ppermute x10, starting transfers between devices, shifted(): lax.ppermute(value, axis, [(i, (i + steps) % count) for i in range(count)])  39.3 us
    ppermute x1, waiting for transfers between devices, next_group(): return lax.ppermute(value, BLK, pairs)  17.1 us
    pallas_call x10, Pallas kernels, vmem_call(): pl.pallas_call(body, out_shape=list(outs), in_specs=[pl.BlockSpec(memory_...  14.9 us
    ppermute x10, waiting for transfers between devices, shifted(): lax.ppermute(value, axis, [(i, (i + steps) % count) for i in range(count)])  9.93 us
    ppermute x2, waiting for transfers between devices, across_z(): return lax.ppermute(value, ('core', 'z'), pairs)  9.4 us
    ppermute x2, starting transfers between devices, across_z(): return lax.ppermute(value, ('core', 'z'), pairs)  6.53 us
    all_to_all x1, starting transfers between devices, on_device(): img_all = lax.all_to_all(spread, 'z', 0, 0).reshape(NZ * own, features)  6.06 us
    all_to_all x1, waiting for transfers between devices, on_device(): img_all = lax.all_to_all(spread, 'z', 0, 0).reshape(NZ * own, features)  3.43 us
  transfers between devices with their start and end apart: 18, of which 8 were waited for; matrix products, arithmetic and copies ran while one was open for 0% of the time, Pallas kernels for 5%

profile of v9, /device:TPU:105, one launch (start us, length us, event | category | flops | bytes accessed | tf_op | source)
XLA Modules:
  0.0 115.1 jit_solution(11788397248586976412)
XLA Ops:
  0.6 11.2 %collective-permute-start.3 = (bf16[144,1152]{1,0:T(8,128)(2,1)}, bf16[144,1152]{1,0:T(8,128)(2,1)S(1)}, u32[]{:S(2)}, u32[]{:S(2)}) collective-permute-start(bf16[144,1152]{1,0:T(8,128)(2,1)} %raw_ref.2), channel_id=1, source_target_pairs={{0,16},{16,32},{32,48},{48,64},{64,80},{80,96},{96,112},{112,128},... | collective-permute-start | bytes 995336 | tf_op jit(solution)/shard_map/ppermute | solution.py:28
  11.8 0.0 copy-start
  11.8 1.0 copy-done
  12.8 0.0 copy-start.2
  12.8 1.0 copy-done.2
  13.8 1.3 %shard_map.49 = (bf16[4,144,1152]{2,1,0:T(8,128)(2,1)}, bf16[144,1152]{1,0:T(8,128)(2,1)S(1)}) custom-call(bf16[144,1152]{1,0:T(8,128)(2,1)S(1)} %copy-done.2, bf16[144,1152]{1,0:T(8,128)(2,1)S(1)} %copy-done), custom_call_target="tpu_custom_call" | custom-call | bytes 2322432 | tf_op jit(solution)/shard_map/pallas_call | solution.py:53
  15.1 6.1 %all-to-all-start = ((bf16[4,144,1152]{2,1,0:T(8,128)(2,1)}), bf16[4,144,1152]{2,1,0:T(8,128)(2,1)S(1)}, u32[]{:S(2)}, u32[]{:S(2)}) async-start(bf16[4,144,1152]{2,1,0:T(8,128)(2,1)} %get-tuple-element.21), calls=%async_computation | async-start | bytes 2654208 | tf_op jit(solution)/shard_map/all_to_all | solution.py:257
  21.2 4.6 %collective-permute-start = (bf16[144,1152]{1,0:T(8,128)(2,1)S(1)}, bf16[144,1152]{1,0:T(8,128)(2,1)S(1)}, u32[]{:S(2)}, u32[]{:S(2)}) collective-permute-start(bf16[144,1152]{1,0:T(8,128)(2,1)S(1)} %get-tuple-element.22.refs_2_), channel_id=1, source_target_pairs={{0,8},{4,12},{8,0},{12,4},{1,9},{5,13},{9,1},{13,5},{2,10},{6,14},... | collective-permute-start | bytes 995336 | tf_op jit(solution)/shard_map/ppermute | solution.py:28
  25.8 2.2 %collective-permute-start.1 = (bf16[144,1152]{1,0:T(8,128)(2,1)S(1)}, bf16[144,1152]{1,0:T(8,128)(2,1)S(1)}, u32[]{:S(2)}, u32[]{:S(2)}) collective-permute-start(bf16[144,1152]{1,0:T(8,128)(2,1)S(1)} %get-tuple-element.22.refs_2_), channel_id=1, source_target_pairs={{0,4},{4,8},{8,12},{12,0},{1,5},{5,9},{9,13},{13,1},{2,6},{6,10},{... | collective-permute-start | bytes 995336 | tf_op jit(solution)/shard_map/ppermute | solution.py:28
  28.0 4.3 %collective-permute-start.2 = (bf16[144,1152]{1,0:T(8,128)(2,1)S(1)}, bf16[144,1152]{1,0:T(8,128)(2,1)S(1)}, u32[]{:S(2)}, u32[]{:S(2)}) collective-permute-start(bf16[144,1152]{1,0:T(8,128)(2,1)S(1)} %get-tuple-element.22.refs_2_), channel_id=1, source_target_pairs={{0,12},{4,0},{8,4},{12,8},{1,13},{5,1},{9,5},{13,9},{2,14},{6,2},{... | collective-permute-start | bytes 995336 | tf_op jit(solution)/shard_map/ppermute | solution.py:28
  32.3 0.0 collective-permute-done.3.txt_ref
  32.3 0.2 shard_map.50.refs_6_
  32.5 1.9 %collective-permute-start.4 = (bf16[144,1152]{1,0:T(8,128)(2,1)S(1)}, bf16[144,1152]{1,0:T(8,128)(2,1)S(1)}, u32[]{:S(2)}, u32[]{:S(2)}) collective-permute-start(bf16[144,1152]{1,0:T(8,128)(2,1)S(1)} %shard_map.50.refs_6_), channel_id=1, source_target_pairs={{0,8},{4,12},{8,0},{12,4},{1,9},{5,13},{9,1},{13,5},{2,10},{6,14},... | collective-permute-start | bytes 995336 | tf_op jit(solution)/shard_map/ppermute | solution.py:28
  34.4 2.5 %collective-permute-start.5 = (bf16[144,1152]{1,0:T(8,128)(2,1)S(1)}, bf16[144,1152]{1,0:T(8,128)(2,1)}, u32[]{:S(2)}, u32[]{:S(2)}) collective-permute-start(bf16[144,1152]{1,0:T(8,128)(2,1)S(1)} %shard_map.50.refs_6_), channel_id=1, source_target_pairs={{0,4},{4,8},{8,12},{12,0},{1,5},{5,9},{9,13},{13,1},{2,6},{6,10},{... | collective-permute-start | bytes 995336 | tf_op jit(solution)/shard_map/ppermute | solution.py:28
  36.9 0.0 collective-permute-done.refs_3_
  36.9 4.0 %collective-permute-start.6 = (bf16[144,1152]{1,0:T(8,128)(2,1)S(1)}, bf16[144,1152]{1,0:T(8,128)(2,1)}, u32[]{:S(2)}, u32[]{:S(2)}) collective-permute-start(bf16[144,1152]{1,0:T(8,128)(2,1)S(1)} %shard_map.50.refs_6_), channel_id=1, source_target_pairs={{0,12},{4,0},{8,4},{12,8},{1,13},{5,1},{9,5},{13,9},{2,14},{6,2},{... | collective-permute-start | bytes 995336 | tf_op jit(solution)/shard_map/ppermute | solution.py:28
  41.0 0.1 pad_add_fusion.refs_0_
  41.0 0.8 collective-permute-done.1.refs_4_
  41.8 2.7 %collective-permute-done.2.refs_5_ = bf16[144,1152]{1,0:T(8,128)(2,1)S(1)} collective-permute-done((bf16[144,1152]{1,0:T(8,128)(2,1)S(1)}, bf16[144,1152]{1,0:T(8,128)(2,1)S(1)}, u32[]{:S(2)}, u32[]{:S(2)}) %collective-permute-start.2) | collective-permute-done | bytes 331808 | tf_op jit(solution)/shard_map/ppermute | solution.py:28
  44.5 0.6 collective-permute-done.4.refs_7_
  45.1 4.2 %collective-permute-done.5.refs_8_ = bf16[144,1152]{1,0:T(8,128)(2,1)} collective-permute-done((bf16[144,1152]{1,0:T(8,128)(2,1)S(1)}, bf16[144,1152]{1,0:T(8,128)(2,1)}, u32[]{:S(2)}, u32[]{:S(2)}) %collective-permute-start.5) | collective-permute-done | bytes 331808 | tf_op jit(solution)/shard_map/ppermute | solution.py:28
  49.3 1.7 %collective-permute-done.6.refs_9_ = bf16[144,1152]{1,0:T(8,128)(2,1)} collective-permute-done((bf16[144,1152]{1,0:T(8,128)(2,1)S(1)}, bf16[144,1152]{1,0:T(8,128)(2,1)}, u32[]{:S(2)}, u32[]{:S(2)}) %collective-permute-start.6) | collective-permute-done | bytes 331808 | tf_op jit(solution)/shard_map/ppermute | solution.py:28
  51.0 3.4 %all-to-all-done = bf16[4,144,1152]{2,1,0:T(8,128)(2,1)S(1)} async-done(((bf16[4,144,1152]{2,1,0:T(8,128)(2,1)}), bf16[4,144,1152]{2,1,0:T(8,128)(2,1)S(1)}, u32[]{:S(2)}, u32[]{:S(2)}) %all-to-all-start) | async-done | bytes 1327136 | tf_op jit(solution)/shard_map/all_to_all | solution.py:257
  54.4 7.8 %shard_map.51 = (bf16[576,1152]{1,0:T(8,128)(2,1)S(1)}, bf16[320,1152]{1,0:T(8,128)(2,1)S(1)}, bf16[320,1152]{1,0:T(8,128)(2,1)S(1)}) custom-call(s32[2]{0:T(128)S(1)} %pad_add_fusion.refs_0_, bf16[576,1152]{1,0:T(8,128)(2,1)S(1)} %bitcast.4, bf16[144,1152]{1,0:T(8,128)(2,1)S(1)} %get-tuple-element.22.refs_2_, ...), custom_call_target="tpu_custom_call" | custom-call | flops 3057647616 | bytes 6782984 | tf_op jit(solution)/shard_map/pallas_call | solution.py:53
  62.2 4.6 %collective-permute-start.7 = (bf16[320,1152]{1,0:T(8,128)(2,1)S(1)}, bf16[320,1152]{1,0:T(8,128)(2,1)S(1)}, u32[]{:S(2)}, u32[]{:S(2)}) collective-permute-start(bf16[320,1152]{1,0:T(8,128)(2,1)S(1)} %get-tuple-element.24), channel_id=1, source_target_pairs={{0,1},{1,0},{2,3},{3,2},{16,18},{17,19},{18,16},{19,17},{4,5},{5,4... | collective-permute-start | bytes 2211848 | tf_op jit(solution)/shard_map/ppermute | solution.py:36
  66.8 1.4 %shard_map.53 = (bf16[576,1152]{1,0:T(8,128)(2,1)S(1)}, bf16[144,1152]{1,0:T(8,128)(2,1)S(1)}, bf16[144,1152]{1,0:T(8,128)(2,1)S(1)}, bf16[144,1152]{1,0:T(8,128)(2,1)S(1)}, bf16[144,1152]{1,0:T(8,128)(2,1)S(1)}) custom-call(bf16[576,1152]{1,0:T(8,128)(2,1)S(1)} %get-tuple-element.25.slopes_ref, bf16[576,1152]{1,0:T(8,128)(2,1)S(1)} %bitcast.5), custom_call_target="tpu_custom_call" | custom-call | flops 764411904 | bytes 5308416 | tf_op jit(solution)/shard_map/pallas_call | solution.py:53
  68.2 1.4 %collective-permute-start.9 = (bf16[576,1152]{1,0:T(8,128)(2,1)S(1)}, bf16[576,1152]{1,0:T(8,128)(2,1)S(1)}, u32[]{:S(2)}, u32[]{:S(2)}) collective-permute-start(bf16[576,1152]{1,0:T(8,128)(2,1)S(1)} %get-tuple-element.26), channel_id=1, source_target_pairs={{16,0},{17,1},{18,2},{19,3},{20,4},{21,5},{22,6},{23,7},{24,8},{25... | collective-permute-start | bytes 3981320 | tf_op jit(solution)/shard_map/ppermute | solution.py:270
  69.6 0.7 collective-permute-start.10
  70.3 0.7 collective-permute-start.11
  71.0 0.7 collective-permute-start.12
  71.7 0.0 collective-permute-done.10.b
  71.7 0.0 collective-permute-done.11.c
  71.7 0.0 collective-permute-done.12.d
  71.7 0.2 shard_map.55
  71.9 1.3 %collective-permute-start.13 = (bf16[144,1152]{1,0:T(8,128)(2,1)S(1)}, bf16[144,1152]{1,0:T(8,128)(2,1)S(1)}, u32[]{:S(2)}, u32[]{:S(2)}) collective-permute-start(bf16[144,1152]{1,0:T(8,128)(2,1)S(1)} %shard_map.55), channel_id=1, source_target_pairs={{32,16},{64,48},{96,80},{128,112},{160,144},{192,176},{224,208},{2... | collective-permute-start | bytes 995336 | tf_op jit(solution)/shard_map/ppermute | solution.py:44
  73.2 9.4 %collective-permute-done.7.theirs.near = bf16[320,1152]{1,0:T(8,128)(2,1)S(1)} collective-permute-done((bf16[320,1152]{1,0:T(8,128)(2,1)S(1)}, bf16[320,1152]{1,0:T(8,128)(2,1)S(1)}, u32[]{:S(2)}, u32[]{:S(2)}) %collective-permute-start.7) | collective-permute-done | bytes 737312 | tf_op jit(solution)/shard_map/ppermute | solution.py:36
  82.6 0.1 shard_map.52
  82.7 1.9 %collective-permute-start.8 = (bf16[160,1152]{1,0:T(8,128)(2,1)S(1)}, bf16[160,1152]{1,0:T(8,128)(2,1)S(1)}, u32[]{:S(2)}, u32[]{:S(2)}) collective-permute-start(bf16[160,1152]{1,0:T(8,128)(2,1)S(1)} %shard_map.52), channel_id=1, source_target_pairs={{0,2},{1,3},{2,0},{3,1},{16,17},{17,16},{18,19},{19,18},{4,6},{5,7... | collective-permute-start | bytes 1105928 | tf_op jit(solution)/shard_map/ppermute | solution.py:36
  84.6 0.0 collective-permute-done.9.other
  84.6 1.4 %shard_map.54 = (bf16[144,1152]{1,0:T(8,128)(2,1)S(1)}, bf16[144,1152]{1,0:T(8,128)(2,1)S(1)}, bf16[144,1152]{1,0:T(8,128)(2,1)S(1)}, bf16[144,1152]{1,0:T(8,128)(2,1)S(1)}) custom-call(bf16[576,1152]{1,0:T(8,128)(2,1)S(1)} %get-tuple-element.25.slopes_ref, bf16[576,1152]{1,0:T(8,128)(2,1)S(1)} %bitcast.6, bf16[576,1152]{1,0:T(8,128)(2,1)S(1)} %collective-permute-done.9.other), custom_call_target="tpu_custom_call" | custom-call | flops 764411904 | bytes 5308416 | tf_op jit(solution)/shard_map/pallas_call | solution.py:53
  86.0 3.2 %collective-permute-start.14 = (bf16[144,1152]{1,0:T(8,128)(2,1)S(1)}, bf16[144,1152]{1,0:T(8,128)(2,1)S(1)}, u32[]{:S(2)}, u32[]{:S(2)}) collective-permute-start(bf16[144,1152]{1,0:T(8,128)(2,1)S(1)} %get-tuple-element.32), channel_id=1, source_target_pairs={{0,8},{4,12},{8,0},{12,4},{1,9},{5,13},{9,1},{13,5},{2,10},{6,14},... | collective-permute-start | bytes 995336 | tf_op jit(solution)/shard_map/ppermute | solution.py:28
  89.3 2.8 %collective-permute-start.15 = (bf16[144,1152]{1,0:T(8,128)(2,1)S(1)}, bf16[144,1152]{1,0:T(8,128)(2,1)S(1)}, u32[]{:S(2)}, u32[]{:S(2)}) collective-permute-start(bf16[144,1152]{1,0:T(8,128)(2,1)S(1)} %get-tuple-element.33), channel_id=1, source_target_pairs={{0,12},{4,0},{8,4},{12,8},{1,13},{5,1},{9,5},{13,9},{2,14},{6,2},{... | collective-permute-start | bytes 995336 | tf_op jit(solution)/shard_map/ppermute | solution.py:28
  92.1 2.5 %collective-permute-start.16 = (bf16[144,1152]{1,0:T(8,128)(2,1)S(1)}, bf16[144,1152]{1,0:T(8,128)(2,1)S(1)}, u32[]{:S(2)}, u32[]{:S(2)}) collective-permute-start(bf16[144,1152]{1,0:T(8,128)(2,1)S(1)} %get-tuple-element.34), channel_id=1, source_target_pairs={{0,4},{4,8},{8,12},{12,0},{1,5},{5,9},{9,13},{13,1},{2,6},{6,10},{... | collective-permute-start | bytes 995336 | tf_op jit(solution)/shard_map/ppermute | solution.py:28
  94.6 17.1 %collective-permute-done.13.home = bf16[144,1152]{1,0:T(8,128)(2,1)S(1)} collective-permute-done((bf16[144,1152]{1,0:T(8,128)(2,1)S(1)}, bf16[144,1152]{1,0:T(8,128)(2,1)S(1)}, u32[]{:S(2)}, u32[]{:S(2)}) %collective-permute-start.13) | collective-permute-done | bytes 331808 | tf_op jit(solution)/shard_map/ppermute | solution.py:44
  111.7 0.0 copy-start.1
  111.7 0.1 shard_map.56.base
  111.7 0.0 copy-start.3
  111.7 0.0 collective-permute-done.14.b
  111.8 0.0 collective-permute-done.15.c
  111.8 0.0 collective-permute-done.16.d
  111.8 0.9 copy-done.1
  112.6 1.2 %shard_map.57 = f32[144,1152]{1,0:T(8,128)} custom-call(bf16[144,1152]{1,0:T(8,128)(2,1)S(1)} %copy-done.1, f32[144,1152]{1,0:T(8,128)S(1)} %shard_map.56.base, bf16[144,1152]{1,0:T(8,128)(2,1)S(1)} %collective-permute-done.14.b, bf16[144,1152]{1,0:T(8,128)(2,1)S(1)} %collective-permute-done.15.c, bf16[144,1152]{1,0:T(8,128)(2,1)S(1)} %collective-permute-done.16.d), custom_call_target="tpu_custom_call" | custom-call | bytes 2654208 | tf_op jit(solution)/shard_map/pallas_call | solution.py:53
  113.9 0.0 collective-permute-done.8.far
  113.9 0.0 copy-done.3
  113.9 1.2 %shard_map.58 = (f32[144,1152]{1,0:T(8,128)}, f32[1,144]{1,0:T(1,128)}) custom-call(bf16[144,1152]{1,0:T(8,128)(2,1)S(1)} %copy-done.3, bf16[320,1152]{1,0:T(8,128)(2,1)S(1)} %get-tuple-element.23.mine, bf16[320,1152]{1,0:T(8,128)(2,1)S(1)} %collective-permute-done.7.theirs.near, bf16[160,1152]{1,0:T(8,128)(2,1)S(1)} %collective-permute-done.8.far), custom_call_target="tpu_custom_call" | custom-call | bytes 2839104 | tf_op jit(solution)/shard_map/pallas_call | solution.py:53
Async XLA Ops:
  0.6 31.7 %collective-permute-start.3 = (bf16[144,1152]{1,0:T(8,128)(2,1)}, bf16[144,1152]{1,0:T(8,128)(2,1)S(1)}, u32[]{:S(2)}, u32[]{:S(2)}) collective-permute-start(bf16[144,1152]{1,0:T(8,128)(2,1)} %raw_ref.2), channel_id=1, source_target_pairs={{0,16},{16,32},{32,48},{48,64},{64,80},{80,96},{96,112},{112,128},... | collective-permute-start | bytes 995336 | tf_op jit(solution)/shard_map/ppermute | solution.py:28
  11.8 1.0 copy-start
  12.8 1.0 copy-start.2
  15.1 39.3 %all-to-all-start = ((bf16[4,144,1152]{2,1,0:T(8,128)(2,1)}), bf16[4,144,1152]{2,1,0:T(8,128)(2,1)S(1)}, u32[]{:S(2)}, u32[]{:S(2)}) async-start(bf16[4,144,1152]{2,1,0:T(8,128)(2,1)} %get-tuple-element.21), calls=%async_computation | async-start | bytes 2654208 | tf_op jit(solution)/shard_map/all_to_all | solution.py:257
  21.2 15.8 %collective-permute-start = (bf16[144,1152]{1,0:T(8,128)(2,1)S(1)}, bf16[144,1152]{1,0:T(8,128)(2,1)S(1)}, u32[]{:S(2)}, u32[]{:S(2)}) collective-permute-start(bf16[144,1152]{1,0:T(8,128)(2,1)S(1)} %get-tuple-element.22.refs_2_), channel_id=1, source_target_pairs={{0,8},{4,12},{8,0},{12,4},{1,9},{5,13},{9,1},{13,5},{2,10},{6,14},... | collective-permute-start | bytes 995336 | tf_op jit(solution)/shard_map/ppermute | solution.py:28
  25.8 16.0 %collective-permute-start.1 = (bf16[144,1152]{1,0:T(8,128)(2,1)S(1)}, bf16[144,1152]{1,0:T(8,128)(2,1)S(1)}, u32[]{:S(2)}, u32[]{:S(2)}) collective-permute-start(bf16[144,1152]{1,0:T(8,128)(2,1)S(1)} %get-tuple-element.22.refs_2_), channel_id=1, source_target_pairs={{0,4},{4,8},{8,12},{12,0},{1,5},{5,9},{9,13},{13,1},{2,6},{6,10},{... | collective-permute-start | bytes 995336 | tf_op jit(solution)/shard_map/ppermute | solution.py:28
  28.0 16.5 %collective-permute-start.2 = (bf16[144,1152]{1,0:T(8,128)(2,1)S(1)}, bf16[144,1152]{1,0:T(8,128)(2,1)S(1)}, u32[]{:S(2)}, u32[]{:S(2)}) collective-permute-start(bf16[144,1152]{1,0:T(8,128)(2,1)S(1)} %get-tuple-element.22.refs_2_), channel_id=1, source_target_pairs={{0,12},{4,0},{8,4},{12,8},{1,13},{5,1},{9,5},{13,9},{2,14},{6,2},{... | collective-permute-start | bytes 995336 | tf_op jit(solution)/shard_map/ppermute | solution.py:28
  32.5 12.6 %collective-permute-start.4 = (bf16[144,1152]{1,0:T(8,128)(2,1)S(1)}, bf16[144,1152]{1,0:T(8,128)(2,1)S(1)}, u32[]{:S(2)}, u32[]{:S(2)}) collective-permute-start(bf16[144,1152]{1,0:T(8,128)(2,1)S(1)} %shard_map.50.refs_6_), channel_id=1, source_target_pairs={{0,8},{4,12},{8,0},{12,4},{1,9},{5,13},{9,1},{13,5},{2,10},{6,14},... | collective-permute-start | bytes 995336 | tf_op jit(solution)/shard_map/ppermute | solution.py:28
  34.4 14.9 %collective-permute-start.5 = (bf16[144,1152]{1,0:T(8,128)(2,1)S(1)}, bf16[144,1152]{1,0:T(8,128)(2,1)}, u32[]{:S(2)}, u32[]{:S(2)}) collective-permute-start(bf16[144,1152]{1,0:T(8,128)(2,1)S(1)} %shard_map.50.refs_6_), channel_id=1, source_target_pairs={{0,4},{4,8},{8,12},{12,0},{1,5},{5,9},{9,13},{13,1},{2,6},{6,10},{... | collective-permute-start | bytes 995336 | tf_op jit(solution)/shard_map/ppermute | solution.py:28
  36.9 14.0 %collective-permute-start.6 = (bf16[144,1152]{1,0:T(8,128)(2,1)S(1)}, bf16[144,1152]{1,0:T(8,128)(2,1)}, u32[]{:S(2)}, u32[]{:S(2)}) collective-permute-start(bf16[144,1152]{1,0:T(8,128)(2,1)S(1)} %shard_map.50.refs_6_), channel_id=1, source_target_pairs={{0,12},{4,0},{8,4},{12,8},{1,13},{5,1},{9,5},{13,9},{2,14},{6,2},{... | collective-permute-start | bytes 995336 | tf_op jit(solution)/shard_map/ppermute | solution.py:28
  62.2 20.4 %collective-permute-start.7 = (bf16[320,1152]{1,0:T(8,128)(2,1)S(1)}, bf16[320,1152]{1,0:T(8,128)(2,1)S(1)}, u32[]{:S(2)}, u32[]{:S(2)}) collective-permute-start(bf16[320,1152]{1,0:T(8,128)(2,1)S(1)} %get-tuple-element.24), channel_id=1, source_target_pairs={{0,1},{1,0},{2,3},{3,2},{16,18},{17,19},{18,16},{19,17},{4,5},{5,4... | collective-permute-start | bytes 2211848 | tf_op jit(solution)/shard_map/ppermute | solution.py:36
  68.2 16.4 %collective-permute-start.9 = (bf16[576,1152]{1,0:T(8,128)(2,1)S(1)}, bf16[576,1152]{1,0:T(8,128)(2,1)S(1)}, u32[]{:S(2)}, u32[]{:S(2)}) collective-permute-start(bf16[576,1152]{1,0:T(8,128)(2,1)S(1)} %get-tuple-element.26), channel_id=1, source_target_pairs={{16,0},{17,1},{18,2},{19,3},{20,4},{21,5},{22,6},{23,7},{24,8},{25... | collective-permute-start | bytes 3981320 | tf_op jit(solution)/shard_map/ppermute | solution.py:270
  69.6 2.1 %collective-permute-start.10 = (bf16[144,1152]{1,0:T(8,128)(2,1)S(1)}, bf16[144,1152]{1,0:T(8,128)(2,1)S(1)}, u32[]{:S(2)}, u32[]{:S(2)}) collective-permute-start(bf16[144,1152]{1,0:T(8,128)(2,1)S(1)} %get-tuple-element.29), channel_id=1, source_target_pairs={{0,8},{4,12},{8,0},{12,4},{1,9},{5,13},{9,1},{13,5},{2,10},{6,14},... | collective-permute-start | bytes 995336 | tf_op jit(solution)/shard_map/ppermute | solution.py:48
  70.3 1.4 %collective-permute-start.11 = (bf16[144,1152]{1,0:T(8,128)(2,1)S(1)}, bf16[144,1152]{1,0:T(8,128)(2,1)S(1)}, u32[]{:S(2)}, u32[]{:S(2)}) collective-permute-start(bf16[144,1152]{1,0:T(8,128)(2,1)S(1)} %get-tuple-element.30), channel_id=1, source_target_pairs={{0,12},{4,0},{8,4},{12,8},{1,13},{5,1},{9,5},{13,9},{2,14},{6,2},{... | collective-permute-start | bytes 995336 | tf_op jit(solution)/shard_map/ppermute | solution.py:48
  71.0 0.7 collective-permute-start.12
  71.9 39.8 %collective-permute-start.13 = (bf16[144,1152]{1,0:T(8,128)(2,1)S(1)}, bf16[144,1152]{1,0:T(8,128)(2,1)S(1)}, u32[]{:S(2)}, u32[]{:S(2)}) collective-permute-start(bf16[144,1152]{1,0:T(8,128)(2,1)S(1)} %shard_map.55), channel_id=1, source_target_pairs={{32,16},{64,48},{96,80},{128,112},{160,144},{192,176},{224,208},{2... | collective-permute-start | bytes 995336 | tf_op jit(solution)/shard_map/ppermute | solution.py:44
  82.7 31.2 %collective-permute-start.8 = (bf16[160,1152]{1,0:T(8,128)(2,1)S(1)}, bf16[160,1152]{1,0:T(8,128)(2,1)S(1)}, u32[]{:S(2)}, u32[]{:S(2)}) collective-permute-start(bf16[160,1152]{1,0:T(8,128)(2,1)S(1)} %shard_map.52), channel_id=1, source_target_pairs={{0,2},{1,3},{2,0},{3,1},{16,17},{17,16},{18,19},{19,18},{4,6},{5,7... | collective-permute-start | bytes 1105928 | tf_op jit(solution)/shard_map/ppermute | solution.py:36
  86.0 25.7 %collective-permute-start.14 = (bf16[144,1152]{1,0:T(8,128)(2,1)S(1)}, bf16[144,1152]{1,0:T(8,128)(2,1)S(1)}, u32[]{:S(2)}, u32[]{:S(2)}) collective-permute-start(bf16[144,1152]{1,0:T(8,128)(2,1)S(1)} %get-tuple-element.32), channel_id=1, source_target_pairs={{0,8},{4,12},{8,0},{12,4},{1,9},{5,13},{9,1},{13,5},{2,10},{6,14},... | collective-permute-start | bytes 995336 | tf_op jit(solution)/shard_map/ppermute | solution.py:28
  89.3 22.5 %collective-permute-start.15 = (bf16[144,1152]{1,0:T(8,128)(2,1)S(1)}, bf16[144,1152]{1,0:T(8,128)(2,1)S(1)}, u32[]{:S(2)}, u32[]{:S(2)}) collective-permute-start(bf16[144,1152]{1,0:T(8,128)(2,1)S(1)} %get-tuple-element.33), channel_id=1, source_target_pairs={{0,12},{4,0},{8,4},{12,8},{1,13},{5,1},{9,5},{13,9},{2,14},{6,2},{... | collective-permute-start | bytes 995336 | tf_op jit(solution)/shard_map/ppermute | solution.py:28
  92.1 19.7 %collective-permute-start.16 = (bf16[144,1152]{1,0:T(8,128)(2,1)S(1)}, bf16[144,1152]{1,0:T(8,128)(2,1)S(1)}, u32[]{:S(2)}, u32[]{:S(2)}) collective-permute-start(bf16[144,1152]{1,0:T(8,128)(2,1)S(1)} %get-tuple-element.34), channel_id=1, source_target_pairs={{0,4},{4,8},{8,12},{12,0},{1,5},{5,9},{9,13},{13,1},{2,6},{6,10},{... | collective-permute-start | bytes 995336 | tf_op jit(solution)/shard_map/ppermute | solution.py:28
  111.7 1.0 copy-start.1
  111.7 2.2 %copy-start.3 = (bf16[144,1152]{1,0:T(8,128)(2,1)S(1)}, bf16[144,1152]{1,0:T(8,128)(2,1)}, u32[]{:S(2)}) copy-start(bf16[144,1152]{1,0:T(8,128)(2,1)} %raw_ref.3) | copy-start | bytes 995332
